TPU v7x, 128 devices: a whole 4x4x4 slice. The times are simulated.
128 devices in a mesh: dp: 16 (over z, x), ep: 8 (over y, core).
Axes of the slice: x: 4, y: 4, z: 4, core: 2. Of those that a mesh axis runs over, the one named last changes fastest.
Arguments:
- cache_pool: bfloat16 [16384, 64, 576], P(('dp', 'ep')), may hold values from -6 to 6
- page_table: int32 [128, 64], replicated, may hold values from 0 to 16383, as said below
- page_counts: int32 [128, 4], P(('dp', 'ep')), may hold values from 1 to 32, 64 in all within a row
- queries: bfloat16 [2, 512, 64, 576], P(None, ('dp', 'ep')), may hold values from -60 to 60
- new_latent: bfloat16 [2, 512, 576], P(None, ('dp', 'ep')), may hold values from -6 to 6
- residual: bfloat16 [2, 512, 3584], P(None, ('dp', 'ep')), may hold values from -6 to 6
- w_uv: bfloat16 [64, 512, 128], P('ep'), may hold values from -4 to 4
- w_out: bfloat16 [8192, 3584], P('ep'), may hold values from -0.0625 to 0.0625
- norm_gain: float32 [3584], replicated, may hold values from 0.5 to 1.5
- w_router: float32 [3584, 16], replicated, may hold values from -0.09375 to 0.09375
- w_gate: bfloat16 [16, 3584, 2048], P('dp', None, 'ep'), may hold values from -0.09375 to 0.09375
- w_up: bfloat16 [16, 3584, 2048], P('dp', None, 'ep'), may hold values from -0.09375 to 0.09375
- w_down: bfloat16 [16, 2048, 3584], P('dp', 'ep'), may hold values from -0.125 to 0.125
- routes: int32 [2, 512, 8], P(None, ('dp', 'ep')), may hold values from 0 to 15, all different within a row; in each aligned block of 4 rows (0 to 3, 4 to 7, ..., all dimensions but the last counted through in order) at most 3 rows name the same one
Outputs:
- layer_out: bfloat16 [2, 512, 3584], P(None, ('dp', 'ep'))
Inputs may be any that keep to these rules, and one draw needn't show every extreme that they name: `page_table`: row d lists, request after request of device d, the pool pages of its requests' cache; no pool page is listed twice; at most 1 entries of a row lie among one device's 128 pool pages, and every row reaches that. `page_counts`: each device's counts sum to exactly 64, and the largest is 32. `routes`: each row names 8 different experts; at each step, no expert is named by more than 3 of one device's 4 rows, and that is reached.
All inputs are finite; a program needn't handle non-finite values.
Results may differ from a plain program's by a relative error of at most 0.019.
Values may be sent and summed in bfloat16 or wider, within the bound.
A program may use at most 192 MiB of HBM per device.

v0:
```python
import jax
import jax.numpy as jnp
from jax import lax
from jax.sharding import PartitionSpec as P

LATENT = 512


score_scale = 192.0 ** (-0.5)
route_scale = 2.5
norm_eps = 1e-06
highest = lax.Precision.HIGHEST


def expert_apply(rows_in, gate_w, up_w, down_w):
    gate_out = jnp.dot(rows_in, gate_w, preferred_element_type=jnp.float32)
    up_out = jnp.dot(rows_in, up_w, preferred_element_type=jnp.float32)
    inner_act = (jax.nn.silu(gate_out) * up_out).astype(jnp.bfloat16)
    return jnp.dot(inner_act, down_w, preferred_element_type=jnp.float32)


def shards(
    cache_pool,
    page_table,
    page_counts,
    queries,
    new_latent,
    residual,
    w_uv,
    w_out,
    norm_gain,
    w_router,
    w_gate,
    w_up,
    w_down,
    routes,
):
    dp_size = lax.axis_size("dp")
    ep_size = lax.axis_size("ep")
    device_count = dp_size * ep_size
    my_index = lax.axis_index("dp") * ep_size + lax.axis_index("ep")
    pool_dev = cache_pool.shape[0]
    slot_count = pool_dev // device_count
    owner_all = page_table // pool_dev
    local_all = page_table % pool_dev
    is_mine = (owner_all == my_index).astype(jnp.int32)
    ranked = jnp.cumsum(is_mine, axis=1) - 1
    wanted = (is_mine[:, None, :] == 1) & (
        ranked[:, None, :] == jnp.arange(slot_count)[None, :, None]
    )
    source = jnp.sum(jnp.where(wanted, local_all[:, None, :], 0), axis=2)
    filled = jnp.any(wanted, axis=2)
    outgoing = jnp.where(
        filled[:, :, None, None], cache_pool[source], jnp.zeros((), cache_pool.dtype)
    )
    incoming = lax.all_to_all(outgoing, ("dp", "ep"), split_axis=0, concat_axis=0, tiled=True)
    my_table = lax.dynamic_index_in_dim(page_table, my_index, 0, keepdims=False)
    my_owner = my_table // pool_dev
    page_index = jnp.arange(my_table.shape[0])
    earlier = (my_owner[None, :] == my_owner[:, None]) & (page_index[None, :] < page_index[:, None])
    rank_own = jnp.sum(earlier, axis=1)
    packed = incoming.reshape((-1,) + incoming.shape[2:])[my_owner * slot_count + rank_own]
    packed_latent = packed[:, :, :LATENT]
    rows_dev = queries.shape[1]
    heads_all = queries.shape[2]
    width = queries.shape[3]
    page_total = packed.shape[0]
    counts = page_counts[0]
    row_ends = jnp.cumsum(counts)
    row_of = jnp.sum(page_index[:, None] >= row_ends[None, :], axis=1)
    member = row_of[None, :] == jnp.arange(rows_dev)[:, None]
    member_real = member.astype(jnp.float32)
    member_low = member.astype(jnp.bfloat16)
    top_count = routes.shape[2]
    d_model = residual.shape[2]
    capacity = min(rows_dev, (3 * rows_dev * top_count + 2 * dp_size - 1) // (2 * dp_size))
    outputs = []
    for step_index in range(queries.shape[0]):
        queries_now = queries[step_index]
        per_page = jnp.dot(
            member_low.T, queries_now.reshape(rows_dev, -1), preferred_element_type=jnp.float32
        )
        per_page = per_page.astype(jnp.bfloat16).reshape(page_total, heads_all, width)
        scores = (
            jnp.einsum("jhc,jtc->jht", per_page, packed, preferred_element_type=jnp.float32)
            * score_scale
        )
        own_latent = new_latent[: step_index + 1]
        own_scores = (
            jnp.einsum("rhc,src->rhs", queries_now, own_latent, preferred_element_type=jnp.float32)
            * score_scale
        )
        page_max = jnp.max(scores, axis=2)
        row_max = jnp.max(jnp.where(member[:, :, None], page_max[None, :, :], -jnp.inf), axis=1)
        row_max = jnp.maximum(row_max, jnp.max(own_scores, axis=2))
        page_top = jnp.dot(member_real.T, row_max, precision=highest)
        weights = jnp.exp(scores - page_top[:, :, None])
        own_weights = jnp.exp(own_scores - row_max[:, :, None])
        total = jnp.dot(member_real, jnp.sum(weights, axis=2), precision=highest) + jnp.sum(
            own_weights, axis=2
        )
        per_page_out = jnp.einsum(
            "jht,jtc->jhc",
            weights.astype(jnp.bfloat16),
            packed_latent,
            preferred_element_type=jnp.float32,
        )
        gathered = jnp.dot(
            member_real, per_page_out.reshape(page_total, -1), precision=highest
        ).reshape(rows_dev, heads_all, -1)
        gathered = gathered + jnp.einsum(
            "rhs,src->rhc",
            own_weights.astype(jnp.bfloat16),
            own_latent[:, :, :LATENT],
            preferred_element_type=jnp.float32,
        )
        attended = (gathered / total[:, :, None]).astype(jnp.bfloat16)
        grouped = lax.all_to_all(attended, "ep", split_axis=1, concat_axis=0, tiled=True)
        head_values = jnp.einsum(
            "rhc,hcv->rhv", grouped, w_uv, preferred_element_type=jnp.float32
        ).astype(jnp.bfloat16)
        head_flat = head_values.reshape(grouped.shape[0], -1)
        attention_out = lax.psum_scatter(
            jnp.dot(head_flat, w_out, preferred_element_type=jnp.float32).astype(jnp.bfloat16),
            "ep",
            scatter_dimension=0,
            tiled=True,
        ).astype(jnp.float32)
        hidden = residual[step_index].astype(jnp.float32) + attention_out
        normed = (
            hidden
            * lax.rsqrt(jnp.mean(hidden * hidden, axis=-1, keepdims=True) + norm_eps)
            * norm_gain
        ).astype(jnp.bfloat16)
        affinity = jax.nn.sigmoid(jnp.dot(normed.astype(jnp.float32), w_router, precision=highest))
        route_now = routes[step_index]
        chosen = jnp.take_along_axis(affinity, route_now, axis=1)
        gate_weights = route_scale * chosen / jnp.sum(chosen, axis=1, keepdims=True)
        flat_routes = route_now.reshape(-1)
        expert_hit = (flat_routes[:, None] == jnp.arange(dp_size)[None, :]).astype(jnp.int32)
        arrival = jnp.sum((jnp.cumsum(expert_hit, axis=0) - 1) * expert_hit, axis=1)
        slot_id = flat_routes * capacity + arrival
        slot_hit = (slot_id[:, None] == jnp.arange(dp_size * capacity)[None, :]).astype(jnp.float32)
        slot_hit = slot_hit.reshape(rows_dev, top_count, dp_size * capacity)
        dispatch = jnp.sum(slot_hit, axis=1).T.astype(jnp.bfloat16)
        combine = jnp.einsum("rk,rks->rs", gate_weights, slot_hit, precision=highest)
        outgoing_rows = jnp.dot(dispatch, normed, preferred_element_type=jnp.float32).astype(
            jnp.bfloat16
        )
        outgoing_rows = outgoing_rows.reshape(dp_size, capacity, d_model)
        spread = jnp.broadcast_to(
            outgoing_rows[:, None], (dp_size, ep_size, capacity, d_model)
        ).reshape(dp_size * ep_size, capacity, d_model)
        arrived = lax.all_to_all(spread, ("dp", "ep"), split_axis=0, concat_axis=0, tiled=True)
        partial_value = expert_apply(arrived.reshape(-1, d_model), w_gate[0], w_up[0], w_down[0])
        partial_value = partial_value.astype(jnp.bfloat16).reshape(arrived.shape)
        back_parts = lax.all_to_all(
            partial_value, ("dp", "ep"), split_axis=0, concat_axis=0, tiled=True
        )
        returned = jnp.sum(
            back_parts.reshape(dp_size, ep_size, capacity, d_model).astype(jnp.float32), axis=1
        ).astype(jnp.bfloat16)
        expert_mix = jnp.dot(
            combine,
            returned.reshape(dp_size * capacity, d_model).astype(jnp.float32),
            precision=highest,
        )
        outputs.append((hidden + expert_mix).astype(jnp.bfloat16))
    return jnp.stack(outputs)


def solution(mesh):
    return jax.shard_map(
        shards,
        mesh=mesh,
        in_specs=(
            P(("dp", "ep"), None, None),
            P(),
            P(("dp", "ep"), None),
            P(None, ("dp", "ep"), None, None),
            P(None, ("dp", "ep"), None),
            P(None, ("dp", "ep"), None),
            P("ep", None, None),
            P("ep", None),
            P(),
            P(),
            P("dp", None, "ep"),
            P("dp", None, "ep"),
            P("dp", "ep", None),
            P(None, ("dp", "ep"), None),
        ),
        out_specs=P(None, ("dp", "ep"), None),
        check_vma=False,
    )
```

profile of v0, /device:TPU:1, one launch (start us, length us, event | category | flops | bytes accessed | tf_op | source)
XLA Modules:
  0.0 567.4 jit_solution(456762711317371955)
XLA Ops:
  9.2 14.8 %copy.56 = bf16[128,64,576]{2,1,0:T(8,128)(2,1)} copy(bf16[128,64,576]{0,2,1:T(8,128)(2,1)} %param.16) | data formatting | bytes 18874368 | tf_op args[0]
  24.0 11.5 %gather_fusion = bf16[128,64,576]{2,1,0:T(8,128)(2,1)} fusion(bf16[128,64,576]{2,1,0:T(8,128)(2,1)} %copy.56, s32[1024]{0:T(1024)S(1)} %pad_clamp_fusion.1), kind=kCustom, calls=%fused_computation.2 | custom fusion | bytes 18874880 | tf_op jit(solution)/shard_map/gather | solution.py:54
  35.4 10.0 %fusion = bf16[128,1,64,576]{3,2,1,0:T(8,128)(2,1)} fusion(bf16[128,64,576]{2,1,0:T(8,128)(2,1)} %gather_fusion, pred[128]{0:T(512)(128)(4,1)S(1)} %get-tuple-element.16), kind=kLoop, calls=%fused_computation.7 | loop fusion | flops 4718592 | bytes 18874496 | tf_op jit(solution)/shard_map/jit(_where)/select_n | solution.py:53
  45.4 11.9 %all-to-all-start = ((bf16[128,1,64,576]{3,2,1,0:T(8,128)(2,1)}), bf16[128,1,64,576]{3,2,1,0:T(8,128)(2,1)}, u32[]{:S(2)}, u32[]{:S(2)}) async-start(bf16[128,1,64,576]{3,2,1,0:T(8,128)(2,1)} %fusion), calls=%async_computation | async-start | bytes 20971520 | tf_op jit(solution)/shard_map/all_to_all | solution.py:56
  58.2 3.7 convolution_convert_fusion
  61.9 10.0 %reshape.359 = bf16[64,64,576]{2,1,0:T(8,128)(2,1)} reshape(bf16[64,36864]{1,0:T(8,128)(2,1)} %convolution_convert_fusion) | data formatting | bytes 9437184 | tf_op jit(solution)/shard_map/reshape | solution.py:83
  72.3 3.5 convolution_convert_fusion.1
  75.8 10.2 %reshape.348 = bf16[64,64,576]{2,1,0:T(8,128)(2,1)} reshape(bf16[64,36864]{1,0:T(8,128)(2,1)} %convolution_convert_fusion.1) | data formatting | bytes 9437184 | tf_op jit(solution)/shard_map/reshape | solution.py:83
  87.5 94.2 %all-to-all-done = bf16[128,1,64,576]{3,2,1,0:T(8,128)(2,1)} async-done(((bf16[128,1,64,576]{3,2,1,0:T(8,128)(2,1)}), bf16[128,1,64,576]{3,2,1,0:T(8,128)(2,1)}, u32[]{:S(2)}, u32[]{:S(2)}) %all-to-all-start) | async-done | bytes 9437216 | tf_op jit(solution)/shard_map/all_to_all | solution.py:56
  181.7 7.5 %gather_fusion.1 = bf16[64,64,576]{2,1,0:T(8,128)(2,1)} fusion(bf16[128,64,576]{2,1,0:T(8,128)(2,1)} %bitcast.8, s32[1024]{0:T(1024)S(1)} %pad_clamp_fusion), kind=kCustom, calls=%fused_computation.3 | custom fusion | bytes 9437440 | tf_op jit(solution)/shard_map/gather | solution.py:62
  189.2 6.0 %multiply_reduce_fusion = (f32[64,64]{1,0:T(8,128)S(1)}, f32[64,64,64]{1,2,0:T(8,128)S(1)}) fusion(bf16[64,64,576]{2,1,0:T(8,128)(2,1)} %reshape.359, bf16[64,64,576]{2,1,0:T(8,128)(2,1)} %gather_fusion.1), kind=kOutput, calls=%fused_computation.34 | convolution fusion | flops 302510080 | bytes 10502144 | tf_op jit(solution)/shard_map/jhc,jtc->jht/dot_general | solution.py:85
  195.2 1.1 copy-done.2
  196.3 1.8 multiply_reduce_fusion.1
  198.5 4.5 fusion.11
  203.8 4.5 fusion.13
  209.4 22.6 %fusion.54 = bf16[4,64,512]{2,0,1:T(4,128)(2,1)} fusion(f32[4,64,512]{2,1,0:T(8,128)S(1)} %fusion.112, f32[4,64]{0,1:T(8,128)S(1)} %copy.69, s32[64]{0:T(128)S(1)} %convert_reduce_fusion.3, f32[8,8,64,512]{3,2,1,0:T(8,128)} %bitcast.236), kind=kOutput, calls=%fused_computation.57 | convolution fusion | flops 101056768 | bytes 9176320 | tf_op jit(solution)/shard_map/dot_general | solution.py:108
  232.0 3.4 all-to-all-start.4
  235.7 11.3 %fusion.60 = bf16[4,64,512]{2,0,1:T(4,128)(2,1)} fusion(f32[4,64]{0,1:T(8,128)S(1)} %copy.61, f32[4,512]{1,0:T(4,128)S(1)} %bitcast_convert_fusion, f32[4,64]{0,1:T(8,128)S(1)} %copy.60, s32[64]{0:T(128)S(1)} %convert_reduce_fusion.3, f32[8,8,64,512]{3,2,1,0:T(8,128)} %bitcast.235), kind=kOutput, calls=%fused_computation.59 | convolution fusion | flops 101187840 | bytes 8661248 | tf_op jit(solution)/shard_map/dot_general | solution.py:108
  247.0 4.7 all-to-all-start.1
  254.2 1.7 all_to_all.51
  255.9 2.4 all-to-all-done.1
  258.4 1.2 fusion.64
  259.9 5.2 convolution_convert_fusion.6
  265.1 5.1 convolution_convert_fusion.7
  270.3 59.3 %all-reduce.5.cloned.1.call-done = (bf16[32,3584]{1,0:T(8,128)(2,1)}, bf16[32,3584]{1,0:T(8,128)(2,1)}) async-done(((bf16[32,3584]{1,0:T(8,128)(2,1)}, bf16[32,3584]{1,0:T(8,128)(2,1)}), (bf16[32,3584]{1,0:T(8,128)(2,1)}, bf16[32,3584]{1,0:T(8,128)(2,1)})) %all-reduce.5.cloned.1.call-update) | async-done | bytes 458768
  330.7 1.1 convolution_convert_fusion.5
  332.0 2.7 broadcast_in_dim.60
  334.8 9.9 %all-to-all-start.2 = ((bf16[128,3,3584]{2,1,0:T(4,128)(2,1)}), bf16[128,3,3584]{2,1,0:T(4,128)(2,1)}, u32[]{:S(2)}, u32[]{:S(2)}) async-start(bf16[128,3,3584]{2,1,0:T(4,128)(2,1)} %bitcast.238), calls=%async_computation.2 | async-start | bytes 7340032 | tf_op jit(solution)/shard_map/all_to_all | solution.py:154
  344.6 1.1 convolution_convert_fusion.4
  346.0 45.9 %all-to-all-done.2 = bf16[128,3,3584]{2,1,0:T(4,128)(2,1)} async-done(((bf16[128,3,3584]{2,1,0:T(4,128)(2,1)}), bf16[128,3,3584]{2,1,0:T(4,128)(2,1)}, u32[]{:S(2)}, u32[]{:S(2)}) %all-to-all-start.2) | async-done | bytes 2752544 | tf_op jit(solution)/shard_map/all_to_all | solution.py:154
  391.9 2.9 broadcast_in_dim.63
  394.7 5.3 all-to-all-start.5
  400.1 7.1 %reshape.355 = bf16[384,3584]{1,0:T(8,128)(2,1)} reshape(bf16[128,3,3584]{2,1,0:T(4,128)(2,1)} %all-to-all-done.2) | data formatting | bytes 5505024 | tf_op jit(solution)/shard_map/reshape | solution.py:155
  407.2 3.2 fusion.23
  410.4 6.9 %convolution_convert_fusion.3 = bf16[384,3584]{1,0:T(8,128)(2,1)} fusion(bf16[1,256,3584]{2,1,0:T(8,128)(2,1)S(1)} %copy-done, bf16[384,3584]{1,0:T(8,128)(2,1)} %reshape.355, bf16[1,3584,256]{2,1,0:T(8,128)(2,1)} %param.27, f32[384,256]{1,0:T(8,128)S(1)} %fusion.23), kind=kOutput, calls=%fused_computation.15 | convolution fusion | flops 1411252224 | bytes 9568256 | tf_op jit(solution)/shard_map/dot_general | solution.py:19
  417.2 6.7 %reshape.356 = bf16[128,3,3584]{2,1,0:T(4,128)(2,1)} reshape(bf16[384,3584]{1,0:T(8,128)(2,1)} %convolution_convert_fusion.3) | data formatting | bytes 5505024 | tf_op jit(solution)/shard_map/reshape | solution.py:156
  423.9 23.5 %all-to-all-done.5 = bf16[128,3,3584]{2,1,0:T(4,128)(2,1)} async-done(((bf16[128,3,3584]{2,1,0:T(4,128)(2,1)}), bf16[128,3,3584]{2,1,0:T(4,128)(2,1)}, u32[]{:S(2)}, u32[]{:S(2)}) %all-to-all-start.5) | async-done | bytes 2752544 | tf_op jit(solution)/shard_map/all_to_all | solution.py:154
  447.4 5.3 all-to-all-start.3
  452.8 7.1 %reshape.363 = bf16[384,3584]{1,0:T(8,128)(2,1)} reshape(bf16[128,3,3584]{2,1,0:T(4,128)(2,1)} %all-to-all-done.5) | data formatting | bytes 5505024 | tf_op jit(solution)/shard_map/reshape | solution.py:155
  459.9 3.2 fusion.21
  463.1 6.9 %convolution_convert_fusion.2 = bf16[384,3584]{1,0:T(8,128)(2,1)} fusion(bf16[1,256,3584]{2,1,0:T(8,128)(2,1)S(1)} %copy-done, bf16[384,3584]{1,0:T(8,128)(2,1)} %reshape.363, bf16[1,3584,256]{2,1,0:T(8,128)(2,1)} %param.27, f32[384,256]{1,0:T(8,128)S(1)} %fusion.21), kind=kOutput, calls=%fused_computation.14 | convolution fusion | flops 1411252224 | bytes 9568256 | tf_op jit(solution)/shard_map/dot_general | solution.py:19
  469.9 6.7 %reshape.364 = bf16[128,3,3584]{2,1,0:T(4,128)(2,1)} reshape(bf16[384,3584]{1,0:T(8,128)(2,1)} %convolution_convert_fusion.2) | data formatting | bytes 5505024 | tf_op jit(solution)/shard_map/reshape | solution.py:156
  476.6 23.6 %all-to-all-done.3 = bf16[128,3,3584]{2,1,0:T(4,128)(2,1)} async-done(((bf16[128,3,3584]{2,1,0:T(4,128)(2,1)}), bf16[128,3,3584]{2,1,0:T(4,128)(2,1)}, u32[]{:S(2)}, u32[]{:S(2)}) %all-to-all-start.3) | async-done | bytes 2752544 | tf_op jit(solution)/shard_map/all_to_all | solution.py:157
  500.2 5.7 %all-to-all-start.6 = ((bf16[128,3,3584]{2,1,0:T(4,128)(2,1)}), bf16[128,3,3584]{2,1,0:T(4,128)(2,1)}, u32[]{:S(2)}, u32[]{:S(2)}) async-start(bf16[128,3,3584]{2,1,0:T(4,128)(2,1)} %reshape.364), calls=%async_computation.6 | async-start | bytes 7340032 | tf_op jit(solution)/shard_map/all_to_all | solution.py:157
  506.1 1.1 fusion.67
  510.7 3.9 bitcast_reduce_fusion.1
  514.9 38.3 %all-to-all-done.6 = bf16[128,3,3584]{2,1,0:T(4,128)(2,1)} async-done(((bf16[128,3,3584]{2,1,0:T(4,128)(2,1)}), bf16[128,3,3584]{2,1,0:T(4,128)(2,1)}, u32[]{:S(2)}, u32[]{:S(2)}) %all-to-all-start.6) | async-done | bytes 2752544 | tf_op jit(solution)/shard_map/all_to_all | solution.py:157
  553.2 3.9 bitcast_reduce_fusion
  (103 shorter events, 18.7 us)
Async XLA Ops:
  6.5 403.8 %copy-start = (bf16[1,256,3584]{2,1,0:T(8,128)(2,1)S(1)}, bf16[1,256,3584]{2,1,0:T(8,128)(2,1)}, u32[]{:S(2)}) copy-start(bf16[1,256,3584]{2,1,0:T(8,128)(2,1)} %param.28) | copy-start | bytes 5505028
  45.4 12.0 %copy-start.11 = (s32[1,4]{1,0:T(1,128)S(1)}, s32[1,4]{1,0:T(1,128)}, u32[]{:S(2)}) copy-start(s32[1,4]{1,0:T(1,128)} %param.18) | copy-start | bytes 52
  45.4 12.2 %copy-start.6 = (bf16[2,4,64,576]{3,2,1,0:T(8,128)(2,1)S(1)}, bf16[2,4,64,576]{3,2,1,0:T(8,128)(2,1)}, u32[]{:S(2)}) copy-start(bf16[2,4,64,576]{3,2,1,0:T(8,128)(2,1)} %param.19) | copy-start | bytes 1769476
  45.4 136.2 %all-to-all-start = ((bf16[128,1,64,576]{3,2,1,0:T(8,128)(2,1)}), bf16[128,1,64,576]{3,2,1,0:T(8,128)(2,1)}, u32[]{:S(2)}, u32[]{:S(2)}) async-start(bf16[128,1,64,576]{3,2,1,0:T(8,128)(2,1)} %fusion), calls=%async_computation | async-start | bytes 20971520 | tf_op jit(solution)/shard_map/all_to_all | solution.py:56
  75.8 10.2 %copy-start.10 = (bf16[2,4,576]{2,1,0:T(4,128)(2,1)S(1)}, bf16[2,4,576]{2,1,0:T(4,128)(2,1)}, u32[]{:S(2)}) copy-start(bf16[2,4,576]{2,1,0:T(4,128)(2,1)} %param.20) | copy-start | bytes 27652
  75.8 10.2 %copy-start.9 = (s32[2,4,8]{2,1,0:T(4,128)S(1)}, s32[2,4,8]{2,1,0:T(4,128)}, u32[]{:S(2)}) copy-start(s32[2,4,8]{2,1,0:T(4,128)} %param.29) | copy-start | bytes 772
  75.8 10.8 %copy-start.7 = (s32[128,64]{0,1:T(8,128)S(1)}, s32[128,64]{0,1:T(8,128)}, u32[]{:S(2)}) copy-start(s32[128,64]{0,1:T(8,128)} %param.17) | copy-start | bytes 98308
  189.2 6.0 %copy-start.1 = (bf16[64,64,576]{2,1,0:T(8,128)(2,1)S(1)}, bf16[64,64,576]{2,1,0:T(8,128)(2,1)}, u32[]{:S(2)}) copy-start(bf16[64,64,576]{2,1,0:T(8,128)(2,1)} %gather_fusion.1) | copy-start | bytes 14155780
  189.2 7.1 %copy-start.2 = (bf16[64,64,576]{2,1,0:T(8,128)(2,1)S(1)}, bf16[64,64,576]{2,1,0:T(8,128)(2,1)}, u32[]{:S(2)}) copy-start(bf16[64,64,576]{2,1,0:T(8,128)(2,1)} %reshape.348) | copy-start | bytes 14155780
  232.0 15.0 %all-to-all-start.4 = ((bf16[4,64,512]{2,0,1:T(4,128)(2,1)}), bf16[4,64,512]{2,0,1:T(4,128)(2,1)S(1)}, u32[]{:S(2)}, u32[]{:S(2)}) async-start(bf16[4,64,512]{2,0,1:T(4,128)(2,1)} %fusion.54), calls=%async_computation.4 | async-start | bytes 524288 | tf_op jit(solution)/shard_map/all_to_all | solution.py:118
  235.7 16.4 %copy-start.12 = (u32[128]{0:T(128)S(1)}, u32[128]{0:T(128)}, u32[]{:S(2)}) copy-start(u32[128]{0:T(128)} %constant.163) | copy-start | bytes 1540
  235.7 22.7 %copy-start.3 = (bf16[8,512,128]{2,1,0:T(8,128)(2,1)S(1)}, bf16[8,512,128]{2,1,0:T(8,128)(2,1)}, u32[]{:S(2)}) copy-start(bf16[8,512,128]{2,1,0:T(8,128)(2,1)} %param.22) | copy-start | bytes 3145732
  247.0 11.2 %all-to-all-start.1 = ((bf16[4,64,512]{2,0,1:T(4,128)(2,1)}), bf16[4,64,512]{2,0,1:T(4,128)(2,1)S(1)}, u32[]{:S(2)}, u32[]{:S(2)}) async-start(bf16[4,64,512]{2,0,1:T(4,128)(2,1)} %fusion.60), calls=%async_computation.1 | async-start | bytes 524288 | tf_op jit(solution)/shard_map/all_to_all | solution.py:118
  251.7 77.9 %all-reduce.5.cloned.1.call-start = ((), (), s32[]{:S(2)}) async-start(), calls=%async_computation.7 | async-start | bytes 917504
  265.1 64.5 %copy-start.4 = (bf16[2,4,3584]{2,1,0:T(4,128)(2,1)S(1)}, bf16[2,4,3584]{2,1,0:T(4,128)(2,1)}, u32[]{:S(2)}) copy-start(bf16[2,4,3584]{2,1,0:T(4,128)(2,1)} %param.21) | copy-start | bytes 172036
  265.1 65.6 %copy-start.8 = (f32[3584]{0:T(1024)S(1)}, f32[3584]{0:T(1024)}, u32[]{:S(2)}) copy-start(f32[3584]{0:T(1024)} %param.24) | copy-start | bytes 43012
  334.8 57.1 %all-to-all-start.2 = ((bf16[128,3,3584]{2,1,0:T(4,128)(2,1)}), bf16[128,3,3584]{2,1,0:T(4,128)(2,1)}, u32[]{:S(2)}, u32[]{:S(2)}) async-start(bf16[128,3,3584]{2,1,0:T(4,128)(2,1)} %bitcast.238), calls=%async_computation.2 | async-start | bytes 7340032 | tf_op jit(solution)/shard_map/all_to_all | solution.py:154
  394.7 52.7 %all-to-all-start.5 = ((bf16[128,3,3584]{2,1,0:T(4,128)(2,1)}), bf16[128,3,3584]{2,1,0:T(4,128)(2,1)}, u32[]{:S(2)}, u32[]{:S(2)}) async-start(bf16[128,3,3584]{2,1,0:T(4,128)(2,1)} %bitcast.237), calls=%async_computation.5 | async-start | bytes 7340032 | tf_op jit(solution)/shard_map/all_to_all | solution.py:154
  447.4 52.7 %all-to-all-start.3 = ((bf16[128,3,3584]{2,1,0:T(4,128)(2,1)}), bf16[128,3,3584]{2,1,0:T(4,128)(2,1)}, u32[]{:S(2)}, u32[]{:S(2)}) async-start(bf16[128,3,3584]{2,1,0:T(4,128)(2,1)} %reshape.356), calls=%async_computation.3 | async-start | bytes 7340032 | tf_op jit(solution)/shard_map/all_to_all | solution.py:157
  476.6 29.5 %copy-start.5 = (f32[3584,16]{0,1:T(8,128)S(1)}, f32[3584,16]{0,1:T(8,128)}, u32[]{:S(2)}) copy-start(f32[3584,16]{0,1:T(8,128)} %param.25) | copy-start | bytes 688132
  500.2 53.0 %all-to-all-start.6 = ((bf16[128,3,3584]{2,1,0:T(4,128)(2,1)}), bf16[128,3,3584]{2,1,0:T(4,128)(2,1)}, u32[]{:S(2)}, u32[]{:S(2)}) async-start(bf16[128,3,3584]{2,1,0:T(4,128)(2,1)} %reshape.364), calls=%async_computation.6 | async-start | bytes 7340032 | tf_op jit(solution)/shard_map/all_to_all | solution.py:157
Sparse Core Ops, SparseCore 0:
  270.4 59.2 all-reduce.4
where the time goes:
time: 577 us; the launch traced here: 567 us
  waiting for transfers between devices  287 us (50%)
  matrix products  98.2 us (17%)
  local copies, waits for them, and re-layouts  96 us (17%)
  starting transfers between devices  46.3 us (8%)
  other arithmetic  25 us (4%)
  between operations  14.9 us (3%)
    all_to_all x1, waiting for transfers between devices, shards(): lax.all_to_all(outgoing, ('dp', 'ep'), split_axis=0, concat_axis=0, tiled...  94.2 us
    all_to_all x2, waiting for transfers between devices, shards(): lax.all_to_all(spread, ('dp', 'ep'), split_axis=0, concat_axis=0, tiled=T...  69.4 us
    all_to_all x2, waiting for transfers between devices, shards(): lax.all_to_all(partial_value, ('dp', 'ep'), split_axis=0, concat_axis=0,...  61.8 us
    unnamed x2, waiting for transfers between devices  59.3 us
    dot_general x2, matrix products, shards(): jnp.dot(member_real, per_page_out.reshape(page_total, -1), precision=high...  33.9 us
    reshape x2, local copies, waits for them, and re-layouts, shards(): per_page.astype(jnp.bfloat16).reshape(page_total, heads_all, width)  20.1 us
    unnamed x29, local copies, waits for them, and re-layouts  16.5 us
    all_to_all x2, starting transfers between devices, shards(): lax.all_to_all(spread, ('dp', 'ep'), split_axis=0, concat_axis=0, tiled=T...  15.2 us
  transfers between devices with their start and end apart: 8, of which 7 were waited for; matrix products, arithmetic and copies ran while one was open for 18% of the time, Pallas kernels for 0%

commit v1 on v0

v1 whole, which is shorter than its diff:
```python
import functools

import jax
import jax.numpy as jnp
from jax import lax
from jax.experimental import pallas as pl
from jax.experimental.pallas import tpu as pltpu
from jax.sharding import PartitionSpec as P

MESH = pl.DeviceIdType.MESH
F32 = jnp.float32
BF16 = jnp.bfloat16

LATENT = 512
PAGE = 64
TILE = 8
score_scale = 192.0 ** (-0.5)
route_scale = 2.5
norm_eps = 1e-06

HALF = 1792
PART = 640
ORDERS = ((0, 1, 2), (1, 2, 0), (2, 0, 1))
WIDTHS = (640, 640, 512)


def attend_kernel(owner, starts, counts, q_ref, own_ref, slots, out_ref, keys, scores, sem):
    rows = 64 * PAGE

    def fetch(j, _):
        at = pl.multiple_of(j * PAGE, PAGE)
        pltpu.make_async_copy(slots.at[owner[j]], keys.at[pl.ds(at, PAGE)], sem).start()
        return 0

    lax.fori_loop(0, 64, fetch, 0)

    def clear(j, _):
        at = pl.multiple_of(rows + j * PAGE, PAGE)
        keys[pl.ds(at, PAGE), :] = jnp.zeros((PAGE, keys.shape[1]), BF16)
        return 0

    lax.fori_loop(0, TILE, clear, 0)
    filled = keys.at[pl.ds(0, rows)]
    pltpu.make_async_copy(filled, filled, sem).wait()
    width = TILE * PAGE
    step_of = lax.broadcasted_iota(jnp.int32, (128, 16), 0) // 64
    token = lax.broadcasted_iota(jnp.int32, (128, 16), 1)

    def request(r, _):
        q = jnp.concatenate([q_ref[0, r], q_ref[1, r]], axis=0)
        own = own_ref[r]
        s_own = lax.dot_general(q, own, (((1,), (1,)), ((), ())), preferred_element_type=F32)
        s_own = jnp.where(token <= step_of, s_own * score_scale, -jnp.inf)
        start = starts[r] * PAGE
        length = counts[r] * PAGE
        tiles = (length + width - 1) // width

        def score(t, top):
            at = pl.multiple_of(start + t * width, PAGE)
            s = lax.dot_general(
                q, keys[pl.ds(at, width), :], (((1,), (1,)), ((), ())), preferred_element_type=F32
            )
            place = t * width + lax.broadcasted_iota(jnp.int32, (128, width), 1)
            s = jnp.where(place < length, s * score_scale, -jnp.inf)
            scores[t] = s
            return jnp.maximum(top, jnp.max(s, axis=1, keepdims=True))

        top = lax.fori_loop(0, tiles, score, jnp.max(s_own, axis=1, keepdims=True))
        p_own = jnp.exp(s_own - top)
        total = jnp.sum(p_own, axis=1, keepdims=True)
        acc = jnp.dot(p_own.astype(BF16), own[:, :LATENT], preferred_element_type=F32)

        def mix(t, carry):
            total, acc = carry
            at = pl.multiple_of(start + t * width, PAGE)
            p = jnp.exp(scores[t] - top)
            total = total + jnp.sum(p, axis=1, keepdims=True)
            acc = acc + jnp.dot(
                p.astype(BF16), keys[pl.ds(at, width), :LATENT], preferred_element_type=F32
            )
            return total, acc

        total, acc = lax.fori_loop(0, tiles, mix, (total, acc))
        res = (acc / total).reshape(2, 8, 8, LATENT)
        at = pl.multiple_of(r * 16, 16)
        for g in range(8):
            block = jnp.concatenate([res[0, g], res[1, g]], axis=0)
            out_ref[g, pl.ds(at, 16), :] = block.astype(BF16)
        return 0

    lax.fori_loop(0, 4, request, 0)


def attend(owner, starts, counts, queries, own, slots):
    smem = pl.BlockSpec(memory_space=pltpu.SMEM)
    vmem = pl.BlockSpec(memory_space=pltpu.VMEM)
    return pl.pallas_call(
        attend_kernel,
        out_shape=jax.ShapeDtypeStruct((8, 64, LATENT), BF16),
        in_specs=[smem, smem, smem, vmem, vmem, pl.BlockSpec(memory_space=pl.ANY)],
        out_specs=vmem,
        scratch_shapes=[
            pltpu.VMEM(((64 + TILE) * PAGE, slots.shape[-1]), BF16),
            pltpu.VMEM((32 // TILE, 128, TILE * PAGE), F32),
            pltpu.SemaphoreType.DMA,
        ],
        compiler_params=pltpu.CompilerParams(vmem_limit_bytes=40 * 2**20),
        name="attend",
    )(owner, starts, counts, queries, own, slots)


def layer_kernel(
    attended, resid, member, gain, router, w_uv, w_out, w_gate, w_up, w_down,
    out_ref,
    heads_in, masked, part_out, part_in, res_all, mem_all, stat_out, stat_in, hidden,
    gath, v_uv, v_out, v_gate, v_up, v_down, inner,
    mix, sib_out, sib_in, t1, ul1, ur1, t2, ul2, ur2, last, fin_out, fin_in,
    wsem, lsem, head_s, head_r, part_s, part_r, pair_s, pair_r,
    ag_s, ag_r, sib_s, sib_r, red_s, red_r, sum_s, sum_r,
):
    dp = lax.axis_index("dp")
    ep = lax.axis_index("ep")
    pos = (dp // 4, dp % 4, ep // 2)
    core = ep % 2
    other = 1 - core

    def device(coords, c):
        return (coords[0] * 4 + coords[1], coords[2] * 2 + c)

    def along(axis, delta):
        coords = [pos[0], pos[1], pos[2]]
        coords[axis] = (coords[axis] + delta) % 4
        return device(coords, core)

    sibling = device(pos, other)
    ep_peers = [(dp, (ep + o) % 8) for o in range(1, 8)]
    ring_peers = [along(a, d) for a in (0, 1) for d in (1, 2, 3)]

    def remote(src, dst, ssem, rsem, peer):
        copy = pltpu.make_async_remote_copy(
            src_ref=src, dst_ref=dst, send_sem=ssem, recv_sem=rsem,
            device_id=peer, device_id_type=MESH,
        )
        copy.start()
        sent.append((src, ssem))

    def landed(ref, rsem):
        pltpu.make_async_copy(ref, ref, rsem).wait()

    sent = []

    loads = [(w_uv, v_uv), (w_out, v_out), (w_gate, v_gate), (w_up, v_up), (w_down, v_down)]
    copies = [pltpu.make_async_copy(a, b, wsem.at[i]) for i, (a, b) in enumerate(loads)]
    for copy in copies:
        copy.start()

    barrier = pltpu.get_barrier_semaphore()
    for peer in ep_peers + ring_peers:
        pl.semaphore_signal(barrier, inc=1, device_id=peer, device_id_type=MESH)
    pl.semaphore_wait(barrier, len(ep_peers) + len(ring_peers))

    for o in range(1, 8):
        to = (ep + o) % 8
        remote(attended.at[to], heads_in.at[ep], head_s.at[o], head_r.at[o], (dp, to))
    own_heads = pltpu.make_async_copy(attended.at[ep], heads_in.at[ep], lsem)
    own_heads.start()
    own_rows = pl.ds(pl.multiple_of(core * 8, 8), 8)
    other_rows = pl.ds(pl.multiple_of(other * 8, 8), 8)
    remote(resid.at[other], res_all.at[own_rows], pair_s.at[0], pair_r.at[0], sibling)
    remote(member, mem_all.at[own_rows], pair_s.at[1], pair_r.at[1], sibling)
    res_all[own_rows, :] = resid[core]
    mem_all[own_rows, :] = member[...]
    own_heads.wait()
    for o in range(1, 8):
        landed(heads_in.at[(ep + 8 - o) % 8], head_r.at[o])

    copies[0].wait()
    x = heads_in[...].reshape(512, LATENT)
    row_head = lax.broadcasted_iota(jnp.int32, (512, 128), 0) % 8
    for h in range(8):
        y = jnp.dot(x, v_uv[h], preferred_element_type=F32)
        masked[:, h * 128 : (h + 1) * 128] = jnp.where(row_head == h, y, 0.0).astype(BF16)
    to_row = lax.broadcasted_iota(jnp.int32, (64, 512), 0)
    from_row = lax.broadcasted_iota(jnp.int32, (64, 512), 1) // 8
    wanted = (to_row // 8) * 8 + (to_row % 4) * 2 + (to_row % 8) // 4
    pick = jnp.where(from_row == wanted, 1.0, 0.0).astype(BF16)
    flat = jnp.dot(pick, masked[...], preferred_element_type=F32).astype(BF16)

    copies[1].wait()
    for h in range(2):
        for t in range(HALF // 256):
            col = h * HALF + t * 256
            y = jnp.dot(flat, v_out[:, col : col + 256], preferred_element_type=F32)
            part_out[h, :, :, t * 256 : (t + 1) * 256] = y.astype(BF16).reshape(4, 16, 256)
    for o in range(1, 8):
        to = (ep + o) % 8
        remote(
            part_out.at[to % 2, to // 2], part_in.at[ep], part_s.at[o], part_r.at[o], (dp, to)
        )
    landed(res_all.at[other_rows], pair_r.at[0])
    landed(mem_all.at[other_rows], pair_r.at[1])
    hid = part_out[core, pos[2]].astype(F32)
    for o in range(1, 8):
        src = (ep + 8 - o) % 8
        landed(part_in.at[src], part_r.at[o])
        hid = hid + part_in[src].astype(F32)
    hid = hid + res_all[...]
    hidden[...] = hid

    half_cols = pl.ds(pl.multiple_of(core * HALF, 128), HALF)
    scaled = hid * gain[:, half_cols]
    stat_out[0] = lax.dot_general(
        scaled, router[:, half_cols], (((1,), (1,)), ((), ())),
        preferred_element_type=F32, precision=lax.Precision.HIGHEST,
    )
    stat_out[1] = jnp.broadcast_to(jnp.sum(hid * hid, axis=1, keepdims=True), (16, 128))
    remote(stat_out, stat_in, pair_s.at[2], pair_r.at[2], sibling)
    landed(stat_in, pair_r.at[2])
    square = stat_out[1] + stat_in[1]
    inv = lax.rsqrt(square / (2 * HALF) + norm_eps)
    affinity = jax.nn.sigmoid((stat_out[0] + stat_in[0]) * inv) * mem_all[...]
    gates = route_scale * affinity / jnp.sum(affinity, axis=1, keepdims=True)
    coarse = gates.astype(BF16)
    fine = (gates - coarse.astype(F32)).astype(BF16)
    normed = (scaled * inv[:, 0:1]).astype(BF16)
    z, xx, yy = pos
    gath[core, 0, z, xx, yy] = normed[:, 0:640]
    gath[core, 1, z, xx, yy] = normed[:, 640:1280]
    gath[core, 2, z, xx, yy, :, 0:512] = normed[:, 1280:1792]
    gath[core, 2, z, xx, yy, :, 512:640] = jnp.where(core == 0, coarse, fine)

    whole = pl.ds(0, 4)
    halves = (pl.ds(0, 2), pl.ds(2, 2))

    def g_at(cls, spec):
        return gath.at[core, cls, spec[0], spec[1], spec[2]]

    def spec_of(order, values):
        spec = [None, None, None]
        for axis, value in zip(order, values):
            spec[axis] = value
        return spec

    for cls, order in enumerate(ORDERS):
        own = g_at(cls, pos)
        for d in (1, 2, 3):
            remote(own, own, ag_s.at[cls, 0, d], ag_r.at[cls, 0, d], along(order[0], d))
    for cls, order in enumerate(ORDERS):
        a1, a2, a3 = order
        for d in (1, 2, 3):
            src = list(pos)
            src[a1] = (pos[a1] + 4 - d) % 4
            landed(g_at(cls, src), ag_r.at[cls, 0, d])
    for phase in (1, 2):

        def block(cls, shift, half):
            a1, a2, a3 = ORDERS[cls]
            if phase == 1:
                return g_at(cls, spec_of((a1, a2, a3), (half, (pos[a2] + shift) % 4, pos[a3])))
            return g_at(cls, spec_of((a1, a2, a3), (half, whole, (pos[a3] + shift) % 4)))

        for cls, order in enumerate(ORDERS):
            if phase == 2:
                plane = g_at(cls, spec_of(order, (whole, whole, pos[order[2]])))
                remote(plane, plane, sib_s.at[cls, 0], sib_r.at[cls, 0], sibling)
            axis = order[phase]
            for half, delta, k in ((0, 1, 0), (1, 3, 1), (1, 1, 2), (0, 3, 3)):
                b = block(cls, 0, halves[half])
                remote(b, b, ag_s.at[cls, phase, k], ag_r.at[cls, phase, k], along(axis, delta))
        for cls, order in enumerate(ORDERS):
            axis = order[phase]
            b = block(cls, 3, halves[0])
            landed(b, ag_r.at[cls, phase, 0])
            remote(b, b, ag_s.at[cls, phase, 4], ag_r.at[cls, phase, 4], along(axis, 1))
            b = block(cls, 1, halves[1])
            landed(b, ag_r.at[cls, phase, 1])
            remote(b, b, ag_s.at[cls, phase, 5], ag_r.at[cls, phase, 5], along(axis, 3))
        for cls, order in enumerate(ORDERS):
            landed(block(cls, 3, halves[1]), ag_r.at[cls, phase, 2])
            landed(block(cls, 1, halves[0]), ag_r.at[cls, phase, 3])
            if phase == 2:
                for k, shift in ((1, 3), (2, 1)):
                    plane = block(cls, shift, whole)
                    remote(plane, plane, sib_s.at[cls, k], sib_r.at[cls, k], sibling)
        for cls, order in enumerate(ORDERS):
            landed(block(cls, 2, halves[0]), ag_r.at[cls, phase, 4])
            landed(block(cls, 2, halves[1]), ag_r.at[cls, phase, 5])
            if phase == 2:
                plane = block(cls, 2, whole)
                remote(plane, plane, sib_s.at[cls, 3], sib_r.at[cls, 3], sibling)
    for cls, order in enumerate(ORDERS):
        a1, a2, a3 = order
        for k, shift in ((0, 0), (1, 3), (2, 1), (3, 2)):
            spec = spec_of(order, (whole, whole, (pos[a3] + shift) % 4))
            landed(gath.at[other, cls, spec[0], spec[1], spec[2]], sib_r.at[cls, k])

    for copy in copies[2:]:
        copy.wait()

    def expert_in(i, _):
        gate = jnp.zeros((256, 256), F32)
        up = jnp.zeros((256, 256), F32)
        for h in range(2):
            for cls in range(3):
                n = WIDTHS[cls]
                k0 = h * HALF + cls * PART
                rows_in = gath[h, cls, i].reshape(256, PART)[:, :n]
                gate = gate + jnp.dot(rows_in, v_gate[0, k0 : k0 + n, :], preferred_element_type=F32)
                up = up + jnp.dot(rows_in, v_up[0, k0 : k0 + n, :], preferred_element_type=F32)
        act = gate / (1.0 + jnp.exp(-gate)) * up
        at = pl.multiple_of(i * 256, 256)
        inner[pl.ds(at, 256), :] = act.astype(BF16)
        return 0

    lax.fori_loop(0, 4, expert_in, 0)
    lane = lax.broadcasted_iota(jnp.int32, (256, 128), 1)

    def expert_out(i, half, dest):
        at = pl.multiple_of(i * 256, 256)
        weights = gath[0, 2, i, :, :, :, 512:640].astype(F32) + gath[1, 2, i, :, :, :, 512:640].astype(F32)
        weight = jnp.sum(
            jnp.where(lane == dp, weights.reshape(256, 128), 0.0), axis=1, keepdims=True
        )
        act = inner[pl.ds(at, 256), :]
        for cls in range(3):
            n = WIDTHS[cls]
            cols = pl.ds(pl.multiple_of(half * HALF + cls * PART, 128), n)
            y = jnp.dot(act, v_down[0, :, cols], preferred_element_type=F32) * weight
            dest[cls, i, :, :, :, 0:n] = y.astype(BF16).reshape(4, 4, 16, n)

    def to_sibling(i, _):
        expert_out(i, other, sib_out)
        return 0

    lax.fori_loop(0, 4, to_sibling, 0)
    remote(sib_out, sib_in, red_s.at[0], red_r.at[0], sibling)

    def to_self(i, _):
        expert_out(i, core, mix)
        return 0

    lax.fori_loop(0, 4, to_self, 0)
    landed(sib_in, red_r.at[0])

    def add_sibling(i, _):
        for cls in range(3):
            n = WIDTHS[cls]
            total = mix[cls, i, :, :, :, 0:n].astype(F32) + sib_in[cls, i, :, :, :, 0:n].astype(F32)
            mix[cls, i, :, :, :, 0:n] = total.astype(BF16)
        return 0

    lax.fori_loop(0, 4, add_sibling, 0)

    def cut(ref, n):
        return ref.at[..., pl.ds(0, n)]

    for phase in (2, 1):
        bt, bl, br = (t1, ul1, ur1) if phase == 2 else (t2, ul2, ur2)
        red = 0 if phase == 2 else 1

        def block(cls, shift, half):
            a1, a2, a3 = ORDERS[cls]
            if phase == 1:
                spec = spec_of((a1, a2, a3), (half, (pos[a2] + shift) % 4, pos[a3]))
            else:
                spec = spec_of((a1, a2, a3), (half, whole, (pos[a3] + shift) % 4))
            return (cls, spec[0], spec[1], spec[2], slice(None), pl.ds(0, WIDTHS[cls]))

        def temp(cls, half):
            a1, a2, a3 = ORDERS[cls]
            if phase == 1:
                return (cls, half, slice(None), pl.ds(0, WIDTHS[cls]))
            if a1 < a2:
                return (cls, half, whole, slice(None), pl.ds(0, WIDTHS[cls]))
            return (cls, whole, half, slice(None), pl.ds(0, WIDTHS[cls]))

        def send(cls, shift, half, buf, k, delta):
            remote(
                mix.at[block(cls, shift, halves[half])], buf.at[temp(cls, halves[half])],
                sum_s.at[cls, red, k], sum_r.at[cls, red, k], along(ORDERS[cls][phase], delta),
            )

        for cls in range(3):
            send(cls, 2, 0, bt, 0, 1)
            send(cls, 2, 1, bt, 1, 3)
            send(cls, 1, 1, bl, 2, 1)
            send(cls, 3, 0, br, 3, 3)
        for cls in range(3):
            for half, shift, buf, k, delta in ((0, 1, bl, 0, 1), (1, 3, br, 1, 3)):
                at, tmp = block(cls, shift, halves[half]), temp(cls, halves[half])
                landed(bt.at[tmp], sum_r.at[cls, red, k])
                mix[at] = (mix[at].astype(F32) + bt[tmp].astype(F32)).astype(BF16)
                send(cls, shift, half, buf, k + 4, delta)
        for cls in range(3):
            for half, ks in ((0, (4, 3)), (1, (2, 5))):
                at, tmp = block(cls, 0, halves[half]), temp(cls, halves[half])
                landed(bl.at[tmp], sum_r.at[cls, red, ks[0]])
                landed(br.at[tmp], sum_r.at[cls, red, ks[1]])
                total = mix[at].astype(F32) + bl[tmp].astype(F32) + br[tmp].astype(F32)
                mix[at] = total.astype(BF16)

    for cls, order in enumerate(ORDERS):
        a1 = order[0]
        for d in (1, 2, 3):
            coords = list(pos)
            coords[a1] = (pos[a1] + d) % 4
            src = mix.at[cls, coords[0], coords[1], coords[2], :, pl.ds(0, WIDTHS[cls])]
            dst = last.at[cls, d - 1, :, pl.ds(0, WIDTHS[cls])]
            remote(src, dst, sum_s.at[cls, 2, d], sum_r.at[cls, 2, d], along(a1, d))
    for cls in range(3):
        n = WIDTHS[cls]
        total = mix[cls, pos[0], pos[1], pos[2], :, 0:n].astype(F32)
        for d in (1, 2, 3):
            landed(last.at[cls, d - 1, :, pl.ds(0, n)], sum_r.at[cls, 2, d])
            total = total + last[cls, d - 1, :, 0:n].astype(F32)
        total = total + hidden[:, cls * PART : cls * PART + n]
        fin_out[0, :, cls * PART : cls * PART + n] = total[0:8]
        fin_out[1, :, cls * PART : cls * PART + n] = total[8:16]
    remote(fin_out.at[other], fin_in, pair_s.at[3], pair_r.at[3], sibling)
    out_ref[:, half_cols] = fin_out[core].astype(BF16)
    landed(fin_in, pair_r.at[3])
    out_ref[:, pl.ds(pl.multiple_of(other * HALF, 128), HALF)] = fin_in[...].astype(BF16)
    for src, ssem in sent:
        pltpu.make_async_copy(src, src, ssem).wait()


def layer(attended, resid, member, gain, router, w_uv, w_out, w_gate, w_up, w_down):
    vmem = pl.BlockSpec(memory_space=pltpu.VMEM)
    hbm = pl.BlockSpec(memory_space=pl.ANY)
    dma = pltpu.SemaphoreType.DMA
    grid = (3, 4, 4, 4, 16, PART)
    return pl.pallas_call(
        layer_kernel,
        out_shape=jax.ShapeDtypeStruct((8, 2 * HALF), BF16),
        in_specs=[vmem] * 5 + [hbm] * 5,
        out_specs=vmem,
        scratch_shapes=[
            pltpu.VMEM((8, 64, LATENT), BF16),
            pltpu.VMEM((512, 1024), BF16),
            pltpu.VMEM((2, 4, 16, HALF), BF16),
            pltpu.VMEM((8, 16, HALF), BF16),
            pltpu.VMEM((16, HALF), F32),
            pltpu.VMEM((16, 128), F32),
            pltpu.VMEM((2, 16, 128), F32),
            pltpu.VMEM((2, 16, 128), F32),
            pltpu.VMEM((16, HALF), F32),
            pltpu.VMEM((2,) + grid, BF16),
            pltpu.VMEM(w_uv.shape, BF16),
            pltpu.VMEM(w_out.shape, BF16),
            pltpu.VMEM(w_gate.shape, BF16),
            pltpu.VMEM(w_up.shape, BF16),
            pltpu.VMEM(w_down.shape, BF16),
            pltpu.VMEM((1024, 256), BF16),
            pltpu.VMEM(grid, BF16),
            pltpu.VMEM(grid, BF16),
            pltpu.VMEM(grid, BF16),
            pltpu.VMEM((3, 4, 4, 16, PART), BF16),
            pltpu.VMEM((3, 4, 4, 16, PART), BF16),
            pltpu.VMEM((3, 4, 4, 16, PART), BF16),
            pltpu.VMEM((3, 4, 16, PART), BF16),
            pltpu.VMEM((3, 4, 16, PART), BF16),
            pltpu.VMEM((3, 4, 16, PART), BF16),
            pltpu.VMEM((3, 3, 16, PART), BF16),
            pltpu.VMEM((2, 8, HALF), F32),
            pltpu.VMEM((8, HALF), F32),
            dma((5,)), dma, dma((8,)), dma((8,)), dma((8,)), dma((8,)), dma((4,)), dma((4,)),
            dma((3, 3, 6)), dma((3, 3, 6)), dma((3, 4)), dma((3, 4)), dma((1,)), dma((1,)),
            dma((3, 3, 6)), dma((3, 3, 6)),
        ],
        compiler_params=pltpu.CompilerParams(
            collective_id=1, has_side_effects=True, vmem_limit_bytes=56 * 2**20
        ),
        name="layer",
    )(attended, resid, member, gain, router, w_uv, w_out, w_gate, w_up, w_down)


def shards(
    cache_pool,
    page_table,
    page_counts,
    queries,
    new_latent,
    residual,
    w_uv,
    w_out,
    norm_gain,
    w_router,
    w_gate,
    w_up,
    w_down,
    routes,
):
    ep_size = lax.axis_size("ep")
    my_index = lax.axis_index("dp") * ep_size + lax.axis_index("ep")
    pool_dev = cache_pool.shape[0]
    owner_all = page_table // pool_dev
    local_all = page_table % pool_dev
    source = jnp.sum(jnp.where(owner_all == my_index, local_all, 0), axis=1)
    outgoing = cache_pool[source]
    incoming = lax.all_to_all(outgoing, ("dp", "ep"), split_axis=0, concat_axis=0, tiled=True)
    owner = lax.dynamic_index_in_dim(owner_all, my_index, 0, keepdims=False)
    counts = page_counts[0]
    starts = jnp.cumsum(counts) - counts
    own = jnp.pad(jnp.transpose(new_latent, (1, 0, 2)), ((0, 0), (0, 14), (0, 0)))
    attended = attend(owner, starts, counts, queries, own, incoming)

    d_model = residual.shape[2]
    resid = residual.reshape(8, 2, d_model // 2).transpose(1, 0, 2).astype(F32)
    experts = w_router.shape[1]
    member = jnp.any(routes.reshape(8, -1)[:, :, None] == jnp.arange(128)[None, None, :], axis=1)
    router = jnp.pad(w_router.T, ((0, 128 - experts), (0, 0)))
    out = layer(
        attended, resid, member.astype(F32), norm_gain.reshape(1, -1), router,
        w_uv, w_out, w_gate, w_up, w_down,
    )
    return out.reshape(residual.shape)


def solution(mesh):
    return jax.shard_map(
        shards,
        mesh=mesh,
        in_specs=(
            P(("dp", "ep"), None, None),
            P(),
            P(("dp", "ep"), None),
            P(None, ("dp", "ep"), None, None),
            P(None, ("dp", "ep"), None),
            P(None, ("dp", "ep"), None),
            P("ep", None, None),
            P("ep", None),
            P(),
            P(),
            P("dp", None, "ep"),
            P("dp", None, "ep"),
            P("dp", "ep", None),
            P(None, ("dp", "ep"), None),
        ),
        out_specs=P(None, ("dp", "ep"), None),
        check_vma=False,
    )
```

time: 577 us -> 275 us (0.48); the launches traced: 567 us -> 274 us
  waiting for transfers between devices: 287 us -> 120 us
  Pallas kernels: 0 us -> 109 us
  matrix products: 98.2 us -> 0 us
  local copies, waits for them, and re-layouts: 96 us -> 31.7 us
  starting transfers between devices: 46.3 us -> 12 us
  other arithmetic: 25 us -> 1.7 us
  between operations: 14.9 us -> 0.12 us
    all_to_all x6 -> x0, waiting for transfers between devices: 134 us -> none  [the longest x2 69.4 us: shards(): lax.all_to_all(spread, ('dp', 'ep'), split_axis=0, concat_axis=0, tiled=T...]
    pallas_call x0 -> x2, Pallas kernels: none -> 109 us  [the longest x1 97.2 us: layer(): pl.pallas_call(layer_kernel, out_shape=jax.ShapeDtypeStruct((8, 2 * HALF)...]
    dot_general x31 -> x0, matrix products: 98.2 us -> none  [the longest x2 33.9 us: shards(): jnp.dot(member_real, per_page_out.reshape(page_total, -1), precision=high...]
    unnamed x2 -> x0, waiting for transfers between devices: 59.3 us -> none
    reshape x8 -> x2, local copies, waits for them, and re-layouts: 48.3 us -> 2.07 us  [the longest x1 1.46 us: shards(): return out.reshape(residual.shape)]
    all_to_all x6 -> x0, starting transfers between devices: 34.3 us -> none  [the longest x2 15.2 us: shards(): lax.all_to_all(spread, ('dp', 'ep'), split_axis=0, concat_axis=0, tiled=T...]
    all_to_all x1, waiting for transfers between devices: 94.2 us -> 120 us  [shards(): lax.all_to_all(outgoing, ('dp', 'ep'), split_axis=0, concat_axis=0, tiled...]
    reduce_sum x13 -> x1, other arithmetic: 11.6 us -> 0.81 us  [shards(): source = jnp.sum(jnp.where(owner_all == my_index, local_all, 0), axis=1)]
  transfers between devices with their start and end apart: 8 -> 1, of which waited for: 7 -> 1; matrix products, arithmetic and copies ran while one was open for 18% -> 1% of each run, Pallas kernels for 0% -> 0%
where the time goes in v1:
time: 275 us; the launch traced here: 274 us
  waiting for transfers between devices  120 us (44%)
  Pallas kernels  109 us (40%)
  local copies, waits for them, and re-layouts  31.7 us (12%)
  starting transfers between devices  12 us (4%)
    all_to_all x1, waiting for transfers between devices, shards(): lax.all_to_all(outgoing, ('dp', 'ep'), split_axis=0, concat_axis=0, tiled...  120 us
    pallas_call x1, Pallas kernels, layer(): pl.pallas_call(layer_kernel, out_shape=jax.ShapeDtypeStruct((8, 2 * HALF)...  97.2 us
    unnamed x18, local copies, waits for them, and re-layouts  15.6 us
    all_to_all x1, starting transfers between devices, shards(): lax.all_to_all(outgoing, ('dp', 'ep'), split_axis=0, concat_axis=0, tiled...  12 us
    gather x1, local copies, waits for them, and re-layouts, shards(): outgoing = cache_pool[source]  11.7 us
    pallas_call x1, Pallas kernels, attend(): pl.pallas_call(attend_kernel, out_shape=jax.ShapeDtypeStruct((8, 64, LATE...  11.4 us
  transfers between devices with their start and end apart: 1, of which 1 were waited for; matrix products, arithmetic and copies ran while one was open for 1% of the time, Pallas kernels for 0%

profile of v1, /device:TPU:1, one launch (start us, length us, event | category | flops | bytes accessed | tf_op | source)
XLA Modules:
  0.0 274.4 jit_solution(14607973362732913891)
XLA Ops:
  0.0 0.8 fusion.1
  0.8 14.8 %copy.20 = bf16[128,64,576]{2,1,0:T(8,128)(2,1)} copy(bf16[128,64,576]{0,2,1:T(8,128)(2,1)} %param.14) | data formatting | bytes 18874368 | tf_op args[0]
  15.6 11.7 %gather_fusion = bf16[128,64,576]{2,1,0:T(8,128)(2,1)} fusion(bf16[128,64,576]{2,1,0:T(8,128)(2,1)} %copy.20, s32[1024]{0:T(1024)S(1)} %pad_clamp_fusion), kind=kCustom, calls=%fused_computation | custom fusion | bytes 18874880 | tf_op jit(solution)/shard_map/gather | solution.py:499
  27.2 0.0 copy-start.6
  27.2 0.0 copy-start.2
  27.3 0.0 copy-start.4
  27.3 0.0 copy-start.5
  27.3 0.0 copy-start.7
  27.3 0.0 copy-start.3
  27.3 0.0 copy-start.1
  27.3 12.0 %all-to-all-start = ((bf16[128,64,576]{2,1,0:T(8,128)(2,1)}), bf16[128,64,576]{2,1,0:T(8,128)(2,1)}, u32[]{:S(2)}, u32[]{:S(2)}) async-start(bf16[128,64,576]{2,1,0:T(8,128)(2,1)} %gather_fusion), calls=%async_computation | async-start | bytes 20971520 | tf_op jit(solution)/shard_map/all_to_all | solution.py:500
  39.3 0.0 copy-done.6
  39.3 0.0 copy-done.2
  39.3 0.2 reduce-window.9
  39.5 0.0 copy-done.4
  39.5 0.1 reshape.54
  39.6 0.7 copy.24
  40.2 0.0 copy-done.5
  40.2 0.6 reshape.52.gain
  40.8 0.0 copy-done.7
  40.8 0.1 fusion.3
  40.9 0.6 convert_element_type.17.member
  41.5 0.0 copy-done.3
  41.6 1.4 pad.9.router
  43.0 0.2 dynamic-slice_reduce_fusion.owner
  43.2 120.4 %all-to-all-done.slots = bf16[128,64,576]{2,1,0:T(8,128)(2,1)} async-done(((bf16[128,64,576]{2,1,0:T(8,128)(2,1)}), bf16[128,64,576]{2,1,0:T(8,128)(2,1)}, u32[]{:S(2)}, u32[]{:S(2)}) %all-to-all-start) | async-done | bytes 9437216 | tf_op jit(solution)/shard_map/all_to_all | solution.py:500
  163.6 0.0 copy-done.1
  163.6 11.4 %attend.1.attended = bf16[8,64,512]{2,1,0:T(8,128)(2,1)S(1)} custom-call(s32[64]{0:T(128)S(1)} %dynamic-slice_reduce_fusion.owner, s32[4]{0:T(128)S(1)} %bitcast_subtract_fusion.starts, s32[4]{0:T(128)S(1)} %bitcast.18, bf16[2,4,64,576]{3,2,1,0:T(8,128)(2,1)S(1)} %copy-done.1, bf16[4,16,576]{2,1,0:T(8,128)(2,1)S(1)} %pad.8.own_ref, ...), custom_call_target="tpu_custom_call" | custom-call | tf_op jit(solution)/shard_map/attend/pallas_call | solution.py:97
  174.9 0.0 copy-start
  174.9 0.8 copy-done
  175.7 97.2 %layer.1 = bf16[8,3584]{1,0:T(8,128)(2,1)} custom-call(bf16[8,64,512]{2,1,0:T(8,128)(2,1)} %copy-done, f32[2,8,1792]{2,1,0:T(8,128)} %bitcast.19, f32[8,128]{1,0:T(8,128)} %convert_element_type.17.member, f32[1,3584]{1,0:T(1,128)} %reshape.52.gain, f32[128,3584]{1,0:T(8,128)} %pad.9.router, bf16[8,512,128]{2,1,0:T(8,128)(2,1)} %w_uv.1, ...), custom_call_target="tpu_custom_call" | custom-call | tf_op jit(solution)/shard_map/layer/pallas_call | solution.py:432
  272.9 1.5 reshape.53
  (5 shorter events, 0.0 us)
Async XLA Ops:
  27.2 12.0 %copy-start.6 = (bf16[2,4,576]{2,1,0:T(4,128)(2,1)S(1)}, bf16[2,4,576]{2,1,0:T(4,128)(2,1)}, u32[]{:S(2)}) copy-start(bf16[2,4,576]{2,1,0:T(4,128)(2,1)} %param.18) | copy-start | bytes 27652
  27.2 12.1 %copy-start.2 = (s32[1,4]{1,0:T(1,128)S(1)}, s32[1,4]{1,0:T(1,128)}, u32[]{:S(2)}) copy-start(s32[1,4]{1,0:T(1,128)} %param.16) | copy-start | bytes 52
  27.3 12.2 %copy-start.4 = (bf16[2,4,3584]{2,1,0:T(4,128)(2,1)S(1)}, bf16[2,4,3584]{2,1,0:T(4,128)(2,1)}, u32[]{:S(2)}) copy-start(bf16[2,4,3584]{2,1,0:T(4,128)(2,1)} %param.19) | copy-start | bytes 172036
  27.3 13.0 %copy-start.5 = (f32[3584]{0:T(1024)S(1)}, f32[3584]{0:T(1024)}, u32[]{:S(2)}) copy-start(f32[3584]{0:T(1024)} %param.22) | copy-start | bytes 43012
  27.3 13.6 %copy-start.7 = (s32[2,4,8]{2,1,0:T(4,128)S(1)}, s32[2,4,8]{2,1,0:T(4,128)}, u32[]{:S(2)}) copy-start(s32[2,4,8]{2,1,0:T(4,128)} %param.27) | copy-start | bytes 772
  27.3 14.3 %copy-start.3 = (f32[3584,16]{0,1:T(8,128)S(1)}, f32[3584,16]{0,1:T(8,128)}, u32[]{:S(2)}) copy-start(f32[3584,16]{0,1:T(8,128)} %param.23) | copy-start | bytes 688132
  27.3 136.3 %copy-start.1 = (bf16[2,4,64,576]{3,2,1,0:T(8,128)(2,1)S(1)}, bf16[2,4,64,576]{3,2,1,0:T(8,128)(2,1)}, u32[]{:S(2)}) copy-start(bf16[2,4,64,576]{3,2,1,0:T(8,128)(2,1)} %q_ref.1) | copy-start | bytes 1769476
  27.3 136.3 %all-to-all-start = ((bf16[128,64,576]{2,1,0:T(8,128)(2,1)}), bf16[128,64,576]{2,1,0:T(8,128)(2,1)}, u32[]{:S(2)}, u32[]{:S(2)}) async-start(bf16[128,64,576]{2,1,0:T(8,128)(2,1)} %gather_fusion), calls=%async_computation | async-start | bytes 20971520 | tf_op jit(solution)/shard_map/all_to_all | solution.py:500
  174.9 0.8 copy-start

commit v2 on v1

--- a/solution.py
+++ b/solution.py
@@ -12,6 +12,7 @@
 BF16 = jnp.bfloat16
 
 LATENT = 512
+ROPE = 64
 PAGE = 64
 TILE = 8
 score_scale = 192.0 ** (-0.5)
@@ -24,42 +25,257 @@
 WIDTHS = (640, 640, 512)
 
 
-def attend_kernel(owner, starts, counts, q_ref, own_ref, slots, out_ref, keys, scores, sem):
-    rows = 64 * PAGE
+def exchange_kernel(
+    source, pool, out,
+    pool_v, slots, held1, held2, stage,
+    psem, lsem, csem, send1, recv1, send2, recv2, send3, recv3,
+):
+    dp = lax.axis_index("dp")
+    ep = lax.axis_index("ep")
+    pos = (dp // 4, dp % 4, ep // 2)
+    core = ep % 2
+    other = 1 - core
+    whole = pl.ds(0, 4)
+
+    loads = [
+        pltpu.make_async_copy(
+            pool.at[pl.ds(i * 16, 16)], pool_v.at[pl.ds(i * 16, 16)], psem.at[i]
+        )
+        for i in range(4)
+    ]
+    for load in loads:
+        load.start()
+
+    def along(axis, delta, c):
+        coords = list(pos)
+        coords[axis] = (coords[axis] + delta) % 4
+        return (coords[0] * 4 + coords[1], coords[2] * 2 + c)
+
+    def spec_of(order, values):
+        spec = [None, None, None]
+        for axis, value in zip(order, values):
+            spec[axis] = value
+        return tuple(spec)
+
+    barrier = pltpu.get_barrier_semaphore()
+    peers = [along(a, d, c) for a in range(3) for d in (1, 2, 3) for c in (core, other)]
+    peers.append(along(0, 0, other))
+    for peer in peers:
+        pl.semaphore_signal(barrier, inc=1, device_id=peer, device_id_type=MESH)
+
+    lane = lax.broadcasted_iota(jnp.int32, (128, 128), 1)
+    onehot = jnp.where(source[...] == lane, 1.0, 0.0).astype(BF16)
+
+    def put(cls, row, pieces):
+        for j in range(0, 16, 4):
+            x = jnp.concatenate(pieces(j), axis=0)
+            y = lax.dot_general(onehot, x, (((1,), (1,)), ((), ())), preferred_element_type=F32)
+            for i in range(4):
+                stage[:, j + i, :] = y[:, i * 128 : (i + 1) * 128]
+        at = pl.multiple_of(row, 16)
+        block = stage[...].astype(BF16).reshape(4, 4, 4, 2, 16, 128)
+        slots[cls, :, :, :, :, pl.ds(at, 16), :] = block
+
+    def latent_rows(cls, chunk, first, count, row):
+        def unit(u, _):
+            def pieces(j):
+                t = (first + u) * 16 + j
+                return [pool_v[pl.ds(t, 4), chunk * 128 : (chunk + 1) * 128, :].reshape(512, 128)]
+
+            put(cls, row + u * 16, pieces)
+            return 0
+
+        lax.fori_loop(0, count, unit, 0)
+
+    def rope_rows(cls, row):
+        def unit(u, _):
+            def pieces(j):
+                found = []
+                for i in range(4):
+                    found.append(pool_v[u * 16 + j + i, 512:576, :])
+                    found.append(pool_v[32 + u * 16 + j + i, 512:576, :])
+                return found
+
+            put(cls, row + u * 16, pieces)
+            return 0
+
+        lax.fori_loop(0, 2, unit, 0)
+
+    sends = []
+
+    def remote(src, dst, ssem, rsem, peer):
+        pltpu.make_async_remote_copy(
+            src_ref=src, dst_ref=dst, send_sem=ssem, recv_sem=rsem,
+            device_id=peer, device_id_type=MESH,
+        ).start()
+        sends.append((src, ssem))
+
+    def landed(ref, sem):
+        pltpu.make_async_copy(ref, ref, sem).wait()
+
+    for load in loads:
+        load.wait()
+    for cls, order in enumerate(ORDERS):
+        a1, a2, a3 = order
+        latent_rows(cls, cls, 0, 4, 0)
+        if cls < 2:
+            latent_rows(cls, 3, 2 * cls, 2, 64)
+        else:
+            rope_rows(cls, 64)
+        if cls == 0:
+            pl.semaphore_wait(barrier, len(peers))
+        for d in (1, 2, 3):
+            src = spec_of(order, ((pos[a1] + d) % 4, whole, whole))
+            dst = spec_of(order, (pos[a1], whole, whole))
+            remote(
+                slots.at[(cls,) + src], held1.at[(cls,) + dst],
+                send1.at[cls, d], recv1.at[cls, d], along(a1, d, core),
+            )
+        own = spec_of(order, (pos[a1], whole, whole))
+        pltpu.make_async_copy(slots.at[(cls,) + own], held1.at[(cls,) + own], lsem.at[cls]).start()
+
+    def second(cls, buf, e):
+        a1, a2, a3 = order = ORDERS[cls]
+        src1 = (pos[a1] + 4 - e) % 4
+        for d in (1, 2, 3):
+            src = spec_of(order, (src1, (pos[a2] + d) % 4, whole))
+            dst = spec_of(order, (src1, pos[a2], whole))
+            remote(
+                buf.at[(cls,) + src], held2.at[(cls,) + dst],
+                send2.at[cls, d, e], recv2.at[cls, d, e], along(a2, d, core),
+            )
+
+    def third(cls, buf, f):
+        a1, a2, a3 = order = ORDERS[cls]
+        src2 = (pos[a2] + 4 - f) % 4
+        for d in (1, 2, 3, 0):
+            for k, c in ((0, core), (1, other)):
+                src = spec_of(order, (whole, src2, (pos[a3] + d) % 4))
+                dst = spec_of(order, (whole, src2, pos[a3]))
+                a = buf.at[(cls,) + src + (c,)]
+                b = out.at[dst + (core, cls)]
+                if d == 0 and k == 0:
+                    pltpu.make_async_copy(a, b, csem.at[cls, f]).start()
+                else:
+                    remote(a, b, send3.at[cls, f, d, k], recv3.at[cls, f, d, k], along(a3, d, c))
+
+    for cls in range(3):
+        second(cls, slots, 0)
+    for e in (1, 3, 2):
+        for cls, order in enumerate(ORDERS):
+            src1 = (pos[order[0]] + 4 - e) % 4
+            at = spec_of(order, (src1, whole, whole))
+            landed(held1.at[(cls,) + at], recv1.at[cls, e])
+            second(cls, held1, e)
+    for cls, order in enumerate(ORDERS):
+        own = spec_of(order, (pos[order[0]], whole, whole))
+        landed(held1.at[(cls,) + own], lsem.at[cls])
+        third(cls, held1, 0)
+    for f in (1, 3, 2):
+        for cls, order in enumerate(ORDERS):
+            a1, a2, a3 = order
+            for e in range(4):
+                at = spec_of(order, ((pos[a1] + 4 - e) % 4, (pos[a2] + 4 - f) % 4, whole))
+                landed(held2.at[(cls,) + at], recv2.at[cls, f, e])
+            third(cls, held2, f)
+    for cls, order in enumerate(ORDERS):
+        a1, a2, a3 = order
+        for f in range(4):
+            for d in range(4):
+                for k, c in ((0, core), (1, other)):
+                    at = spec_of(order, (whole, (pos[a2] + 4 - f) % 4, (pos[a3] + 4 - d) % 4))
+                    ref = out.at[at + (c, cls)]
+                    landed(ref, csem.at[cls, f] if d == 0 and k == 0 else recv3.at[cls, f, d, k])
+    for src, ssem in sends:
+        landed(src, ssem)
+
+
+def exchange(source, pool):
+    vmem = pl.BlockSpec(memory_space=pltpu.VMEM)
+    hbm = pl.BlockSpec(memory_space=pl.ANY)
+    dma = pltpu.SemaphoreType.DMA
+    held = (3, 4, 4, 4, 2, 96, 128)
+    return pl.pallas_call(
+        exchange_kernel,
+        out_shape=jax.ShapeDtypeStruct((4, 4, 4, 2, 3, 96, 128), BF16),
+        in_specs=[vmem, hbm],
+        out_specs=hbm,
+        scratch_shapes=[
+            pltpu.VMEM(pool.shape, BF16),
+            pltpu.VMEM(held, BF16),
+            pltpu.VMEM(held, BF16),
+            pltpu.VMEM(held, BF16),
+            pltpu.VMEM((128, 16, 128), F32),
+            dma((4,)), dma((3,)), dma((3, 4)), dma((3, 4)), dma((3, 4)), dma((3, 4, 4)),
+            dma((3, 4, 4)), dma((3, 4, 4, 2)), dma((3, 4, 4, 2)),
+        ],
+        compiler_params=pltpu.CompilerParams(
+            collective_id=2, has_side_effects=True, vmem_limit_bytes=56 * 2**20
+        ),
+        name="exchange",
+    )(source, pool)
+
+
+def attend_kernel(
+    owner, starts, counts, q_ref, own_ref, slots, out_ref, keys, last, ropes, scores, sem
+):
+    pages = 64
 
     def fetch(j, _):
         at = pl.multiple_of(j * PAGE, PAGE)
-        pltpu.make_async_copy(slots.at[owner[j]], keys.at[pl.ds(at, PAGE)], sem).start()
+        slot = slots.at[owner[j]]
+        pltpu.make_async_copy(
+            slot.at[:, pl.ds(0, 64), :], keys.at[:, pl.ds(at, PAGE), :], sem.at[0]
+        ).start()
+        pltpu.make_async_copy(
+            slot.at[pl.ds(0, 2), pl.ds(64, 32), :], last.at[j], sem.at[1]
+        ).start()
+        pltpu.make_async_copy(slot.at[2, pl.ds(64, 32), :], ropes.at[j], sem.at[2]).start()
         return 0
 
-    lax.fori_loop(0, 64, fetch, 0)
+    lax.fori_loop(0, pages, fetch, 0)
 
     def clear(j, _):
-        at = pl.multiple_of(rows + j * PAGE, PAGE)
-        keys[pl.ds(at, PAGE), :] = jnp.zeros((PAGE, keys.shape[1]), BF16)
+        at = pl.multiple_of((pages + j) * PAGE, PAGE)
+        keys[:, pl.ds(at, PAGE), :] = jnp.zeros((3, PAGE, 128), BF16)
+        last[pages + j] = jnp.zeros((2, 32, 128), BF16)
+        ropes[pages + j] = jnp.zeros((32, 128), BF16)
         return 0
 
     lax.fori_loop(0, TILE, clear, 0)
-    filled = keys.at[pl.ds(0, rows)]
-    pltpu.make_async_copy(filled, filled, sem).wait()
+    for k, ref in enumerate(
+        (keys.at[:, pl.ds(0, pages * PAGE), :], last.at[pl.ds(0, pages)], ropes.at[pl.ds(0, pages)])
+    ):
+        pltpu.make_async_copy(ref, ref, sem.at[k]).wait()
     width = TILE * PAGE
     step_of = lax.broadcasted_iota(jnp.int32, (128, 16), 0) // 64
     token = lax.broadcasted_iota(jnp.int32, (128, 16), 1)
+    low = lax.broadcasted_iota(jnp.int32, (TILE, 32, 128), 2) < ROPE
+
+    def values_of(page):
+        at = pl.multiple_of(page * PAGE, PAGE)
+        parts = [keys[k, pl.ds(at, width), :] for k in range(3)]
+        parts.append(last[pl.ds(page, TILE)].reshape(width, 128))
+        return jnp.concatenate(parts, axis=1)
 
     def request(r, _):
         q = jnp.concatenate([q_ref[0, r], q_ref[1, r]], axis=0)
         own = own_ref[r]
         s_own = lax.dot_general(q, own, (((1,), (1,)), ((), ())), preferred_element_type=F32)
         s_own = jnp.where(token <= step_of, s_own * score_scale, -jnp.inf)
-        start = starts[r] * PAGE
+        q_rope = q[:, LATENT:]
+        q_wide = jnp.concatenate([q[:, :LATENT], q_rope, q_rope], axis=1)
+        start = starts[r]
         length = counts[r] * PAGE
         tiles = (length + width - 1) // width
 
         def score(t, top):
-            at = pl.multiple_of(start + t * width, PAGE)
-            s = lax.dot_general(
-                q, keys[pl.ds(at, width), :], (((1,), (1,)), ((), ())), preferred_element_type=F32
-            )
+            page = start + t * TILE
+            rope = ropes[pl.ds(page, TILE)]
+            zero = jnp.zeros_like(rope)
+            pair = jnp.concatenate([jnp.where(low, rope, zero), jnp.where(low, zero, rope)], axis=1)
+            key = jnp.concatenate([values_of(page), pair.reshape(width, 128)], axis=1)
+            s = lax.dot_general(q_wide, key, (((1,), (1,)), ((), ())), preferred_element_type=F32)
             place = t * width + lax.broadcasted_iota(jnp.int32, (128, width), 1)
             s = jnp.where(place < length, s * score_scale, -jnp.inf)
             scores[t] = s
@@ -72,11 +288,10 @@
 
         def mix(t, carry):
             total, acc = carry
-            at = pl.multiple_of(start + t * width, PAGE)
             p = jnp.exp(scores[t] - top)
             total = total + jnp.sum(p, axis=1, keepdims=True)
             acc = acc + jnp.dot(
-                p.astype(BF16), keys[pl.ds(at, width), :LATENT], preferred_element_type=F32
+                p.astype(BF16), values_of(start + t * TILE), preferred_element_type=F32
             )
             return total, acc
 
@@ -100,9 +315,11 @@
         in_specs=[smem, smem, smem, vmem, vmem, pl.BlockSpec(memory_space=pl.ANY)],
         out_specs=vmem,
         scratch_shapes=[
-            pltpu.VMEM(((64 + TILE) * PAGE, slots.shape[-1]), BF16),
+            pltpu.VMEM((3, (64 + TILE) * PAGE, 128), BF16),
+            pltpu.VMEM((64 + TILE, 2, 32, 128), BF16),
+            pltpu.VMEM((64 + TILE, 32, 128), BF16),
             pltpu.VMEM((32 // TILE, 128, TILE * PAGE), F32),
-            pltpu.SemaphoreType.DMA,
+            pltpu.SemaphoreType.DMA((3,)),
         ],
         compiler_params=pltpu.CompilerParams(vmem_limit_bytes=40 * 2**20),
         name="attend",
@@ -496,8 +713,8 @@
     owner_all = page_table // pool_dev
     local_all = page_table % pool_dev
     source = jnp.sum(jnp.where(owner_all == my_index, local_all, 0), axis=1)
-    outgoing = cache_pool[source]
-    incoming = lax.all_to_all(outgoing, ("dp", "ep"), split_axis=0, concat_axis=0, tiled=True)
+    incoming = exchange(source.reshape(-1, 1), jnp.transpose(cache_pool, (1, 2, 0)))
+    incoming = incoming.reshape(-1, 3, 96, 128)
     owner = lax.dynamic_index_in_dim(owner_all, my_index, 0, keepdims=False)
     counts = page_counts[0]
     starts = jnp.cumsum(counts) - counts

time: 275 us -> 249 us (0.905)
  Pallas kernels: 109 us -> 237 us
  waiting for transfers between devices: 120 us -> 0 us
  local copies, waits for them, and re-layouts: 31.7 us -> 9.66 us
  starting transfers between devices: 12 us -> 0 us
    pallas_call x0 -> x1, Pallas kernels: none -> 129 us  [exchange(): pl.pallas_call(exchange_kernel, out_shape=jax.ShapeDtypeStruct((4, 4, 4,...]
    all_to_all x1 -> x0, waiting for transfers between devices: 120 us -> none  [shards(): lax.all_to_all(outgoing, ('dp', 'ep'), split_axis=0, concat_axis=0, tiled...]
    all_to_all x1 -> x0, starting transfers between devices: 12 us -> none  [shards(): lax.all_to_all(outgoing, ('dp', 'ep'), split_axis=0, concat_axis=0, tiled...]
    gather x1 -> x0, local copies, waits for them, and re-layouts: 11.7 us -> none  [shards(): outgoing = cache_pool[source]]
    unnamed x18 -> x19, local copies, waits for them, and re-layouts: 15.6 us -> 4.52 us
  transfers between devices with their start and end apart: 1 -> 0, of which waited for: 1 -> 0; matrix products, arithmetic and copies ran while one was open for 1% -> 0% of each run, Pallas kernels for 0% -> 0%
where the time goes in v2:
time: 249 us; the launch traced here: 248 us
  Pallas kernels  237 us (95%)
  local copies, waits for them, and re-layouts  9.66 us (4%)
    pallas_call x1, Pallas kernels, exchange(): pl.pallas_call(exchange_kernel, out_shape=jax.ShapeDtypeStruct((4, 4, 4,...  129 us
    pallas_call x1, Pallas kernels, layer(): pl.pallas_call(layer_kernel, out_shape=jax.ShapeDtypeStruct((8, 2 * HALF)...  95.5 us
    pallas_call x1, Pallas kernels, attend(): pl.pallas_call(attend_kernel, out_shape=jax.ShapeDtypeStruct((8, 64, LATE...  12.4 us

profile of v2, /device:TPU:1, one launch (start us, length us, event | category | flops | bytes accessed | tf_op | source)
XLA Modules:
  0.0 248.2 jit_solution(8971059598665150472)
XLA Ops:
  0.0 0.8 fusion.1
  0.8 0.2 dynamic-slice_reduce_fusion.owner
  1.0 0.7 copy.21.source
  1.7 0.0 copy-start.7
  1.7 0.0 copy-start.3
  1.7 0.0 copy-start.2
  1.7 128.9 %exchange.1 = bf16[4,4,4,2,3,96,128]{6,5,4,3,2,1,0:T(8,128)(2,1)} custom-call(s32[128,1]{1,0:T(8,128)} %copy.21.source, bf16[64,576,128]{2,1,0:T(8,128)(2,1)} %bitcast.19), custom_call_target="tpu_custom_call" | custom-call | tf_op jit(solution)/shard_map/exchange/pallas_call | solution.py:198
  130.6 0.0 copy-done.7
  130.7 0.0 copy-done.3
  130.7 0.2 reduce-window.9
  130.9 0.0 copy-done.2
  130.9 0.0 copy-start
  130.9 3.7 %copy-done = bf16[4,4,4,2,3,96,128]{6,5,4,3,2,1,0:T(8,128)(2,1)S(1)} copy-done((bf16[4,4,4,2,3,96,128]{6,5,4,3,2,1,0:T(8,128)(2,1)S(1)}, bf16[4,4,4,2,3,96,128]{6,5,4,3,2,1,0:T(8,128)(2,1)}, u32[]{:S(2)}) %copy-start) | copy-done | bytes 9437208
  134.6 0.0 copy-start.4
  134.6 12.4 %attend.1.attended = bf16[8,64,512]{2,1,0:T(8,128)(2,1)S(1)} custom-call(s32[64]{0:T(128)S(1)} %dynamic-slice_reduce_fusion.owner, s32[4]{0:T(128)S(1)} %bitcast_subtract_fusion.starts, s32[4]{0:T(128)S(1)} %bitcast.18, bf16[2,4,64,576]{3,2,1,0:T(8,128)(2,1)S(1)} %copy-done.2, bf16[4,16,576]{2,1,0:T(8,128)(2,1)S(1)} %pad.8.own_ref, ...), custom_call_target="tpu_custom_call" | custom-call | tf_op jit(solution)/shard_map/attend/pallas_call | solution.py:312
  147.0 0.0 copy-start.1
  147.0 0.8 copy-done.1
  147.8 0.0 copy-start.5
  147.8 0.0 copy-start.6
  147.8 0.0 copy-start.8
  147.8 0.0 copy-done.4
  147.8 1.4 pad.9.router
  149.2 0.0 copy-done.5
  149.2 0.1 reshape.49
  149.3 0.6 copy.25
  150.0 0.0 copy-done.6
  150.0 0.6 reshape.47.gain
  150.6 0.0 copy-done.8
  150.6 0.1 fusion.3
  150.7 0.6 convert_element_type.17.member
  151.3 95.5 %layer.1 = bf16[8,3584]{1,0:T(8,128)(2,1)} custom-call(bf16[8,64,512]{2,1,0:T(8,128)(2,1)} %copy-done.1, f32[2,8,1792]{2,1,0:T(8,128)} %bitcast.20, f32[8,128]{1,0:T(8,128)} %convert_element_type.17.member, f32[1,3584]{1,0:T(1,128)} %reshape.47.gain, f32[128,3584]{1,0:T(8,128)} %pad.9.router, bf16[8,512,128]{2,1,0:T(8,128)(2,1)} %w_uv.1, ...), custom_call_target="tpu_custom_call" | custom-call | tf_op jit(solution)/shard_map/layer/pallas_call | solution.py:649
  246.8 1.5 reshape.48
  (3 shorter events, 0.0 us)
Async XLA Ops:
  1.7 128.9 %copy-start.7 = (bf16[2,4,576]{2,1,0:T(4,128)(2,1)S(1)}, bf16[2,4,576]{2,1,0:T(4,128)(2,1)}, u32[]{:S(2)}) copy-start(bf16[2,4,576]{2,1,0:T(4,128)(2,1)} %param.18) | copy-start | bytes 27652
  1.7 129.0 %copy-start.3 = (s32[1,4]{1,0:T(1,128)S(1)}, s32[1,4]{1,0:T(1,128)}, u32[]{:S(2)}) copy-start(s32[1,4]{1,0:T(1,128)} %param.16) | copy-start | bytes 52
  1.7 129.2 %copy-start.2 = (bf16[2,4,64,576]{3,2,1,0:T(8,128)(2,1)S(1)}, bf16[2,4,64,576]{3,2,1,0:T(8,128)(2,1)}, u32[]{:S(2)}) copy-start(bf16[2,4,64,576]{3,2,1,0:T(8,128)(2,1)} %q_ref.1) | copy-start | bytes 1769476
  130.9 3.7 %copy-start = (bf16[4,4,4,2,3,96,128]{6,5,4,3,2,1,0:T(8,128)(2,1)S(1)}, bf16[4,4,4,2,3,96,128]{6,5,4,3,2,1,0:T(8,128)(2,1)}, u32[]{:S(2)}) copy-start(bf16[4,4,4,2,3,96,128]{6,5,4,3,2,1,0:T(8,128)(2,1)} %exchange.1) | copy-start | bytes 28311556
  134.6 13.2 %copy-start.4 = (f32[3584,16]{0,1:T(8,128)S(1)}, f32[3584,16]{0,1:T(8,128)}, u32[]{:S(2)}) copy-start(f32[3584,16]{0,1:T(8,128)} %param.23) | copy-start | bytes 688132
  147.0 0.8 copy-start.1
  147.8 1.4 copy-start.5
  147.8 2.2 copy-start.6
  147.8 2.8 %copy-start.8 = (s32[2,4,8]{2,1,0:T(4,128)S(1)}, s32[2,4,8]{2,1,0:T(4,128)}, u32[]{:S(2)}) copy-start(s32[2,4,8]{2,1,0:T(4,128)} %param.27) | copy-start | bytes 772

commit v3 on v2

--- a/solution.py
+++ b/solution.py
@@ -26,7 +26,7 @@
 
 
 def exchange_kernel(
-    source, pool, out,
+    table, pool, out,
     pool_v, slots, held1, held2, stage,
     psem, lsem, csem, send1, recv1, send2, recv2, send3, recv3,
 ):
@@ -63,8 +63,11 @@
     for peer in peers:
         pl.semaphore_signal(barrier, inc=1, device_id=peer, device_id_type=MESH)
 
-    lane = lax.broadcasted_iota(jnp.int32, (128, 128), 1)
-    onehot = jnp.where(source[...] == lane, 1.0, 0.0).astype(BF16)
+    pages = table[...]
+    wanted = jnp.where(pages // 128 == dp * 8 + ep, pages % 128, 0)
+    wanted = jnp.sum(wanted, axis=0, keepdims=True)
+    page = lax.broadcasted_iota(jnp.int32, (128, 128), 0)
+    onehot = jnp.transpose(jnp.where(wanted == page, 1.0, 0.0)).astype(BF16)
 
     def put(cls, row, pieces):
         for j in range(0, 16, 4):
@@ -113,26 +116,31 @@
     def landed(ref, sem):
         pltpu.make_async_copy(ref, ref, sem).wait()
 
-    for load in loads:
-        load.wait()
-    for cls, order in enumerate(ORDERS):
-        a1, a2, a3 = order
-        latent_rows(cls, cls, 0, 4, 0)
-        if cls < 2:
-            latent_rows(cls, 3, 2 * cls, 2, 64)
-        else:
-            rope_rows(cls, 64)
-        if cls == 0:
-            pl.semaphore_wait(barrier, len(peers))
-        for d in (1, 2, 3):
-            src = spec_of(order, ((pos[a1] + d) % 4, whole, whole))
-            dst = spec_of(order, (pos[a1], whole, whole))
-            remote(
-                slots.at[(cls,) + src], held1.at[(cls,) + dst],
-                send1.at[cls, d], recv1.at[cls, d], along(a1, d, core),
-            )
-        own = spec_of(order, (pos[a1], whole, whole))
-        pltpu.make_async_copy(slots.at[(cls,) + own], held1.at[(cls,) + own], lsem.at[cls]).start()
+    for part in range(3):
+        rows = pl.ds(part * 32, 32)
+        for load in loads[2 * part : 2 * part + 2]:
+            load.wait()
+        for cls, order in enumerate(ORDERS):
+            a1, a2, a3 = order
+            if part < 2:
+                latent_rows(cls, cls, 2 * part, 2, 32 * part)
+            elif cls < 2:
+                latent_rows(cls, 3, 2 * cls, 2, 64)
+            else:
+                rope_rows(cls, 64)
+            if part == 0 and cls == 0:
+                pl.semaphore_wait(barrier, len(peers))
+            for d in (1, 2, 3):
+                src = spec_of(order, ((pos[a1] + d) % 4, whole, whole))
+                dst = spec_of(order, (pos[a1], whole, whole))
+                remote(
+                    slots.at[(cls,) + src + (pl.ds(0, 2), rows)],
+                    held1.at[(cls,) + dst + (pl.ds(0, 2), rows)],
+                    send1.at[cls, d, part], recv1.at[cls, d, part], along(a1, d, core),
+                )
+            if part == 2:
+                own = (cls,) + spec_of(order, (pos[a1], whole, whole))
+                pltpu.make_async_copy(slots.at[own], held1.at[own], lsem.at[cls]).start()
 
     def second(cls, buf, e):
         a1, a2, a3 = order = ORDERS[cls]
@@ -165,7 +173,9 @@
         for cls, order in enumerate(ORDERS):
             src1 = (pos[order[0]] + 4 - e) % 4
             at = spec_of(order, (src1, whole, whole))
-            landed(held1.at[(cls,) + at], recv1.at[cls, e])
+            for part in range(3):
+                rows = pl.ds(part * 32, 32)
+                landed(held1.at[(cls,) + at + (pl.ds(0, 2), rows)], recv1.at[cls, e, part])
             second(cls, held1, e)
     for cls, order in enumerate(ORDERS):
         own = spec_of(order, (pos[order[0]], whole, whole))
@@ -190,7 +200,7 @@
         landed(src, ssem)
 
 
-def exchange(source, pool):
+def exchange(table, pool):
     vmem = pl.BlockSpec(memory_space=pltpu.VMEM)
     hbm = pl.BlockSpec(memory_space=pl.ANY)
     dma = pltpu.SemaphoreType.DMA
@@ -206,14 +216,14 @@
             pltpu.VMEM(held, BF16),
             pltpu.VMEM(held, BF16),
             pltpu.VMEM((128, 16, 128), F32),
-            dma((4,)), dma((3,)), dma((3, 4)), dma((3, 4)), dma((3, 4)), dma((3, 4, 4)),
+            dma((4,)), dma((3,)), dma((3, 4)), dma((3, 4, 3)), dma((3, 4, 3)), dma((3, 4, 4)),
             dma((3, 4, 4)), dma((3, 4, 4, 2)), dma((3, 4, 4, 2)),
         ],
         compiler_params=pltpu.CompilerParams(
             collective_id=2, has_side_effects=True, vmem_limit_bytes=56 * 2**20
         ),
         name="exchange",
-    )(source, pool)
+    )(table, pool)
 
 
 def attend_kernel(
@@ -321,15 +331,15 @@
             pltpu.VMEM((32 // TILE, 128, TILE * PAGE), F32),
             pltpu.SemaphoreType.DMA((3,)),
         ],
-        compiler_params=pltpu.CompilerParams(vmem_limit_bytes=40 * 2**20),
+        compiler_params=pltpu.CompilerParams(vmem_limit_bytes=60 * 2**20),
         name="attend",
     )(owner, starts, counts, queries, own, slots)
 
 
 def layer_kernel(
-    attended, resid, member, gain, router, w_uv, w_out, w_gate, w_up, w_down,
+    attended, residual, routes, gain, router, w_uv, w_out, w_gate, w_up, w_down,
     out_ref,
-    heads_in, masked, part_out, part_in, res_all, mem_all, stat_out, stat_in, hidden,
+    resid, member, heads_in, masked, part_out, part_in, res_all, mem_all, stat_out, stat_in, hidden,
     gath, v_uv, v_out, v_gate, v_up, v_down, inner,
     mix, sib_out, sib_in, t1, ul1, ur1, t2, ul2, ur2, last, fin_out, fin_in,
     wsem, lsem, head_s, head_r, part_s, part_r, pair_s, pair_r,
@@ -374,6 +384,16 @@
     barrier = pltpu.get_barrier_semaphore()
     for peer in ep_peers + ring_peers:
         pl.semaphore_signal(barrier, inc=1, device_id=peer, device_id_type=MESH)
+    for h in range(2):
+        cols = slice(h * HALF, (h + 1) * HALF)
+        both = [residual[s, :, cols].astype(F32) for s in range(2)]
+        resid[h] = jnp.concatenate(both, axis=0)
+    route = jnp.concatenate([routes[0], routes[1]], axis=0)
+    lanes = lax.broadcasted_iota(jnp.int32, (8, 128), 1)
+    named = jnp.zeros((8, 128), F32)
+    for k in range(8):
+        named = jnp.where(route[:, k : k + 1] == lanes, 1.0, named)
+    member[...] = named
     pl.semaphore_wait(barrier, len(ep_peers) + len(ring_peers))
 
     for o in range(1, 8):
@@ -425,8 +445,9 @@
     hidden[...] = hid
 
     half_cols = pl.ds(pl.multiple_of(core * HALF, 128), HALF)
-    scaled = hid * gain[:, half_cols]
-    stat_out[0] = lax.dot_general(
+    scaled = hid * gain[half_cols].reshape(1, HALF)
+    stat_out[0] = jnp.zeros((16, 128), F32)
+    stat_out[0, :, 0:16] = lax.dot_general(
         scaled, router[:, half_cols], (((1,), (1,)), ((), ())),
         preferred_element_type=F32, precision=lax.Precision.HIGHEST,
     )
@@ -634,24 +655,29 @@
         fin_out[0, :, cls * PART : cls * PART + n] = total[0:8]
         fin_out[1, :, cls * PART : cls * PART + n] = total[8:16]
     remote(fin_out.at[other], fin_in, pair_s.at[3], pair_r.at[3], sibling)
-    out_ref[:, half_cols] = fin_out[core].astype(BF16)
+    for s in range(2):
+        out_ref[s, :, half_cols] = fin_out[core, s * 4 : s * 4 + 4].astype(BF16)
     landed(fin_in, pair_r.at[3])
-    out_ref[:, pl.ds(pl.multiple_of(other * HALF, 128), HALF)] = fin_in[...].astype(BF16)
+    for s in range(2):
+        cols = pl.ds(pl.multiple_of(other * HALF, 128), HALF)
+        out_ref[s, :, cols] = fin_in[s * 4 : s * 4 + 4].astype(BF16)
     for src, ssem in sent:
         pltpu.make_async_copy(src, src, ssem).wait()
 
 
-def layer(attended, resid, member, gain, router, w_uv, w_out, w_gate, w_up, w_down):
+def layer(attended, residual, routes, gain, router, w_uv, w_out, w_gate, w_up, w_down):
     vmem = pl.BlockSpec(memory_space=pltpu.VMEM)
     hbm = pl.BlockSpec(memory_space=pl.ANY)
     dma = pltpu.SemaphoreType.DMA
     grid = (3, 4, 4, 4, 16, PART)
     return pl.pallas_call(
         layer_kernel,
-        out_shape=jax.ShapeDtypeStruct((8, 2 * HALF), BF16),
+        out_shape=jax.ShapeDtypeStruct((2, 4, 2 * HALF), BF16),
         in_specs=[vmem] * 5 + [hbm] * 5,
         out_specs=vmem,
         scratch_shapes=[
+            pltpu.VMEM((2, 8, HALF), F32),
+            pltpu.VMEM((8, 128), F32),
             pltpu.VMEM((8, 64, LATENT), BF16),
             pltpu.VMEM((512, 1024), BF16),
             pltpu.VMEM((2, 4, 16, HALF), BF16),
@@ -688,7 +714,7 @@
             collective_id=1, has_side_effects=True, vmem_limit_bytes=56 * 2**20
         ),
         name="layer",
-    )(attended, resid, member, gain, router, w_uv, w_out, w_gate, w_up, w_down)
+    )(attended, residual, routes, gain, router, w_uv, w_out, w_gate, w_up, w_down)
 
 
 def shards(
@@ -711,9 +737,7 @@
     my_index = lax.axis_index("dp") * ep_size + lax.axis_index("ep")
     pool_dev = cache_pool.shape[0]
     owner_all = page_table // pool_dev
-    local_all = page_table % pool_dev
-    source = jnp.sum(jnp.where(owner_all == my_index, local_all, 0), axis=1)
-    incoming = exchange(source.reshape(-1, 1), jnp.transpose(cache_pool, (1, 2, 0)))
+    incoming = exchange(page_table.T, jnp.transpose(cache_pool, (1, 2, 0)))
     incoming = incoming.reshape(-1, 3, 96, 128)
     owner = lax.dynamic_index_in_dim(owner_all, my_index, 0, keepdims=False)
     counts = page_counts[0]
@@ -721,16 +745,9 @@
     own = jnp.pad(jnp.transpose(new_latent, (1, 0, 2)), ((0, 0), (0, 14), (0, 0)))
     attended = attend(owner, starts, counts, queries, own, incoming)
 
-    d_model = residual.shape[2]
-    resid = residual.reshape(8, 2, d_model // 2).transpose(1, 0, 2).astype(F32)
-    experts = w_router.shape[1]
-    member = jnp.any(routes.reshape(8, -1)[:, :, None] == jnp.arange(128)[None, None, :], axis=1)
-    router = jnp.pad(w_router.T, ((0, 128 - experts), (0, 0)))
-    out = layer(
-        attended, resid, member.astype(F32), norm_gain.reshape(1, -1), router,
-        w_uv, w_out, w_gate, w_up, w_down,
+    return layer(
+        attended, residual, routes, norm_gain, w_router.T, w_uv, w_out, w_gate, w_up, w_down
     )
-    return out.reshape(residual.shape)
 
 
 def solution(mesh):

time: 249 us -> 233 us (0.936)
  Pallas kernels: 237 us -> 224 us
  local copies, waits for them, and re-layouts: 9.66 us -> 2.8 us
  other arithmetic: 1.68 us -> 5.06 us
    pallas_call x1, Pallas kernels: 129 us -> 118 us  [exchange(): pl.pallas_call(exchange_kernel, out_shape=jax.ShapeDtypeStruct((4, 4, 4,...]
    reshape x3 -> x0, local copies, waits for them, and re-layouts: 2.81 us -> none  [the longest x1 1.46 us: shards(): return out.reshape(residual.shape)]
    pallas_call x1, Pallas kernels: 95.5 us -> 92.8 us  [layer(): pl.pallas_call(layer_kernel, out_shape=jax.ShapeDtypeStruct((2, 4, 2 * HA...]
where the time goes in v3:
time: 233 us; the launch traced here: 232 us
  Pallas kernels  224 us (96%)
  other arithmetic  5.06 us (2%)
  local copies, waits for them, and re-layouts  2.8 us (1%)
    pallas_call x1, Pallas kernels, exchange(): pl.pallas_call(exchange_kernel, out_shape=jax.ShapeDtypeStruct((4, 4, 4,...  118 us
    pallas_call x1, Pallas kernels, layer(): pl.pallas_call(layer_kernel, out_shape=jax.ShapeDtypeStruct((2, 4, 2 * HA...  92.8 us
    pallas_call x1, Pallas kernels, attend(): pl.pallas_call(attend_kernel, out_shape=jax.ShapeDtypeStruct((8, 64, LATE...  12.8 us

profile of v3, /device:TPU:1, one launch (start us, length us, event | category | flops | bytes accessed | tf_op | source)
XLA Modules:
  0.0 231.9 jit_solution(14187341641299889577)
XLA Ops:
  0.0 0.8 reduce-window.9
  0.8 1.2 bitcast_subtract_fusion.starts
  2.1 0.8 broadcast_compare_fusion
  2.8 0.7 copy.18
  3.5 0.8 negate_select_fusion.2
  4.3 1.5 fusion.1.owner
  5.8 0.6 pad.4.own_ref
  6.4 118.5 %exchange.1 = bf16[4,4,4,2,3,96,128]{6,5,4,3,2,1,0:T(8,128)(2,1)} custom-call(s32[64,128]{1,0:T(8,128)} %bitcast.14, bf16[64,576,128]{2,1,0:T(8,128)(2,1)} %bitcast.13), custom_call_target="tpu_custom_call" | custom-call | tf_op jit(solution)/shard_map/exchange/pallas_call | solution.py:208
  124.9 12.8 %attend.1.attended = bf16[8,64,512]{2,1,0:T(8,128)(2,1)} custom-call(s32[64]{0:T(128)} %fusion.1.owner, s32[4]{0:T(128)} %bitcast_subtract_fusion.starts, s32[4]{0:T(128)} %bitcast.18, bf16[2,4,64,576]{3,2,1,0:T(8,128)(2,1)} %q_ref.1, bf16[4,16,576]{2,1,0:T(8,128)(2,1)} %pad.4.own_ref, bf16[128,3,96,128]{3,2,1,0:T(8,128)(2,1)} %bitcast.12), custom_call_target="tpu_custom_call" | custom-call | tf_op jit(solution)/shard_map/attend/pallas_call | solution.py:322
  137.7 92.8 %layer.1 = bf16[2,4,3584]{2,1,0:T(4,128)(2,1)} custom-call(bf16[8,64,512]{2,1,0:T(8,128)(2,1)} %attend.1.attended, bf16[2,4,3584]{2,1,0:T(4,128)(2,1)} %residual.1, s32[2,4,8]{2,1,0:T(4,128)} %routes.1, f32[3584]{0:T(1024)} %gain.1, f32[16,3584]{1,0:T(8,128)} %bitcast.15, bf16[8,512,128]{2,1,0:T(8,128)(2,1)} %w_uv.1, bf16[1024,3584]{1,0:T(8,128)(2,1)} %w_out.1, ...), custom_call_target="tpu_custom_call" | custom-call | tf_op jit(solution)/shard_map/layer/pallas_call | solution.py:673
  230.5 1.5 copy.20

commit v4 on v3

--- a/solution.py
+++ b/solution.py
@@ -14,7 +14,7 @@
 LATENT = 512
 ROPE = 64
 PAGE = 64
-TILE = 8
+TILE = 16
 score_scale = 192.0 ** (-0.5)
 route_scale = 2.5
 norm_eps = 1e-06
@@ -227,13 +227,14 @@
 
 
 def attend_kernel(
-    owner, starts, counts, q_ref, own_ref, slots, out_ref, keys, last, ropes, scores, sem
+    table, counts, q_ref, new_ref, slots, out_ref, own_ref, keys, last, ropes, scores, sem
 ):
     pages = 64
+    me = lax.axis_index("dp") * 8 + lax.axis_index("ep")
 
     def fetch(j, _):
         at = pl.multiple_of(j * PAGE, PAGE)
-        slot = slots.at[owner[j]]
+        slot = slots.at[table[j, me] // 128]
         pltpu.make_async_copy(
             slot.at[:, pl.ds(0, 64), :], keys.at[:, pl.ds(at, PAGE), :], sem.at[0]
         ).start()
@@ -253,6 +254,11 @@
         return 0
 
     lax.fori_loop(0, TILE, clear, 0)
+    own_ref[...] = jnp.zeros_like(own_ref)
+    for step in range(2):
+        fresh = new_ref[step].astype(F32)
+        for r in range(4):
+            own_ref[r, step : step + 1, :] = fresh[r : r + 1]
     for k, ref in enumerate(
         (keys.at[:, pl.ds(0, pages * PAGE), :], last.at[pl.ds(0, pages)], ropes.at[pl.ds(0, pages)])
     ):
@@ -268,15 +274,14 @@
         parts.append(last[pl.ds(page, TILE)].reshape(width, 128))
         return jnp.concatenate(parts, axis=1)
 
-    def request(r, _):
+    def request(r, start):
         q = jnp.concatenate([q_ref[0, r], q_ref[1, r]], axis=0)
-        own = own_ref[r]
+        own = own_ref[r].astype(BF16)
         s_own = lax.dot_general(q, own, (((1,), (1,)), ((), ())), preferred_element_type=F32)
         s_own = jnp.where(token <= step_of, s_own * score_scale, -jnp.inf)
         q_rope = q[:, LATENT:]
         q_wide = jnp.concatenate([q[:, :LATENT], q_rope, q_rope], axis=1)
-        start = starts[r]
-        length = counts[r] * PAGE
+        length = counts[0, r] * PAGE
         tiles = (length + width - 1) // width
 
         def score(t, top):
@@ -311,20 +316,21 @@
         for g in range(8):
             block = jnp.concatenate([res[0, g], res[1, g]], axis=0)
             out_ref[g, pl.ds(at, 16), :] = block.astype(BF16)
-        return 0
+        return start + counts[0, r]
 
     lax.fori_loop(0, 4, request, 0)
 
 
-def attend(owner, starts, counts, queries, own, slots):
+def attend(table, counts, queries, new_latent, slots):
     smem = pl.BlockSpec(memory_space=pltpu.SMEM)
     vmem = pl.BlockSpec(memory_space=pltpu.VMEM)
     return pl.pallas_call(
         attend_kernel,
         out_shape=jax.ShapeDtypeStruct((8, 64, LATENT), BF16),
-        in_specs=[smem, smem, smem, vmem, vmem, pl.BlockSpec(memory_space=pl.ANY)],
+        in_specs=[smem, smem, vmem, vmem, pl.BlockSpec(memory_space=pl.ANY)],
         out_specs=vmem,
         scratch_shapes=[
+            pltpu.VMEM((4, 16, LATENT + ROPE), F32),
             pltpu.VMEM((3, (64 + TILE) * PAGE, 128), BF16),
             pltpu.VMEM((64 + TILE, 2, 32, 128), BF16),
             pltpu.VMEM((64 + TILE, 32, 128), BF16),
@@ -333,17 +339,17 @@
         ],
         compiler_params=pltpu.CompilerParams(vmem_limit_bytes=60 * 2**20),
         name="attend",
-    )(owner, starts, counts, queries, own, slots)
+    )(table, counts, queries, new_latent, slots)
 
 
 def layer_kernel(
     attended, residual, routes, gain, router, w_uv, w_out, w_gate, w_up, w_down,
     out_ref,
     resid, member, heads_in, masked, part_out, part_in, res_all, mem_all, stat_out, stat_in, hidden,
-    gath, v_uv, v_out, v_gate, v_up, v_down, inner,
+    gath, v_uv, v_out, v_gate, v_up, v_down, acc, inner,
     mix, sib_out, sib_in, t1, ul1, ur1, t2, ul2, ur2, last, fin_out, fin_in,
     wsem, lsem, head_s, head_r, part_s, part_r, pair_s, pair_r,
-    ag_s, ag_r, sib_s, sib_r, red_s, red_r, sum_s, sum_r,
+    ag1_s, ag1_r, ag2_s, ag2_r, ag3_s, ag3_r, sib_s, sib_r, red_s, red_r, sum_s, sum_r,
 ):
     dp = lax.axis_index("dp")
     ep = lax.axis_index("ep")
@@ -394,6 +400,13 @@
     for k in range(8):
         named = jnp.where(route[:, k : k + 1] == lanes, 1.0, named)
     member[...] = named
+
+    def clear(i, _):
+        acc[0, i] = jnp.zeros((4, 4, 16, 256), F32)
+        acc[1, i] = jnp.zeros((4, 4, 16, 256), F32)
+        return 0
+
+    lax.fori_loop(0, 4, clear, 0)
     pl.semaphore_wait(barrier, len(ep_peers) + len(ring_peers))
 
     for o in range(1, 8):
@@ -479,118 +492,135 @@
             spec[axis] = value
         return spec
 
+    def line(cls, e, f):
+        a1, a2, a3 = ORDERS[cls]
+        where = spec_of((a1, a2, a3), ((pos[a1] + 4 - e) % 4, (pos[a2] + 4 - f) % 4, pos[a3]))
+        return g_at(cls, where)
+
+    def quarter(cls, f, shift, half=whole):
+        a1, a2, a3 = ORDERS[cls]
+        at = (half, (pos[a2] + 4 - f) % 4, (pos[a3] + shift) % 4)
+        return g_at(cls, spec_of((a1, a2, a3), at))
+
+    def plane_at(cls, shift):
+        a1, a2, a3 = ORDERS[cls]
+        return tuple(spec_of((a1, a2, a3), (whole, whole, (pos[a3] + shift) % 4)))
+
+    def to_pair(cls, k, shift):
+        plane = gath.at[(core, cls) + plane_at(cls, shift)]
+        remote(plane, plane, sib_s.at[cls, k], sib_r.at[cls, k], sibling)
+
+    def second(cls, e):
+        b = line(cls, e, 0)
+        for d in (1, 3, 2):
+            remote(b, b, ag2_s.at[cls, d, e], ag2_r.at[cls, d, e], along(ORDERS[cls][1], d))
+
+    def third(cls, f):
+        b = quarter(cls, f, 0)
+        for k, d in ((0, 1), (1, 3)):
+            remote(b, b, ag3_s.at[cls, f, k], ag3_r.at[cls, f, k], along(ORDERS[cls][2], d))
+
     for cls, order in enumerate(ORDERS):
         own = g_at(cls, pos)
-        for d in (1, 2, 3):
-            remote(own, own, ag_s.at[cls, 0, d], ag_r.at[cls, 0, d], along(order[0], d))
-    for cls, order in enumerate(ORDERS):
-        a1, a2, a3 = order
-        for d in (1, 2, 3):
-            src = list(pos)
-            src[a1] = (pos[a1] + 4 - d) % 4
-            landed(g_at(cls, src), ag_r.at[cls, 0, d])
-    for phase in (1, 2):
-
-        def block(cls, shift, half):
-            a1, a2, a3 = ORDERS[cls]
-            if phase == 1:
-                return g_at(cls, spec_of((a1, a2, a3), (half, (pos[a2] + shift) % 4, pos[a3])))
-            return g_at(cls, spec_of((a1, a2, a3), (half, whole, (pos[a3] + shift) % 4)))
-
+        for d in (1, 3, 2):
+            remote(own, own, ag1_s.at[cls, d], ag1_r.at[cls, d], along(order[0], d))
+    for cls in range(3):
+        second(cls, 0)
+    for e in (1, 3, 2):
+        for cls in range(3):
+            landed(line(cls, e, 0), ag1_r.at[cls, e])
+            second(cls, e)
+    for cls in range(3):
+        third(cls, 0)
+    for f in (1, 3, 2):
+        for cls in range(3):
+            for e in range(4):
+                landed(line(cls, e, f), ag2_r.at[cls, f, e])
+            third(cls, f)
+    for cls in range(3):
+        to_pair(cls, 0, 0)
+    for f in (0, 1, 3, 2):
         for cls, order in enumerate(ORDERS):
-            if phase == 2:
-                plane = g_at(cls, spec_of(order, (whole, whole, pos[order[2]])))
-                remote(plane, plane, sib_s.at[cls, 0], sib_r.at[cls, 0], sibling)
-            axis = order[phase]
-            for half, delta, k in ((0, 1, 0), (1, 3, 1), (1, 1, 2), (0, 3, 3)):
-                b = block(cls, 0, halves[half])
-                remote(b, b, ag_s.at[cls, phase, k], ag_r.at[cls, phase, k], along(axis, delta))
-        for cls, order in enumerate(ORDERS):
-            axis = order[phase]
-            b = block(cls, 3, halves[0])
-            landed(b, ag_r.at[cls, phase, 0])
-            remote(b, b, ag_s.at[cls, phase, 4], ag_r.at[cls, phase, 4], along(axis, 1))
-            b = block(cls, 1, halves[1])
-            landed(b, ag_r.at[cls, phase, 1])
-            remote(b, b, ag_s.at[cls, phase, 5], ag_r.at[cls, phase, 5], along(axis, 3))
-        for cls, order in enumerate(ORDERS):
-            landed(block(cls, 3, halves[1]), ag_r.at[cls, phase, 2])
-            landed(block(cls, 1, halves[0]), ag_r.at[cls, phase, 3])
-            if phase == 2:
-                for k, shift in ((1, 3), (2, 1)):
-                    plane = block(cls, shift, whole)
-                    remote(plane, plane, sib_s.at[cls, k], sib_r.at[cls, k], sibling)
-        for cls, order in enumerate(ORDERS):
-            landed(block(cls, 2, halves[0]), ag_r.at[cls, phase, 4])
-            landed(block(cls, 2, halves[1]), ag_r.at[cls, phase, 5])
-            if phase == 2:
-                plane = block(cls, 2, whole)
-                remote(plane, plane, sib_s.at[cls, 3], sib_r.at[cls, 3], sibling)
-    for cls, order in enumerate(ORDERS):
-        a1, a2, a3 = order
-        for k, shift in ((0, 0), (1, 3), (2, 1), (3, 2)):
-            spec = spec_of(order, (whole, whole, (pos[a3] + shift) % 4))
-            landed(gath.at[other, cls, spec[0], spec[1], spec[2]], sib_r.at[cls, k])
+            landed(quarter(cls, f, 3), ag3_r.at[cls, f, 0])
+            b = quarter(cls, f, 3, halves[0])
+            remote(b, b, ag3_s.at[cls, f, 2], ag3_r.at[cls, f, 2], along(order[2], 1))
+            landed(quarter(cls, f, 1), ag3_r.at[cls, f, 1])
+            b = quarter(cls, f, 1, halves[1])
+            remote(b, b, ag3_s.at[cls, f, 3], ag3_r.at[cls, f, 3], along(order[2], 3))
+    for k, shift in ((1, 3), (2, 1)):
+        for cls in range(3):
+            to_pair(cls, k, shift)
 
     for copy in copies[2:]:
         copy.wait()
 
-    def expert_in(i, _):
-        gate = jnp.zeros((256, 256), F32)
-        up = jnp.zeros((256, 256), F32)
-        for h in range(2):
-            for cls in range(3):
-                n = WIDTHS[cls]
-                k0 = h * HALF + cls * PART
-                rows_in = gath[h, cls, i].reshape(256, PART)[:, :n]
-                gate = gate + jnp.dot(rows_in, v_gate[0, k0 : k0 + n, :], preferred_element_type=F32)
-                up = up + jnp.dot(rows_in, v_up[0, k0 : k0 + n, :], preferred_element_type=F32)
-        act = gate / (1.0 + jnp.exp(-gate)) * up
-        at = pl.multiple_of(i * 256, 256)
-        inner[pl.ds(at, 256), :] = act.astype(BF16)
+    def expert_in(h, cls, shift):
+        at = plane_at(cls, shift)
+        n = WIDTHS[cls]
+        x = gath[(h, cls) + at].reshape(256, PART)[:, :n]
+        rows = pl.ds(pl.multiple_of(h * HALF + cls * PART, 128), n)
+        for k, w in enumerate((v_gate, v_up)):
+            y = jnp.dot(x, w[0, rows, :], preferred_element_type=F32).reshape(4, 4, 16, 256)
+            acc[(k,) + at] = acc[(k,) + at] + y
+
+    def from_pair(cls, k, shift):
+        landed(gath.at[(other, cls) + plane_at(cls, shift)], sib_r.at[cls, k])
+
+    for cls in range(3):
+        expert_in(core, cls, 0)
+    for cls in range(3):
+        from_pair(cls, 0, 0)
+        expert_in(other, cls, 0)
+    for k, shift in ((1, 3), (2, 1)):
+        for cls in range(3):
+            expert_in(core, cls, shift)
+    for cls in range(3):
+        for f in range(4):
+            landed(quarter(cls, f, 2, halves[0]), ag3_r.at[cls, f, 2])
+            landed(quarter(cls, f, 2, halves[1]), ag3_r.at[cls, f, 3])
+        to_pair(cls, 3, 2)
+    for k, shift in ((1, 3), (2, 1)):
+        for cls in range(3):
+            from_pair(cls, k, shift)
+            expert_in(other, cls, shift)
+    for cls in range(3):
+        expert_in(core, cls, 2)
+    for cls in range(3):
+        from_pair(cls, 3, 2)
+        expert_in(other, cls, 2)
+
+    lane = lax.broadcasted_iota(jnp.int32, (256, 128), 1)
+
+    def activate(i, _):
+        both = gath[0, 2, i, :, :, :, 512:640].astype(F32) + gath[1, 2, i, :, :, :, 512:640].astype(F32)
+        weight = jnp.sum(jnp.where(lane == dp, both.reshape(256, 128), 0.0), axis=1, keepdims=True)
+        gate = acc[0, i].reshape(256, 256)
+        act = gate / (1.0 + jnp.exp(-gate)) * acc[1, i].reshape(256, 256) * weight
+        inner[i] = act.astype(BF16).reshape(4, 4, 16, 256)
         return 0
 
-    lax.fori_loop(0, 4, expert_in, 0)
-    lane = lax.broadcasted_iota(jnp.int32, (256, 128), 1)
-
-    def expert_out(i, half, dest):
-        at = pl.multiple_of(i * 256, 256)
-        weights = gath[0, 2, i, :, :, :, 512:640].astype(F32) + gath[1, 2, i, :, :, :, 512:640].astype(F32)
-        weight = jnp.sum(
-            jnp.where(lane == dp, weights.reshape(256, 128), 0.0), axis=1, keepdims=True
-        )
-        act = inner[pl.ds(at, 256), :]
-        for cls in range(3):
-            n = WIDTHS[cls]
-            cols = pl.ds(pl.multiple_of(half * HALF + cls * PART, 128), n)
-            y = jnp.dot(act, v_down[0, :, cols], preferred_element_type=F32) * weight
-            dest[cls, i, :, :, :, 0:n] = y.astype(BF16).reshape(4, 4, 16, n)
-
-    def to_sibling(i, _):
-        expert_out(i, other, sib_out)
-        return 0
-
-    lax.fori_loop(0, 4, to_sibling, 0)
-    remote(sib_out, sib_in, red_s.at[0], red_r.at[0], sibling)
-
-    def to_self(i, _):
-        expert_out(i, core, mix)
-        return 0
-
-    lax.fori_loop(0, 4, to_self, 0)
-    landed(sib_in, red_r.at[0])
-
-    def add_sibling(i, _):
-        for cls in range(3):
-            n = WIDTHS[cls]
-            total = mix[cls, i, :, :, :, 0:n].astype(F32) + sib_in[cls, i, :, :, :, 0:n].astype(F32)
-            mix[cls, i, :, :, :, 0:n] = total.astype(BF16)
-        return 0
-
-    lax.fori_loop(0, 4, add_sibling, 0)
-
-    def cut(ref, n):
-        return ref.at[..., pl.ds(0, n)]
+    lax.fori_loop(0, 4, activate, 0)
+
+    def expert_out(half, cls, at):
+        cols = pl.ds(pl.multiple_of(half * HALF + cls * PART, 128), WIDTHS[cls])
+        act = inner[at].reshape(256, 256)
+        y = jnp.dot(act, v_down[0, :, cols], preferred_element_type=F32)
+        return y.reshape(4, 4, 16, WIDTHS[cls])
+
+    def for_pair(shift):
+        for cls in range(3):
+            at = plane_at(cls, shift)
+            b = (cls,) + at + (slice(None), pl.ds(0, WIDTHS[cls]))
+            sib_out[b] = expert_out(other, cls, at).astype(BF16)
+            remote(sib_out.at[b], sib_in.at[b], red_s.at[cls, shift], red_r.at[cls, shift], sibling)
+
+    def for_self(shift):
+        for cls in range(3):
+            at = plane_at(cls, shift)
+            b = (cls,) + at + (slice(None), pl.ds(0, WIDTHS[cls]))
+            y = expert_out(core, cls, at)
+            landed(sib_in.at[b], red_r.at[cls, shift])
+            mix[b] = (y + sib_in[b].astype(F32)).astype(BF16)
 
     for phase in (2, 1):
         bt, bl, br = (t1, ul1, ur1) if phase == 2 else (t2, ul2, ur2)
@@ -618,10 +648,21 @@
                 sum_s.at[cls, red, k], sum_r.at[cls, red, k], along(ORDERS[cls][phase], delta),
             )
 
+        if phase == 2:
+            for_pair(2)
+            for_pair(1)
+            for_self(2)
         for cls in range(3):
             send(cls, 2, 0, bt, 0, 1)
             send(cls, 2, 1, bt, 1, 3)
+        if phase == 2:
+            for_pair(3)
+            for_self(1)
+        for cls in range(3):
             send(cls, 1, 1, bl, 2, 1)
+        if phase == 2:
+            for_self(3)
+        for cls in range(3):
             send(cls, 3, 0, br, 3, 3)
         for cls in range(3):
             for half, shift, buf, k, delta in ((0, 1, bl, 0, 1), (1, 3, br, 1, 3)):
@@ -629,6 +670,9 @@
                 landed(bt.at[tmp], sum_r.at[cls, red, k])
                 mix[at] = (mix[at].astype(F32) + bt[tmp].astype(F32)).astype(BF16)
                 send(cls, shift, half, buf, k + 4, delta)
+        if phase == 2:
+            for_pair(0)
+            for_self(0)
         for cls in range(3):
             for half, ks in ((0, (4, 3)), (1, (2, 5))):
                 at, tmp = block(cls, 0, halves[half]), temp(cls, halves[half])
@@ -693,7 +737,8 @@
             pltpu.VMEM(w_gate.shape, BF16),
             pltpu.VMEM(w_up.shape, BF16),
             pltpu.VMEM(w_down.shape, BF16),
-            pltpu.VMEM((1024, 256), BF16),
+            pltpu.VMEM((2, 4, 4, 4, 16, 256), F32),
+            pltpu.VMEM((4, 4, 4, 16, 256), BF16),
             pltpu.VMEM(grid, BF16),
             pltpu.VMEM(grid, BF16),
             pltpu.VMEM(grid, BF16),
@@ -707,7 +752,8 @@
             pltpu.VMEM((2, 8, HALF), F32),
             pltpu.VMEM((8, HALF), F32),
             dma((5,)), dma, dma((8,)), dma((8,)), dma((8,)), dma((8,)), dma((4,)), dma((4,)),
-            dma((3, 3, 6)), dma((3, 3, 6)), dma((3, 4)), dma((3, 4)), dma((1,)), dma((1,)),
+            dma((3, 4)), dma((3, 4)), dma((3, 4, 4)), dma((3, 4, 4)), dma((3, 4, 4)), dma((3, 4, 4)),
+            dma((3, 4)), dma((3, 4)), dma((3, 4)), dma((3, 4)),
             dma((3, 3, 6)), dma((3, 3, 6)),
         ],
         compiler_params=pltpu.CompilerParams(
@@ -733,18 +779,9 @@
     w_down,
     routes,
 ):
-    ep_size = lax.axis_size("ep")
-    my_index = lax.axis_index("dp") * ep_size + lax.axis_index("ep")
-    pool_dev = cache_pool.shape[0]
-    owner_all = page_table // pool_dev
-    incoming = exchange(page_table.T, jnp.transpose(cache_pool, (1, 2, 0)))
-    incoming = incoming.reshape(-1, 3, 96, 128)
-    owner = lax.dynamic_index_in_dim(owner_all, my_index, 0, keepdims=False)
-    counts = page_counts[0]
-    starts = jnp.cumsum(counts) - counts
-    own = jnp.pad(jnp.transpose(new_latent, (1, 0, 2)), ((0, 0), (0, 14), (0, 0)))
-    attended = attend(owner, starts, counts, queries, own, incoming)
-
+    table = page_table.T
+    incoming = exchange(table, jnp.transpose(cache_pool, (1, 2, 0))).reshape(-1, 3, 96, 128)
+    attended = attend(table, page_counts, queries, new_latent, incoming)
     return layer(
         attended, residual, routes, norm_gain, w_router.T, w_uv, w_out, w_gate, w_up, w_down
     )

time: 233 us -> 215 us (0.923)
  Pallas kernels: 224 us -> 214 us
  other arithmetic: 5.06 us -> 0 us
    pallas_call x1, Pallas kernels: 92.8 us -> 82.5 us  [layer(): pl.pallas_call(layer_kernel, out_shape=jax.ShapeDtypeStruct((2, 4, 2 * HA...]
where the time goes in v4:
time: 215 us
  Pallas kernels  214 us (100%)
    pallas_call x1, Pallas kernels, exchange(): pl.pallas_call(exchange_kernel, out_shape=jax.ShapeDtypeStruct((4, 4, 4,...  118 us
    pallas_call x1, Pallas kernels, layer(): pl.pallas_call(layer_kernel, out_shape=jax.ShapeDtypeStruct((2, 4, 2 * HA...  82.5 us
    pallas_call x1, Pallas kernels, attend(): pl.pallas_call(attend_kernel, out_shape=jax.ShapeDtypeStruct((8, 64, LATE...  12.6 us

profile of v4, /device:TPU:1, one launch (start us, length us, event | category | flops | bytes accessed | tf_op | source)
XLA Modules:
  0.0 215.0 jit_solution(8445024539005537813)
XLA Ops:
  0.0 118.5 %exchange.1 = bf16[4,4,4,2,3,96,128]{6,5,4,3,2,1,0:T(8,128)(2,1)} custom-call(s32[64,128]{1,0:T(8,128)} %bitcast.7, bf16[64,576,128]{2,1,0:T(8,128)(2,1)} %bitcast.5), custom_call_target="tpu_custom_call" | custom-call | tf_op jit(solution)/shard_map/exchange/pallas_call | solution.py:208
  118.5 12.6 %attend.1.attended = bf16[8,64,512]{2,1,0:T(8,128)(2,1)} custom-call(s32[64,128]{1,0:T(8,128)} %bitcast.8, s32[1,4]{1,0:T(1,128)} %counts.1, bf16[2,4,64,576]{3,2,1,0:T(8,128)(2,1)} %q_ref.1, bf16[2,4,576]{2,1,0:T(4,128)(2,1)} %new_ref.1, bf16[128,3,96,128]{3,2,1,0:T(8,128)(2,1)} %bitcast.4), custom_call_target="tpu_custom_call" | custom-call | tf_op jit(solution)/shard_map/attend/pallas_call | solution.py:327
  131.1 82.5 %layer.1 = bf16[2,4,3584]{2,1,0:T(4,128)(2,1)} custom-call(bf16[8,64,512]{2,1,0:T(8,128)(2,1)} %attend.1.attended, bf16[2,4,3584]{2,1,0:T(4,128)(2,1)} %residual.1, s32[2,4,8]{2,1,0:T(4,128)} %routes.1, f32[3584]{0:T(1024)} %gain.1, f32[16,3584]{1,0:T(8,128)} %bitcast.6, bf16[8,512,128]{2,1,0:T(8,128)(2,1)} %w_uv.1, bf16[1024,3584]{1,0:T(8,128)(2,1)} %w_out.1, ...), custom_call_target="tpu_custom_call" | custom-call | tf_op jit(solution)/shard_map/layer/pallas_call | solution.py:717
  213.6 1.5 copy.16

commit v5 on v4

--- a/solution.py
+++ b/solution.py
@@ -75,34 +75,25 @@
             y = lax.dot_general(onehot, x, (((1,), (1,)), ((), ())), preferred_element_type=F32)
             for i in range(4):
                 stage[:, j + i, :] = y[:, i * 128 : (i + 1) * 128]
-        at = pl.multiple_of(row, 16)
         block = stage[...].astype(BF16).reshape(4, 4, 4, 2, 16, 128)
-        slots[cls, :, :, :, :, pl.ds(at, 16), :] = block
-
-    def latent_rows(cls, chunk, first, count, row):
-        def unit(u, _):
-            def pieces(j):
-                t = (first + u) * 16 + j
-                return [pool_v[pl.ds(t, 4), chunk * 128 : (chunk + 1) * 128, :].reshape(512, 128)]
-
-            put(cls, row + u * 16, pieces)
-            return 0
-
-        lax.fori_loop(0, count, unit, 0)
-
-    def rope_rows(cls, row):
-        def unit(u, _):
-            def pieces(j):
-                found = []
-                for i in range(4):
-                    found.append(pool_v[u * 16 + j + i, 512:576, :])
-                    found.append(pool_v[32 + u * 16 + j + i, 512:576, :])
-                return found
-
-            put(cls, row + u * 16, pieces)
-            return 0
-
-        lax.fori_loop(0, 2, unit, 0)
+        slots[cls, :, :, :, :, row : row + 16, :] = block
+
+    def latent_rows(cls, chunk, unit, row):
+        def pieces(j):
+            t = unit * 16 + j
+            return [pool_v[pl.ds(t, 4), chunk * 128 : (chunk + 1) * 128, :].reshape(512, 128)]
+
+        put(cls, row, pieces)
+
+    def rope_rows(cls, unit, row):
+        def pieces(j):
+            found = []
+            for i in range(4):
+                found.append(pool_v[unit * 16 + j + i, 512:576, :])
+                found.append(pool_v[32 + unit * 16 + j + i, 512:576, :])
+            return found
+
+        put(cls, row, pieces)
 
     sends = []
 
@@ -116,18 +107,18 @@
     def landed(ref, sem):
         pltpu.make_async_copy(ref, ref, sem).wait()
 
-    for part in range(3):
-        rows = pl.ds(part * 32, 32)
-        for load in loads[2 * part : 2 * part + 2]:
-            load.wait()
+    for part in range(6):
+        rows = pl.ds(part * 16, 16)
+        if part < 4:
+            loads[part].wait()
         for cls, order in enumerate(ORDERS):
             a1, a2, a3 = order
-            if part < 2:
-                latent_rows(cls, cls, 2 * part, 2, 32 * part)
+            if part < 4:
+                latent_rows(cls, cls, part, 16 * part)
             elif cls < 2:
-                latent_rows(cls, 3, 2 * cls, 2, 64)
+                latent_rows(cls, 3, 2 * cls + part - 4, 16 * part)
             else:
-                rope_rows(cls, 64)
+                rope_rows(cls, part - 4, 16 * part)
             if part == 0 and cls == 0:
                 pl.semaphore_wait(barrier, len(peers))
             for d in (1, 2, 3):
@@ -138,7 +129,7 @@
                     held1.at[(cls,) + dst + (pl.ds(0, 2), rows)],
                     send1.at[cls, d, part], recv1.at[cls, d, part], along(a1, d, core),
                 )
-            if part == 2:
+            if part == 5:
                 own = (cls,) + spec_of(order, (pos[a1], whole, whole))
                 pltpu.make_async_copy(slots.at[own], held1.at[own], lsem.at[cls]).start()
 
@@ -173,8 +164,8 @@
         for cls, order in enumerate(ORDERS):
             src1 = (pos[order[0]] + 4 - e) % 4
             at = spec_of(order, (src1, whole, whole))
-            for part in range(3):
-                rows = pl.ds(part * 32, 32)
+            for part in range(6):
+                rows = pl.ds(part * 16, 16)
                 landed(held1.at[(cls,) + at + (pl.ds(0, 2), rows)], recv1.at[cls, e, part])
             second(cls, held1, e)
     for cls, order in enumerate(ORDERS):
@@ -216,7 +207,7 @@
             pltpu.VMEM(held, BF16),
             pltpu.VMEM(held, BF16),
             pltpu.VMEM((128, 16, 128), F32),
-            dma((4,)), dma((3,)), dma((3, 4)), dma((3, 4, 3)), dma((3, 4, 3)), dma((3, 4, 4)),
+            dma((4,)), dma((3,)), dma((3, 4)), dma((3, 4, 6)), dma((3, 4, 6)), dma((3, 4, 4)),
             dma((3, 4, 4)), dma((3, 4, 4, 2)), dma((3, 4, 4, 2)),
         ],
         compiler_params=pltpu.CompilerParams(
@@ -227,30 +218,19 @@
 
 
 def attend_kernel(
-    table, counts, q_ref, new_ref, slots, out_ref, own_ref, keys, last, ropes, scores, sem
+    table, counts, q_ref, new_ref, slots, out_ref, own_ref, keys, scores, sem
 ):
     pages = 64
     me = lax.axis_index("dp") * 8 + lax.axis_index("ep")
 
     def fetch(j, _):
-        at = pl.multiple_of(j * PAGE, PAGE)
-        slot = slots.at[table[j, me] // 128]
-        pltpu.make_async_copy(
-            slot.at[:, pl.ds(0, 64), :], keys.at[:, pl.ds(at, PAGE), :], sem.at[0]
-        ).start()
-        pltpu.make_async_copy(
-            slot.at[pl.ds(0, 2), pl.ds(64, 32), :], last.at[j], sem.at[1]
-        ).start()
-        pltpu.make_async_copy(slot.at[2, pl.ds(64, 32), :], ropes.at[j], sem.at[2]).start()
+        pltpu.make_async_copy(slots.at[table[j, me] // 128], keys.at[j], sem).start()
         return 0
 
     lax.fori_loop(0, pages, fetch, 0)
 
     def clear(j, _):
-        at = pl.multiple_of((pages + j) * PAGE, PAGE)
-        keys[:, pl.ds(at, PAGE), :] = jnp.zeros((3, PAGE, 128), BF16)
-        last[pages + j] = jnp.zeros((2, 32, 128), BF16)
-        ropes[pages + j] = jnp.zeros((32, 128), BF16)
+        keys[pages + j] = jnp.zeros((3, 96, 128), BF16)
         return 0
 
     lax.fori_loop(0, TILE, clear, 0)
@@ -259,19 +239,16 @@
         fresh = new_ref[step].astype(F32)
         for r in range(4):
             own_ref[r, step : step + 1, :] = fresh[r : r + 1]
-    for k, ref in enumerate(
-        (keys.at[:, pl.ds(0, pages * PAGE), :], last.at[pl.ds(0, pages)], ropes.at[pl.ds(0, pages)])
-    ):
-        pltpu.make_async_copy(ref, ref, sem.at[k]).wait()
+    filled = keys.at[pl.ds(0, pages)]
+    pltpu.make_async_copy(filled, filled, sem).wait()
     width = TILE * PAGE
     step_of = lax.broadcasted_iota(jnp.int32, (128, 16), 0) // 64
     token = lax.broadcasted_iota(jnp.int32, (128, 16), 1)
     low = lax.broadcasted_iota(jnp.int32, (TILE, 32, 128), 2) < ROPE
 
     def values_of(page):
-        at = pl.multiple_of(page * PAGE, PAGE)
-        parts = [keys[k, pl.ds(at, width), :] for k in range(3)]
-        parts.append(last[pl.ds(page, TILE)].reshape(width, 128))
+        parts = [keys[pl.ds(page, TILE), k, 0:64, :].reshape(width, 128) for k in range(3)]
+        parts.append(keys[pl.ds(page, TILE), 0:2, 64:96, :].reshape(width, 128))
         return jnp.concatenate(parts, axis=1)
 
     def request(r, start):
@@ -286,7 +263,7 @@
 
         def score(t, top):
             page = start + t * TILE
-            rope = ropes[pl.ds(page, TILE)]
+            rope = keys[pl.ds(page, TILE), 2, 64:96, :]
             zero = jnp.zeros_like(rope)
             pair = jnp.concatenate([jnp.where(low, rope, zero), jnp.where(low, zero, rope)], axis=1)
             key = jnp.concatenate([values_of(page), pair.reshape(width, 128)], axis=1)
@@ -331,11 +308,9 @@
         out_specs=vmem,
         scratch_shapes=[
             pltpu.VMEM((4, 16, LATENT + ROPE), F32),
-            pltpu.VMEM((3, (64 + TILE) * PAGE, 128), BF16),
-            pltpu.VMEM((64 + TILE, 2, 32, 128), BF16),
-            pltpu.VMEM((64 + TILE, 32, 128), BF16),
+            pltpu.VMEM((64 + TILE, 3, 96, 128), BF16),
             pltpu.VMEM((32 // TILE, 128, TILE * PAGE), F32),
-            pltpu.SemaphoreType.DMA((3,)),
+            pltpu.SemaphoreType.DMA,
         ],
         compiler_params=pltpu.CompilerParams(vmem_limit_bytes=60 * 2**20),
         name="attend",
@@ -347,7 +322,7 @@
     out_ref,
     resid, member, heads_in, masked, part_out, part_in, res_all, mem_all, stat_out, stat_in, hidden,
     gath, v_uv, v_out, v_gate, v_up, v_down, acc, inner,
-    mix, sib_out, sib_in, t1, ul1, ur1, t2, ul2, ur2, last, fin_out, fin_in,
+    mix, sib_out, sib_in, t1, ul1, ur1, t2, last, fin_out, fin_in,
     wsem, lsem, head_s, head_r, part_s, part_r, pair_s, pair_r,
     ag1_s, ag1_r, ag2_s, ag2_r, ag3_s, ag3_r, sib_s, sib_r, red_s, red_r, sum_s, sum_r,
 ):
@@ -437,16 +412,14 @@
     flat = jnp.dot(pick, masked[...], preferred_element_type=F32).astype(BF16)
 
     copies[1].wait()
-    for h in range(2):
+    for h, turns in ((other, (1, 3, 5, 7)), (core, (2, 4, 6))):
         for t in range(HALF // 256):
-            col = h * HALF + t * 256
-            y = jnp.dot(flat, v_out[:, col : col + 256], preferred_element_type=F32)
+            cols = pl.ds(pl.multiple_of(h * HALF + t * 256, 256), 256)
+            y = jnp.dot(flat, v_out[:, cols], preferred_element_type=F32)
             part_out[h, :, :, t * 256 : (t + 1) * 256] = y.astype(BF16).reshape(4, 16, 256)
-    for o in range(1, 8):
-        to = (ep + o) % 8
-        remote(
-            part_out.at[to % 2, to // 2], part_in.at[ep], part_s.at[o], part_r.at[o], (dp, to)
-        )
+        for o in turns:
+            to = (ep + o) % 8
+            remote(part_out.at[h, to // 2], part_in.at[ep], part_s.at[o], part_r.at[o], (dp, to))
     landed(res_all.at[other_rows], pair_r.at[0])
     landed(mem_all.at[other_rows], pair_r.at[1])
     hid = part_out[core, pos[2]].astype(F32)
@@ -622,73 +595,78 @@
             landed(sib_in.at[b], red_r.at[cls, shift])
             mix[b] = (y + sib_in[b].astype(F32)).astype(BF16)
 
-    for phase in (2, 1):
-        bt, bl, br = (t1, ul1, ur1) if phase == 2 else (t2, ul2, ur2)
-        red = 0 if phase == 2 else 1
-
-        def block(cls, shift, half):
-            a1, a2, a3 = ORDERS[cls]
-            if phase == 1:
-                spec = spec_of((a1, a2, a3), (half, (pos[a2] + shift) % 4, pos[a3]))
-            else:
-                spec = spec_of((a1, a2, a3), (half, whole, (pos[a3] + shift) % 4))
-            return (cls, spec[0], spec[1], spec[2], slice(None), pl.ds(0, WIDTHS[cls]))
-
-        def temp(cls, half):
-            a1, a2, a3 = ORDERS[cls]
-            if phase == 1:
-                return (cls, half, slice(None), pl.ds(0, WIDTHS[cls]))
-            if a1 < a2:
-                return (cls, half, whole, slice(None), pl.ds(0, WIDTHS[cls]))
-            return (cls, whole, half, slice(None), pl.ds(0, WIDTHS[cls]))
-
-        def send(cls, shift, half, buf, k, delta):
-            remote(
-                mix.at[block(cls, shift, halves[half])], buf.at[temp(cls, halves[half])],
-                sum_s.at[cls, red, k], sum_r.at[cls, red, k], along(ORDERS[cls][phase], delta),
-            )
-
-        if phase == 2:
-            for_pair(2)
-            for_pair(1)
-            for_self(2)
-        for cls in range(3):
-            send(cls, 2, 0, bt, 0, 1)
-            send(cls, 2, 1, bt, 1, 3)
-        if phase == 2:
-            for_pair(3)
-            for_self(1)
-        for cls in range(3):
-            send(cls, 1, 1, bl, 2, 1)
-        if phase == 2:
-            for_self(3)
-        for cls in range(3):
-            send(cls, 3, 0, br, 3, 3)
-        for cls in range(3):
-            for half, shift, buf, k, delta in ((0, 1, bl, 0, 1), (1, 3, br, 1, 3)):
-                at, tmp = block(cls, shift, halves[half]), temp(cls, halves[half])
-                landed(bt.at[tmp], sum_r.at[cls, red, k])
-                mix[at] = (mix[at].astype(F32) + bt[tmp].astype(F32)).astype(BF16)
-                send(cls, shift, half, buf, k + 4, delta)
-        if phase == 2:
-            for_pair(0)
-            for_self(0)
-        for cls in range(3):
-            for half, ks in ((0, (4, 3)), (1, (2, 5))):
-                at, tmp = block(cls, 0, halves[half]), temp(cls, halves[half])
-                landed(bl.at[tmp], sum_r.at[cls, red, ks[0]])
-                landed(br.at[tmp], sum_r.at[cls, red, ks[1]])
-                total = mix[at].astype(F32) + bl[tmp].astype(F32) + br[tmp].astype(F32)
-                mix[at] = total.astype(BF16)
-
+    def block(cls, shift, half):
+        a1, a2, a3 = ORDERS[cls]
+        spec = spec_of((a1, a2, a3), (half, whole, (pos[a3] + shift) % 4))
+        return (cls, spec[0], spec[1], spec[2], slice(None), pl.ds(0, WIDTHS[cls]))
+
+    def temp(cls, half):
+        a1, a2, a3 = ORDERS[cls]
+        first, then = (half, whole) if a1 < a2 else (whole, half)
+        return (cls, first, then, slice(None), pl.ds(0, WIDTHS[cls]))
+
+    def send(cls, shift, half, buf, k, delta):
+        remote(
+            mix.at[block(cls, shift, halves[half])], buf.at[temp(cls, halves[half])],
+            sum_s.at[cls, 0, k], sum_r.at[cls, 0, k], along(ORDERS[cls][2], delta),
+        )
+
+    for_pair(2)
+    for_pair(1)
+    for_self(2)
+    for cls in range(3):
+        send(cls, 2, 0, t1, 0, 1)
+        send(cls, 2, 1, t1, 1, 3)
+    for_pair(3)
+    for_self(1)
+    for cls in range(3):
+        send(cls, 1, 1, ul1, 2, 1)
+    for_self(3)
+    for cls in range(3):
+        send(cls, 3, 0, ur1, 3, 3)
+    for cls in range(3):
+        for half, shift, buf, k, delta in ((0, 1, ul1, 0, 1), (1, 3, ur1, 1, 3)):
+            at, tmp = block(cls, shift, halves[half]), temp(cls, halves[half])
+            landed(t1.at[tmp], sum_r.at[cls, 0, k])
+            mix[at] = (mix[at].astype(F32) + t1[tmp].astype(F32)).astype(BF16)
+            send(cls, shift, half, buf, k + 4, delta)
+    for_pair(0)
+    for_self(0)
     for cls, order in enumerate(ORDERS):
-        a1 = order[0]
-        for d in (1, 2, 3):
+        a1, a2, a3 = order
+        n = WIDTHS[cls]
+        for half, ks in ((0, (4, 3)), (1, (2, 5))):
+            tmp = temp(cls, halves[half])
+            landed(ul1.at[tmp], sum_r.at[cls, 0, ks[0]])
+            landed(ur1.at[tmp], sum_r.at[cls, 0, ks[1]])
+        for d in (2, 1, 3, 0):
+            where = (pos[a2] + d) % 4
+            spec = spec_of(order, (whole, where, pos[a3]))
+            at = (cls, spec[0], spec[1], spec[2], slice(None), pl.ds(0, n))
+            first, then = (whole, where) if a1 < a2 else (where, whole)
+            tmp = (cls, first, then, slice(None), pl.ds(0, n))
+            total = mix[at].astype(F32) + ul1[tmp].astype(F32) + ur1[tmp].astype(F32)
+            mix[at] = total.astype(BF16)
+            if d:
+                dst = t2.at[cls, d - 1, :, :, pl.ds(0, n)]
+                remote(mix.at[at], dst, sum_s.at[cls, 1, d], sum_r.at[cls, 1, d], along(a2, d))
+    for cls, order in enumerate(ORDERS):
+        a1, a2, a3 = order
+        n = WIDTHS[cls]
+        for d in (1, 3, 2):
+            landed(t2.at[cls, d - 1, :, :, pl.ds(0, n)], sum_r.at[cls, 1, d])
+        for d in (2, 1, 3, 0):
+            where = (pos[a1] + d) % 4
             coords = list(pos)
-            coords[a1] = (pos[a1] + d) % 4
-            src = mix.at[cls, coords[0], coords[1], coords[2], :, pl.ds(0, WIDTHS[cls])]
-            dst = last.at[cls, d - 1, :, pl.ds(0, WIDTHS[cls])]
-            remote(src, dst, sum_s.at[cls, 2, d], sum_r.at[cls, 2, d], along(a1, d))
+            coords[a1] = where
+            at = (cls, coords[0], coords[1], coords[2], slice(None), pl.ds(0, n))
+            total = mix[at].astype(F32)
+            for k in range(3):
+                total = total + t2[cls, k, where, :, 0:n].astype(F32)
+            mix[at] = total.astype(BF16)
+            if d:
+                dst = last.at[cls, d - 1, :, pl.ds(0, n)]
+                remote(mix.at[at], dst, sum_s.at[cls, 2, d], sum_r.at[cls, 2, d], along(a1, d))
     for cls in range(3):
         n = WIDTHS[cls]
         total = mix[cls, pos[0], pos[1], pos[2], :, 0:n].astype(F32)
@@ -700,11 +678,11 @@
         fin_out[1, :, cls * PART : cls * PART + n] = total[8:16]
     remote(fin_out.at[other], fin_in, pair_s.at[3], pair_r.at[3], sibling)
     for s in range(2):
-        out_ref[s, :, half_cols] = fin_out[core, s * 4 : s * 4 + 4].astype(BF16)
+        out_ref[s, :, half_cols] = fin_out[core, s * 4 : s * 4 + 4]
     landed(fin_in, pair_r.at[3])
     for s in range(2):
         cols = pl.ds(pl.multiple_of(other * HALF, 128), HALF)
-        out_ref[s, :, cols] = fin_in[s * 4 : s * 4 + 4].astype(BF16)
+        out_ref[s, :, cols] = fin_in[s * 4 : s * 4 + 4]
     for src, ssem in sent:
         pltpu.make_async_copy(src, src, ssem).wait()
 
@@ -716,7 +694,7 @@
     grid = (3, 4, 4, 4, 16, PART)
     return pl.pallas_call(
         layer_kernel,
-        out_shape=jax.ShapeDtypeStruct((2, 4, 2 * HALF), BF16),
+        out_shape=jax.ShapeDtypeStruct((2, 4, 2 * HALF), F32),
         in_specs=[vmem] * 5 + [hbm] * 5,
         out_specs=vmem,
         scratch_shapes=[
@@ -745,9 +723,7 @@
             pltpu.VMEM((3, 4, 4, 16, PART), BF16),
             pltpu.VMEM((3, 4, 4, 16, PART), BF16),
             pltpu.VMEM((3, 4, 4, 16, PART), BF16),
-            pltpu.VMEM((3, 4, 16, PART), BF16),
-            pltpu.VMEM((3, 4, 16, PART), BF16),
-            pltpu.VMEM((3, 4, 16, PART), BF16),
+            pltpu.VMEM((3, 3, 4, 16, PART), BF16),
             pltpu.VMEM((3, 3, 16, PART), BF16),
             pltpu.VMEM((2, 8, HALF), F32),
             pltpu.VMEM((8, HALF), F32),
@@ -782,9 +758,10 @@
     table = page_table.T
     incoming = exchange(table, jnp.transpose(cache_pool, (1, 2, 0))).reshape(-1, 3, 96, 128)
     attended = attend(table, page_counts, queries, new_latent, incoming)
-    return layer(
+    out = layer(
         attended, residual, routes, norm_gain, w_router.T, w_uv, w_out, w_gate, w_up, w_down
     )
+    return out.astype(BF16)
 
 
 def solution(mesh):

time: 215 us -> 211 us (0.981)
  Pallas kernels: 214 us -> 209 us
    pallas_call x1, Pallas kernels: 82.5 us -> 79.2 us  [layer(): pl.pallas_call(layer_kernel, out_shape=jax.ShapeDtypeStruct((2, 4, 2 * HA...]
where the time goes in v5:
time: 211 us
  Pallas kernels  209 us (99%)
    pallas_call x1, Pallas kernels, exchange(): pl.pallas_call(exchange_kernel, out_shape=jax.ShapeDtypeStruct((4, 4, 4,...  118 us
    pallas_call x1, Pallas kernels, layer(): pl.pallas_call(layer_kernel, out_shape=jax.ShapeDtypeStruct((2, 4, 2 * HA...  79.2 us
    pallas_call x1, Pallas kernels, attend(): pl.pallas_call(attend_kernel, out_shape=jax.ShapeDtypeStruct((8, 64, LATE...  12.5 us

profile of v5, /device:TPU:1, one launch (start us, length us, event | category | flops | bytes accessed | tf_op | source)
XLA Modules:
  0.0 211.0 jit_solution(6834370451724583208)
XLA Ops:
  0.0 117.7 %exchange.1 = bf16[4,4,4,2,3,96,128]{6,5,4,3,2,1,0:T(8,128)(2,1)} custom-call(s32[64,128]{1,0:T(8,128)} %bitcast.7, bf16[64,576,128]{2,1,0:T(8,128)(2,1)} %bitcast.5), custom_call_target="tpu_custom_call" | custom-call | tf_op jit(solution)/shard_map/exchange/pallas_call | solution.py:199
  117.7 12.5 %attend.1.attended = bf16[8,64,512]{2,1,0:T(8,128)(2,1)} custom-call(s32[64,128]{1,0:T(8,128)} %bitcast.8, s32[1,4]{1,0:T(1,128)} %counts.1, bf16[2,4,64,576]{3,2,1,0:T(8,128)(2,1)} %q_ref.1, bf16[2,4,576]{2,1,0:T(4,128)(2,1)} %new_ref.1, bf16[128,3,96,128]{3,2,1,0:T(8,128)(2,1)} %bitcast.4), custom_call_target="tpu_custom_call" | custom-call | tf_op jit(solution)/shard_map/attend/pallas_call | solution.py:304
  130.2 79.2 %layer.1 = f32[2,4,3584]{2,1,0:T(4,128)} custom-call(bf16[8,64,512]{2,1,0:T(8,128)(2,1)} %attend.1.attended, bf16[2,4,3584]{2,1,0:T(4,128)(2,1)} %residual.1, s32[2,4,8]{2,1,0:T(4,128)} %routes.1, f32[3584]{0:T(1024)} %gain.1, f32[16,3584]{1,0:T(8,128)} %bitcast.6, bf16[8,512,128]{2,1,0:T(8,128)(2,1)} %w_uv.1, bf16[1024,3584]{1,0:T(8,128)(2,1)} %w_out.1, ...), custom_call_target="tpu_custom_call" | custom-call | tf_op jit(solution)/shard_map/layer/pallas_call | solution.py:695
  209.4 1.5 convert_element_type.3

commit v6 on v5

--- a/solution.py
+++ b/solution.py
@@ -28,7 +28,7 @@
 def exchange_kernel(
     table, pool, out,
     pool_v, slots, held1, held2, stage,
-    psem, lsem, csem, send1, recv1, send2, recv2, send3, recv3,
+    psem, lsem, send1, recv1, send2, recv2, send3, recv3,
 ):
     dp = lax.axis_index("dp")
     ep = lax.axis_index("ep")
@@ -95,14 +95,11 @@
 
         put(cls, row, pieces)
 
-    sends = []
-
     def remote(src, dst, ssem, rsem, peer):
         pltpu.make_async_remote_copy(
             src_ref=src, dst_ref=dst, send_sem=ssem, recv_sem=rsem,
             device_id=peer, device_id_type=MESH,
         ).start()
-        sends.append((src, ssem))
 
     def landed(ref, sem):
         pltpu.make_async_copy(ref, ref, sem).wait()
@@ -127,7 +124,7 @@
                 remote(
                     slots.at[(cls,) + src + (pl.ds(0, 2), rows)],
                     held1.at[(cls,) + dst + (pl.ds(0, 2), rows)],
-                    send1.at[cls, d, part], recv1.at[cls, d, part], along(a1, d, core),
+                    send1.at[cls], recv1.at[cls, d], along(a1, d, core),
                 )
             if part == 5:
                 own = (cls,) + spec_of(order, (pos[a1], whole, whole))
@@ -141,7 +138,7 @@
             dst = spec_of(order, (src1, pos[a2], whole))
             remote(
                 buf.at[(cls,) + src], held2.at[(cls,) + dst],
-                send2.at[cls, d, e], recv2.at[cls, d, e], along(a2, d, core),
+                send2.at[cls], recv2.at[cls, d], along(a2, d, core),
             )
 
     def third(cls, buf, f):
@@ -154,19 +151,16 @@
                 a = buf.at[(cls,) + src + (c,)]
                 b = out.at[dst + (core, cls)]
                 if d == 0 and k == 0:
-                    pltpu.make_async_copy(a, b, csem.at[cls, f]).start()
+                    pltpu.make_async_copy(a, b, recv3.at[cls]).start()
                 else:
-                    remote(a, b, send3.at[cls, f, d, k], recv3.at[cls, f, d, k], along(a3, d, c))
+                    remote(a, b, send3.at[cls, d], recv3.at[cls], along(a3, d, c))
 
     for cls in range(3):
         second(cls, slots, 0)
     for e in (1, 3, 2):
         for cls, order in enumerate(ORDERS):
             src1 = (pos[order[0]] + 4 - e) % 4
-            at = spec_of(order, (src1, whole, whole))
-            for part in range(6):
-                rows = pl.ds(part * 16, 16)
-                landed(held1.at[(cls,) + at + (pl.ds(0, 2), rows)], recv1.at[cls, e, part])
+            landed(held1.at[(cls,) + spec_of(order, (src1, whole, whole))], recv1.at[cls, e])
             second(cls, held1, e)
     for cls, order in enumerate(ORDERS):
         own = spec_of(order, (pos[order[0]], whole, whole))
@@ -175,20 +169,19 @@
     for f in (1, 3, 2):
         for cls, order in enumerate(ORDERS):
             a1, a2, a3 = order
-            for e in range(4):
-                at = spec_of(order, ((pos[a1] + 4 - e) % 4, (pos[a2] + 4 - f) % 4, whole))
-                landed(held2.at[(cls,) + at], recv2.at[cls, f, e])
+            at = spec_of(order, (whole, (pos[a2] + 4 - f) % 4, whole))
+            landed(held2.at[(cls,) + at], recv2.at[cls, f])
             third(cls, held2, f)
-    for cls, order in enumerate(ORDERS):
-        a1, a2, a3 = order
-        for f in range(4):
-            for d in range(4):
-                for k, c in ((0, core), (1, other)):
-                    at = spec_of(order, (whole, (pos[a2] + 4 - f) % 4, (pos[a3] + 4 - d) % 4))
-                    ref = out.at[at + (c, cls)]
-                    landed(ref, csem.at[cls, f] if d == 0 and k == 0 else recv3.at[cls, f, d, k])
-    for src, ssem in sends:
-        landed(src, ssem)
+    for cls in range(3):
+        most = held1.at[cls, pl.ds(0, 3)]
+        landed(most, send1.at[cls])
+        landed(most, send2.at[cls])
+    for cls in range(3):
+        landed(held1.at[cls, 0, pl.ds(0, 2)], send3.at[cls, 0])
+        for d in (1, 2, 3):
+            landed(held1.at[cls, 0], send3.at[cls, d])
+    for cls in range(3):
+        landed(out.at[:, :, :, :, cls], recv3.at[cls])
 
 
 def exchange(table, pool):
@@ -207,8 +200,7 @@
             pltpu.VMEM(held, BF16),
             pltpu.VMEM(held, BF16),
             pltpu.VMEM((128, 16, 128), F32),
-            dma((4,)), dma((3,)), dma((3, 4)), dma((3, 4, 6)), dma((3, 4, 6)), dma((3, 4, 4)),
-            dma((3, 4, 4)), dma((3, 4, 4, 2)), dma((3, 4, 4, 2)),
+            dma((4,)), dma((3,)), dma((3,)), dma((3, 4)), dma((3,)), dma((3, 4)), dma((3, 4)), dma((3,)),
         ],
         compiler_params=pltpu.CompilerParams(
             collective_id=2, has_side_effects=True, vmem_limit_bytes=56 * 2**20
@@ -357,6 +349,11 @@
 
     sent = []
 
+    def settle():
+        for src, ssem in sent:
+            pltpu.make_async_copy(src, src, ssem).wait()
+        sent.clear()
+
     loads = [(w_uv, v_uv), (w_out, v_out), (w_gate, v_gate), (w_up, v_up), (w_down, v_down)]
     copies = [pltpu.make_async_copy(a, b, wsem.at[i]) for i, (a, b) in enumerate(loads)]
     for copy in copies:
@@ -423,6 +420,7 @@
     landed(res_all.at[other_rows], pair_r.at[0])
     landed(mem_all.at[other_rows], pair_r.at[1])
     hid = part_out[core, pos[2]].astype(F32)
+    settle()
     for o in range(1, 8):
         src = (ep + 8 - o) % 8
         landed(part_in.at[src], part_r.at[o])
@@ -632,6 +630,7 @@
             send(cls, shift, half, buf, k + 4, delta)
     for_pair(0)
     for_self(0)
+    settle()
     for cls, order in enumerate(ORDERS):
         a1, a2, a3 = order
         n = WIDTHS[cls]
@@ -679,12 +678,11 @@
     remote(fin_out.at[other], fin_in, pair_s.at[3], pair_r.at[3], sibling)
     for s in range(2):
         out_ref[s, :, half_cols] = fin_out[core, s * 4 : s * 4 + 4]
+    settle()
     landed(fin_in, pair_r.at[3])
     for s in range(2):
         cols = pl.ds(pl.multiple_of(other * HALF, 128), HALF)
         out_ref[s, :, cols] = fin_in[s * 4 : s * 4 + 4]
-    for src, ssem in sent:
-        pltpu.make_async_copy(src, src, ssem).wait()
 
 
 def layer(attended, residual, routes, gain, router, w_uv, w_out, w_gate, w_up, w_down):
@@ -695,7 +693,7 @@
     return pl.pallas_call(
         layer_kernel,
         out_shape=jax.ShapeDtypeStruct((2, 4, 2 * HALF), F32),
-        in_specs=[vmem] * 5 + [hbm] * 5,
+        in_specs=[hbm] + [vmem] * 4 + [hbm] * 5,
         out_specs=vmem,
         scratch_shapes=[
             pltpu.VMEM((2, 8, HALF), F32),

time: 211 us -> 207 us (0.981)
  Pallas kernels: 209 us -> 205 us
    pallas_call x1, Pallas kernels: 118 us -> 114 us  [exchange(): pl.pallas_call(exchange_kernel, out_shape=jax.ShapeDtypeStruct((4, 4, 4,...]
where the time goes in v6:
time: 207 us
  Pallas kernels  205 us (99%)
    pallas_call x1, Pallas kernels, exchange(): pl.pallas_call(exchange_kernel, out_shape=jax.ShapeDtypeStruct((4, 4, 4,...  114 us
    pallas_call x1, Pallas kernels, layer(): pl.pallas_call(layer_kernel, out_shape=jax.ShapeDtypeStruct((2, 4, 2 * HA...  79.9 us
    pallas_call x1, Pallas kernels, attend(): pl.pallas_call(attend_kernel, out_shape=jax.ShapeDtypeStruct((8, 64, LATE...  11.5 us

profile of v6, /device:TPU:1, one launch (start us, length us, event | category | flops | bytes accessed | tf_op | source)
XLA Modules:
  0.0 206.7 jit_solution(5134622624628157503)
XLA Ops:
  0.0 113.7 %exchange.1 = bf16[4,4,4,2,3,96,128]{6,5,4,3,2,1,0:T(8,128)(2,1)} custom-call(s32[64,128]{1,0:T(8,128)} %bitcast.7, bf16[64,576,128]{2,1,0:T(8,128)(2,1)} %bitcast.5), custom_call_target="tpu_custom_call" | custom-call | tf_op jit(solution)/shard_map/exchange/pallas_call | solution.py:192
  113.7 11.5 %attend.1.attended = bf16[8,64,512]{2,1,0:T(8,128)(2,1)} custom-call(s32[64,128]{1,0:T(8,128)} %bitcast.8, s32[1,4]{1,0:T(1,128)} %counts.1, bf16[2,4,64,576]{3,2,1,0:T(8,128)(2,1)} %q_ref.1, bf16[2,4,576]{2,1,0:T(4,128)(2,1)} %new_ref.1, bf16[128,3,96,128]{3,2,1,0:T(8,128)(2,1)} %bitcast.4), custom_call_target="tpu_custom_call" | custom-call | tf_op jit(solution)/shard_map/attend/pallas_call | solution.py:296
  125.3 79.9 %layer.1 = f32[2,4,3584]{2,1,0:T(4,128)} custom-call(bf16[8,64,512]{2,1,0:T(8,128)(2,1)} %attend.1.attended, bf16[2,4,3584]{2,1,0:T(4,128)(2,1)} %residual.1, s32[2,4,8]{2,1,0:T(4,128)} %routes.1, f32[3584]{0:T(1024)} %gain.1, f32[16,3584]{1,0:T(8,128)} %bitcast.6, bf16[8,512,128]{2,1,0:T(8,128)(2,1)} %w_uv.1, bf16[1024,3584]{1,0:T(8,128)(2,1)} %w_out.1, ...), custom_call_target="tpu_custom_call" | custom-call | tf_op jit(solution)/shard_map/layer/pallas_call | solution.py:693
  205.1 1.5 convert_element_type.3

commit v7 on v6

--- a/solution.py
+++ b/solution.py
@@ -27,7 +27,7 @@
 
 def exchange_kernel(
     table, pool, out,
-    pool_v, slots, held1, held2, stage,
+    table_v, pool_v, slots, held1, held2, stage,
     psem, lsem, send1, recv1, send2, recv2, send3, recv3,
 ):
     dp = lax.axis_index("dp")
@@ -43,6 +43,8 @@
         )
         for i in range(4)
     ]
+    table_load = pltpu.make_async_copy(table, table_v, psem.at[4])
+    table_load.start()
     for load in loads:
         load.start()
 
@@ -63,7 +65,8 @@
     for peer in peers:
         pl.semaphore_signal(barrier, inc=1, device_id=peer, device_id_type=MESH)
 
-    pages = table[...]
+    table_load.wait()
+    pages = table_v[...]
     wanted = jnp.where(pages // 128 == dp * 8 + ep, pages % 128, 0)
     wanted = jnp.sum(wanted, axis=0, keepdims=True)
     page = lax.broadcasted_iota(jnp.int32, (128, 128), 0)
@@ -185,22 +188,22 @@
 
 
 def exchange(table, pool):
-    vmem = pl.BlockSpec(memory_space=pltpu.VMEM)
     hbm = pl.BlockSpec(memory_space=pl.ANY)
     dma = pltpu.SemaphoreType.DMA
     held = (3, 4, 4, 4, 2, 96, 128)
     return pl.pallas_call(
         exchange_kernel,
         out_shape=jax.ShapeDtypeStruct((4, 4, 4, 2, 3, 96, 128), BF16),
-        in_specs=[vmem, hbm],
+        in_specs=[hbm, hbm],
         out_specs=hbm,
         scratch_shapes=[
+            pltpu.VMEM(table.shape, jnp.int32),
             pltpu.VMEM(pool.shape, BF16),
             pltpu.VMEM(held, BF16),
             pltpu.VMEM(held, BF16),
             pltpu.VMEM(held, BF16),
             pltpu.VMEM((128, 16, 128), F32),
-            dma((4,)), dma((3,)), dma((3,)), dma((3, 4)), dma((3,)), dma((3, 4)), dma((3, 4)), dma((3,)),
+            dma((5,)), dma((3,)), dma((3,)), dma((3, 4)), dma((3,)), dma((3, 4)), dma((3, 4)), dma((3,)),
         ],
         compiler_params=pltpu.CompilerParams(
             collective_id=2, has_side_effects=True, vmem_limit_bytes=56 * 2**20
@@ -210,16 +213,23 @@
 
 
 def attend_kernel(
-    table, counts, q_ref, new_ref, slots, out_ref, own_ref, keys, scores, sem
+    table, counts, queries, new, slots, out_ref, q_ref, new_ref, own_ref, keys, scores, sem, in_sem
 ):
     pages = 64
     me = lax.axis_index("dp") * 8 + lax.axis_index("ep")
 
+    loads = [
+        pltpu.make_async_copy(queries, q_ref, in_sem.at[0]),
+        pltpu.make_async_copy(new, new_ref, in_sem.at[1]),
+    ]
+    loads[1].start()
+
     def fetch(j, _):
         pltpu.make_async_copy(slots.at[table[j, me] // 128], keys.at[j], sem).start()
         return 0
 
     lax.fori_loop(0, pages, fetch, 0)
+    loads[0].start()
 
     def clear(j, _):
         keys[pages + j] = jnp.zeros((3, 96, 128), BF16)
@@ -227,10 +237,12 @@
 
     lax.fori_loop(0, TILE, clear, 0)
     own_ref[...] = jnp.zeros_like(own_ref)
+    loads[1].wait()
     for step in range(2):
         fresh = new_ref[step].astype(F32)
         for r in range(4):
             own_ref[r, step : step + 1, :] = fresh[r : r + 1]
+    loads[0].wait()
     filled = keys.at[pl.ds(0, pages)]
     pltpu.make_async_copy(filled, filled, sem).wait()
     width = TILE * PAGE
@@ -296,13 +308,16 @@
     return pl.pallas_call(
         attend_kernel,
         out_shape=jax.ShapeDtypeStruct((8, 64, LATENT), BF16),
-        in_specs=[smem, smem, vmem, vmem, pl.BlockSpec(memory_space=pl.ANY)],
+        in_specs=[smem, smem] + [pl.BlockSpec(memory_space=pl.ANY)] * 3,
         out_specs=vmem,
         scratch_shapes=[
+            pltpu.VMEM(queries.shape, BF16),
+            pltpu.VMEM(new_latent.shape, BF16),
             pltpu.VMEM((4, 16, LATENT + ROPE), F32),
             pltpu.VMEM((64 + TILE, 3, 96, 128), BF16),
             pltpu.VMEM((32 // TILE, 128, TILE * PAGE), F32),
             pltpu.SemaphoreType.DMA,
+            pltpu.SemaphoreType.DMA((2,)),
         ],
         compiler_params=pltpu.CompilerParams(vmem_limit_bytes=60 * 2**20),
         name="attend",
@@ -310,9 +325,9 @@
 
 
 def layer_kernel(
-    attended, residual, routes, gain, router, w_uv, w_out, w_gate, w_up, w_down,
+    attended, residual_in, routes_in, gain_in, router_in, w_uv, w_out, w_gate, w_up, w_down,
     out_ref,
-    resid, member, heads_in, masked, part_out, part_in, res_all, mem_all, stat_out, stat_in, hidden,
+    residual, routes, gain, router, resid, member, heads_in, masked, part_out, part_in, res_all, mem_all, stat_out, stat_in, hidden,
     gath, v_uv, v_out, v_gate, v_up, v_down, acc, inner,
     mix, sib_out, sib_in, t1, ul1, ur1, t2, last, fin_out, fin_in,
     wsem, lsem, head_s, head_r, part_s, part_r, pair_s, pair_r,
@@ -354,14 +369,26 @@
             pltpu.make_async_copy(src, src, ssem).wait()
         sent.clear()
 
-    loads = [(w_uv, v_uv), (w_out, v_out), (w_gate, v_gate), (w_up, v_up), (w_down, v_down)]
-    copies = [pltpu.make_async_copy(a, b, wsem.at[i]) for i, (a, b) in enumerate(loads)]
-    for copy in copies:
-        copy.start()
-
     barrier = pltpu.get_barrier_semaphore()
     for peer in ep_peers + ring_peers:
         pl.semaphore_signal(barrier, inc=1, device_id=peer, device_id_type=MESH)
+
+    loads = [(residual_in, residual), (routes_in, routes), (gain_in, gain), (router_in, router)]
+    small = [pltpu.make_async_copy(a, b, lsem.at[1 + i]) for i, (a, b) in enumerate(loads)]
+    loads = [(w_uv, v_uv), (w_out, v_out), (w_gate, v_gate), (w_up, v_up), (w_down, v_down)]
+    copies = [pltpu.make_async_copy(a, b, wsem.at[i]) for i, (a, b) in enumerate(loads)]
+    for copy in small + copies:
+        copy.start()
+    pl.semaphore_wait(barrier, len(ep_peers) + len(ring_peers))
+
+    for o in range(1, 8):
+        to = (ep + o) % 8
+        remote(attended.at[to], heads_in.at[ep], head_s.at[o], head_r.at[o], (dp, to))
+    own_heads = pltpu.make_async_copy(attended.at[ep], heads_in.at[ep], lsem.at[0])
+    own_heads.start()
+
+    for copy in small:
+        copy.wait()
     for h in range(2):
         cols = slice(h * HALF, (h + 1) * HALF)
         both = [residual[s, :, cols].astype(F32) for s in range(2)]
@@ -372,26 +399,19 @@
     for k in range(8):
         named = jnp.where(route[:, k : k + 1] == lanes, 1.0, named)
     member[...] = named
-
-    def clear(i, _):
-        acc[0, i] = jnp.zeros((4, 4, 16, 256), F32)
-        acc[1, i] = jnp.zeros((4, 4, 16, 256), F32)
-        return 0
-
-    lax.fori_loop(0, 4, clear, 0)
-    pl.semaphore_wait(barrier, len(ep_peers) + len(ring_peers))
-
-    for o in range(1, 8):
-        to = (ep + o) % 8
-        remote(attended.at[to], heads_in.at[ep], head_s.at[o], head_r.at[o], (dp, to))
-    own_heads = pltpu.make_async_copy(attended.at[ep], heads_in.at[ep], lsem)
-    own_heads.start()
     own_rows = pl.ds(pl.multiple_of(core * 8, 8), 8)
     other_rows = pl.ds(pl.multiple_of(other * 8, 8), 8)
     remote(resid.at[other], res_all.at[own_rows], pair_s.at[0], pair_r.at[0], sibling)
     remote(member, mem_all.at[own_rows], pair_s.at[1], pair_r.at[1], sibling)
     res_all[own_rows, :] = resid[core]
     mem_all[own_rows, :] = member[...]
+
+    def clear(i, _):
+        acc[0, i] = jnp.zeros((4, 4, 16, 256), F32)
+        acc[1, i] = jnp.zeros((4, 4, 16, 256), F32)
+        return 0
+
+    lax.fori_loop(0, 4, clear, 0)
     own_heads.wait()
     for o in range(1, 8):
         landed(heads_in.at[(ep + 8 - o) % 8], head_r.at[o])
@@ -484,7 +504,7 @@
     def second(cls, e):
         b = line(cls, e, 0)
         for d in (1, 3, 2):
-            remote(b, b, ag2_s.at[cls, d, e], ag2_r.at[cls, d, e], along(ORDERS[cls][1], d))
+            remote(b, b, ag2_s.at[cls, d, e], ag2_r.at[cls, d], along(ORDERS[cls][1], d))
 
     def third(cls, f):
         b = quarter(cls, f, 0)
@@ -505,8 +525,7 @@
         third(cls, 0)
     for f in (1, 3, 2):
         for cls in range(3):
-            for e in range(4):
-                landed(line(cls, e, f), ag2_r.at[cls, f, e])
+            landed(quarter(cls, f, 0), ag2_r.at[cls, f])
             third(cls, f)
     for cls in range(3):
         to_pair(cls, 0, 0)
@@ -693,9 +712,13 @@
     return pl.pallas_call(
         layer_kernel,
         out_shape=jax.ShapeDtypeStruct((2, 4, 2 * HALF), F32),
-        in_specs=[hbm] + [vmem] * 4 + [hbm] * 5,
+        in_specs=[hbm] * 10,
         out_specs=vmem,
         scratch_shapes=[
+            pltpu.VMEM(residual.shape, BF16),
+            pltpu.VMEM(routes.shape, jnp.int32),
+            pltpu.VMEM(gain.shape, F32),
+            pltpu.VMEM(router.shape, F32),
             pltpu.VMEM((2, 8, HALF), F32),
             pltpu.VMEM((8, 128), F32),
             pltpu.VMEM((8, 64, LATENT), BF16),
@@ -725,8 +748,8 @@
             pltpu.VMEM((3, 3, 16, PART), BF16),
             pltpu.VMEM((2, 8, HALF), F32),
             pltpu.VMEM((8, HALF), F32),
-            dma((5,)), dma, dma((8,)), dma((8,)), dma((8,)), dma((8,)), dma((4,)), dma((4,)),
-            dma((3, 4)), dma((3, 4)), dma((3, 4, 4)), dma((3, 4, 4)), dma((3, 4, 4)), dma((3, 4, 4)),
+            dma((5,)), dma((5,)), dma((8,)), dma((8,)), dma((8,)), dma((8,)), dma((4,)), dma((4,)),
+            dma((3, 4)), dma((3, 4)), dma((3, 4, 4)), dma((3, 4)), dma((3, 4, 4)), dma((3, 4, 4)),
             dma((3, 4)), dma((3, 4)), dma((3, 4)), dma((3, 4)),
             dma((3, 3, 6)), dma((3, 3, 6)),
         ],

time: 207 us -> 205 us (level)
    pallas_call x1, Pallas kernels: 79.9 us -> 77.5 us  [layer(): pl.pallas_call(layer_kernel, out_shape=jax.ShapeDtypeStruct((2, 4, 2 * HA...]
where the time goes in v7:
time: 205 us
  Pallas kernels  203 us (99%)
    pallas_call x1, Pallas kernels, exchange(): pl.pallas_call(exchange_kernel, out_shape=jax.ShapeDtypeStruct((4, 4, 4,...  113 us
    pallas_call x1, Pallas kernels, layer(): pl.pallas_call(layer_kernel, out_shape=jax.ShapeDtypeStruct((2, 4, 2 * HA...  77.5 us
    pallas_call x1, Pallas kernels, attend(): pl.pallas_call(attend_kernel, out_shape=jax.ShapeDtypeStruct((8, 64, LATE...  12.8 us

profile of v7, /device:TPU:1, one launch (start us, length us, event | category | flops | bytes accessed | tf_op | source)
XLA Modules:
  0.0 204.8 jit_solution(9049266408963549959)
XLA Ops:
  0.0 113.0 %exchange.1 = bf16[4,4,4,2,3,96,128]{6,5,4,3,2,1,0:T(8,128)(2,1)} custom-call(s32[64,128]{1,0:T(8,128)} %bitcast.7, bf16[64,576,128]{2,1,0:T(8,128)(2,1)} %bitcast.5), custom_call_target="tpu_custom_call" | custom-call | tf_op jit(solution)/shard_map/exchange/pallas_call | solution.py:194
  113.0 12.8 %attend.1.attended = bf16[8,64,512]{2,1,0:T(8,128)(2,1)} custom-call(s32[64,128]{1,0:T(8,128)} %bitcast.8, s32[1,4]{1,0:T(1,128)} %counts.1, bf16[2,4,64,576]{3,2,1,0:T(8,128)(2,1)} %queries.1, bf16[2,4,576]{2,1,0:T(4,128)(2,1)} %new.1, bf16[128,3,96,128]{3,2,1,0:T(8,128)(2,1)} %bitcast.4), custom_call_target="tpu_custom_call" | custom-call | tf_op jit(solution)/shard_map/attend/pallas_call | solution.py:308
  125.7 77.5 %layer.1 = f32[2,4,3584]{2,1,0:T(4,128)} custom-call(bf16[8,64,512]{2,1,0:T(8,128)(2,1)} %attend.1.attended, bf16[2,4,3584]{2,1,0:T(4,128)(2,1)} %residual_in.1, s32[2,4,8]{2,1,0:T(4,128)} %routes_in.1, f32[3584]{0:T(1024)} %gain_in.1, f32[16,3584]{1,0:T(8,128)} %bitcast.6, bf16[8,512,128]{2,1,0:T(8,128)(2,1)} %w_uv.1, bf16[1024,3584]{1,0:T(8,128)(2,1)} %w_out.1, ...), custom_call_target="tpu_custom_call" | custom-call | tf_op jit(solution)/shard_map/layer/pallas_call | solution.py:712
  203.3 1.5 convert_element_type.3

commit v8 on v7

--- a/solution.py
+++ b/solution.py
@@ -222,14 +222,17 @@
         pltpu.make_async_copy(queries, q_ref, in_sem.at[0]),
         pltpu.make_async_copy(new, new_ref, in_sem.at[1]),
     ]
-    loads[1].start()
+    for load in loads:
+        load.start()
+
+    def page_copy(j):
+        return pltpu.make_async_copy(slots.at[table[j, me] // 128], keys.at[j], sem.at[j])
 
     def fetch(j, _):
-        pltpu.make_async_copy(slots.at[table[j, me] // 128], keys.at[j], sem).start()
+        page_copy(j).start()
         return 0
 
     lax.fori_loop(0, pages, fetch, 0)
-    loads[0].start()
 
     def clear(j, _):
         keys[pages + j] = jnp.zeros((3, 96, 128), BF16)
@@ -243,8 +246,6 @@
         for r in range(4):
             own_ref[r, step : step + 1, :] = fresh[r : r + 1]
     loads[0].wait()
-    filled = keys.at[pl.ds(0, pages)]
-    pltpu.make_async_copy(filled, filled, sem).wait()
     width = TILE * PAGE
     step_of = lax.broadcasted_iota(jnp.int32, (128, 16), 0) // 64
     token = lax.broadcasted_iota(jnp.int32, (128, 16), 1)
@@ -255,7 +256,12 @@
         parts.append(keys[pl.ds(page, TILE), 0:2, 64:96, :].reshape(width, 128))
         return jnp.concatenate(parts, axis=1)
 
-    def request(r, start):
+    def arrive(j, _):
+        pltpu.make_async_copy(keys.at[j], keys.at[j], sem.at[j]).wait()
+        return 0
+
+    def request(r, carry):
+        start, seen = carry
         q = jnp.concatenate([q_ref[0, r], q_ref[1, r]], axis=0)
         own = own_ref[r].astype(BF16)
         s_own = lax.dot_general(q, own, (((1,), (1,)), ((), ())), preferred_element_type=F32)
@@ -264,6 +270,8 @@
         q_wide = jnp.concatenate([q[:, :LATENT], q_rope, q_rope], axis=1)
         length = counts[0, r] * PAGE
         tiles = (length + width - 1) // width
+        needed = jnp.minimum(start + tiles * TILE, pages)
+        lax.fori_loop(seen, needed, arrive, 0)
 
         def score(t, top):
             page = start + t * TILE
@@ -297,9 +305,9 @@
         for g in range(8):
             block = jnp.concatenate([res[0, g], res[1, g]], axis=0)
             out_ref[g, pl.ds(at, 16), :] = block.astype(BF16)
-        return start + counts[0, r]
-
-    lax.fori_loop(0, 4, request, 0)
+        return start + counts[0, r], jnp.maximum(seen, needed)
+
+    lax.fori_loop(0, 4, request, (jnp.int32(0), jnp.int32(0)))
 
 
 def attend(table, counts, queries, new_latent, slots):
@@ -316,7 +324,7 @@
             pltpu.VMEM((4, 16, LATENT + ROPE), F32),
             pltpu.VMEM((64 + TILE, 3, 96, 128), BF16),
             pltpu.VMEM((32 // TILE, 128, TILE * PAGE), F32),
-            pltpu.SemaphoreType.DMA,
+            pltpu.SemaphoreType.DMA((64,)),
             pltpu.SemaphoreType.DMA((2,)),
         ],
         compiler_params=pltpu.CompilerParams(vmem_limit_bytes=60 * 2**20),
@@ -327,7 +335,7 @@
 def layer_kernel(
     attended, residual_in, routes_in, gain_in, router_in, w_uv, w_out, w_gate, w_up, w_down,
     out_ref,
-    residual, routes, gain, router, resid, member, heads_in, masked, part_out, part_in, res_all, mem_all, stat_out, stat_in, hidden,
+    residual, routes, gain, router, resid, member, heads_in, masked, part_out, part_pair, part_in, res_all, mem_all, stat_out, stat_in, hidden,
     gath, v_uv, v_out, v_gate, v_up, v_down, acc, inner,
     mix, sib_out, sib_in, t1, ul1, ur1, t2, last, fin_out, fin_in,
     wsem, lsem, head_s, head_r, part_s, part_r, pair_s, pair_r,
@@ -429,22 +437,29 @@
     flat = jnp.dot(pick, masked[...], preferred_element_type=F32).astype(BF16)
 
     copies[1].wait()
-    for h, turns in ((other, (1, 3, 5, 7)), (core, (2, 4, 6))):
+    for k, h in ((0, other), (1, core)):
         for t in range(HALF // 256):
             cols = pl.ds(pl.multiple_of(h * HALF + t * 256, 256), 256)
             y = jnp.dot(flat, v_out[:, cols], preferred_element_type=F32)
-            part_out[h, :, :, t * 256 : (t + 1) * 256] = y.astype(BF16).reshape(4, 16, 256)
-        for o in turns:
-            to = (ep + o) % 8
-            remote(part_out.at[h, to // 2], part_in.at[ep], part_s.at[o], part_r.at[o], (dp, to))
+            part_out[k, :, :, t * 256 : (t + 1) * 256] = y.astype(BF16).reshape(4, 16, 256)
+        if k == 0:
+            remote(part_out.at[0], part_pair, part_s.at[0], part_r.at[0], sibling)
+    landed(part_pair, part_r.at[0])
+    for d in (2, 1, 3, 0):
+        to = (pos[2] + d) % 4
+        both = part_out[1, to].astype(F32) + part_pair[to].astype(F32)
+        part_out[1, to] = both.astype(BF16)
+        if d:
+            remote(
+                part_out.at[1, to], part_in.at[d - 1], part_s.at[d], part_r.at[d], along(2, d)
+            )
     landed(res_all.at[other_rows], pair_r.at[0])
     landed(mem_all.at[other_rows], pair_r.at[1])
-    hid = part_out[core, pos[2]].astype(F32)
+    hid = part_out[1, pos[2]].astype(F32)
     settle()
-    for o in range(1, 8):
-        src = (ep + 8 - o) % 8
-        landed(part_in.at[src], part_r.at[o])
-        hid = hid + part_in[src].astype(F32)
+    for d in (1, 3, 2):
+        landed(part_in.at[d - 1], part_r.at[d])
+        hid = hid + part_in[d - 1].astype(F32)
     hid = hid + res_all[...]
     hidden[...] = hid
 
@@ -724,7 +739,8 @@
             pltpu.VMEM((8, 64, LATENT), BF16),
             pltpu.VMEM((512, 1024), BF16),
             pltpu.VMEM((2, 4, 16, HALF), BF16),
-            pltpu.VMEM((8, 16, HALF), BF16),
+            pltpu.VMEM((4, 16, HALF), BF16),
+            pltpu.VMEM((3, 16, HALF), BF16),
             pltpu.VMEM((16, HALF), F32),
             pltpu.VMEM((16, 128), F32),
             pltpu.VMEM((2, 16, 128), F32),
@@ -748,7 +764,7 @@
             pltpu.VMEM((3, 3, 16, PART), BF16),
             pltpu.VMEM((2, 8, HALF), F32),
             pltpu.VMEM((8, HALF), F32),
-            dma((5,)), dma((5,)), dma((8,)), dma((8,)), dma((8,)), dma((8,)), dma((4,)), dma((4,)),
+            dma((5,)), dma((5,)), dma((8,)), dma((8,)), dma((4,)), dma((4,)), dma((4,)), dma((4,)),
             dma((3, 4)), dma((3, 4)), dma((3, 4, 4)), dma((3, 4)), dma((3, 4, 4)), dma((3, 4, 4)),
             dma((3, 4)), dma((3, 4)), dma((3, 4)), dma((3, 4)),
             dma((3, 3, 6)), dma((3, 3, 6)),

time: 205 us -> 202 us (0.985)
  Pallas kernels: 203 us -> 200 us
where the time goes in v8:
time: 202 us
  Pallas kernels  200 us (99%)
    pallas_call x1, Pallas kernels, exchange(): pl.pallas_call(exchange_kernel, out_shape=jax.ShapeDtypeStruct((4, 4, 4,...  113 us
    pallas_call x1, Pallas kernels, layer(): pl.pallas_call(layer_kernel, out_shape=jax.ShapeDtypeStruct((2, 4, 2 * HA...  76.3 us
    pallas_call x1, Pallas kernels, attend(): pl.pallas_call(attend_kernel, out_shape=jax.ShapeDtypeStruct((8, 64, LATE...  11.2 us

profile of v8, /device:TPU:1, one launch (start us, length us, event | category | flops | bytes accessed | tf_op | source)
XLA Modules:
  0.0 202.0 jit_solution(12422643311642932050)
XLA Ops:
  0.0 113.0 %exchange.1 = bf16[4,4,4,2,3,96,128]{6,5,4,3,2,1,0:T(8,128)(2,1)} custom-call(s32[64,128]{1,0:T(8,128)} %bitcast.7, bf16[64,576,128]{2,1,0:T(8,128)(2,1)} %bitcast.5), custom_call_target="tpu_custom_call" | custom-call | tf_op jit(solution)/shard_map/exchange/pallas_call | solution.py:194
  113.0 11.2 %attend.1.attended = bf16[8,64,512]{2,1,0:T(8,128)(2,1)} custom-call(s32[64,128]{1,0:T(8,128)} %bitcast.8, s32[1,4]{1,0:T(1,128)} %counts.1, bf16[2,4,64,576]{3,2,1,0:T(8,128)(2,1)} %queries.1, bf16[2,4,576]{2,1,0:T(4,128)(2,1)} %new.1, bf16[128,3,96,128]{3,2,1,0:T(8,128)(2,1)} %bitcast.4), custom_call_target="tpu_custom_call" | custom-call | tf_op jit(solution)/shard_map/attend/pallas_call | solution.py:316
  124.1 76.3 %layer.1 = f32[2,4,3584]{2,1,0:T(4,128)} custom-call(bf16[8,64,512]{2,1,0:T(8,128)(2,1)} %attend.1.attended, bf16[2,4,3584]{2,1,0:T(4,128)(2,1)} %residual_in.1, s32[2,4,8]{2,1,0:T(4,128)} %routes_in.1, f32[3584]{0:T(1024)} %gain_in.1, f32[16,3584]{1,0:T(8,128)} %bitcast.6, bf16[8,512,128]{2,1,0:T(8,128)(2,1)} %w_uv.1, bf16[1024,3584]{1,0:T(8,128)(2,1)} %w_out.1, ...), custom_call_target="tpu_custom_call" | custom-call | tf_op jit(solution)/shard_map/layer/pallas_call | solution.py:727
  200.5 1.5 convert_element_type.3

commit v9 on v8

--- a/solution.py
+++ b/solution.py
@@ -247,8 +247,8 @@
             own_ref[r, step : step + 1, :] = fresh[r : r + 1]
     loads[0].wait()
     width = TILE * PAGE
-    step_of = lax.broadcasted_iota(jnp.int32, (128, 16), 0) // 64
-    token = lax.broadcasted_iota(jnp.int32, (128, 16), 1)
+    step_of = lax.broadcasted_iota(jnp.int32, (16, 128), 1) // 64
+    token = lax.broadcasted_iota(jnp.int32, (16, 128), 0)
     low = lax.broadcasted_iota(jnp.int32, (TILE, 32, 128), 2) < ROPE
 
     def values_of(page):
@@ -264,10 +264,11 @@
         start, seen = carry
         q = jnp.concatenate([q_ref[0, r], q_ref[1, r]], axis=0)
         own = own_ref[r].astype(BF16)
-        s_own = lax.dot_general(q, own, (((1,), (1,)), ((), ())), preferred_element_type=F32)
+        s_own = lax.dot_general(own, q, (((1,), (1,)), ((), ())), preferred_element_type=F32)
         s_own = jnp.where(token <= step_of, s_own * score_scale, -jnp.inf)
         q_rope = q[:, LATENT:]
         q_wide = jnp.concatenate([q[:, :LATENT], q_rope, q_rope], axis=1)
+        q_turned = jnp.transpose(q_wide)
         length = counts[0, r] * PAGE
         tiles = (length + width - 1) // width
         needed = jnp.minimum(start + tiles * TILE, pages)
@@ -279,35 +280,39 @@
             zero = jnp.zeros_like(rope)
             pair = jnp.concatenate([jnp.where(low, rope, zero), jnp.where(low, zero, rope)], axis=1)
             key = jnp.concatenate([values_of(page), pair.reshape(width, 128)], axis=1)
-            s = lax.dot_general(q_wide, key, (((1,), (1,)), ((), ())), preferred_element_type=F32)
-            place = t * width + lax.broadcasted_iota(jnp.int32, (128, width), 1)
+            s = jnp.dot(key, q_turned, preferred_element_type=F32)
+            place = t * width + lax.broadcasted_iota(jnp.int32, (width, 128), 0)
             s = jnp.where(place < length, s * score_scale, -jnp.inf)
             scores[t] = s
-            return jnp.maximum(top, jnp.max(s, axis=1, keepdims=True))
-
-        top = lax.fori_loop(0, tiles, score, jnp.max(s_own, axis=1, keepdims=True))
+            return jnp.maximum(top, jnp.max(s, axis=0, keepdims=True))
+
+        top = lax.fori_loop(0, tiles, score, jnp.max(s_own, axis=0, keepdims=True))
         p_own = jnp.exp(s_own - top)
-        total = jnp.sum(p_own, axis=1, keepdims=True)
-        acc = jnp.dot(p_own.astype(BF16), own[:, :LATENT], preferred_element_type=F32)
+        total = jnp.sum(p_own, axis=0, keepdims=True)
+
+        def weigh(p, values):
+            turned = jnp.transpose(p).astype(BF16)
+            return jnp.dot(turned, values, preferred_element_type=F32)
+
+        acc = weigh(p_own, own[:, :LATENT])
 
         def mix(t, carry):
             total, acc = carry
             p = jnp.exp(scores[t] - top)
-            total = total + jnp.sum(p, axis=1, keepdims=True)
-            acc = acc + jnp.dot(
-                p.astype(BF16), values_of(start + t * TILE), preferred_element_type=F32
-            )
+            total = total + jnp.sum(p, axis=0, keepdims=True)
+            acc = acc + weigh(p, values_of(start + t * TILE))
             return total, acc
 
         total, acc = lax.fori_loop(0, tiles, mix, (total, acc))
-        res = (acc / total).reshape(2, 8, 8, LATENT)
+        scale = jnp.transpose(jnp.broadcast_to(1.0 / total, (128, 128)))[:, 0:1]
+        res = (acc * scale).reshape(2, 8, 8, LATENT)
         at = pl.multiple_of(r * 16, 16)
         for g in range(8):
             block = jnp.concatenate([res[0, g], res[1, g]], axis=0)
             out_ref[g, pl.ds(at, 16), :] = block.astype(BF16)
         return start + counts[0, r], jnp.maximum(seen, needed)
 
-    lax.fori_loop(0, 4, request, (jnp.int32(0), jnp.int32(0)))
+    lax.fori_loop(0, 4, request, (jnp.int32(0), jnp.int32(0)), unroll=True)
 
 
 def attend(table, counts, queries, new_latent, slots):
@@ -323,7 +328,7 @@
             pltpu.VMEM(new_latent.shape, BF16),
             pltpu.VMEM((4, 16, LATENT + ROPE), F32),
             pltpu.VMEM((64 + TILE, 3, 96, 128), BF16),
-            pltpu.VMEM((32 // TILE, 128, TILE * PAGE), F32),
+            pltpu.VMEM((32 // TILE, TILE * PAGE, 128), F32),
             pltpu.SemaphoreType.DMA((64,)),
             pltpu.SemaphoreType.DMA((2,)),
         ],
@@ -372,10 +377,10 @@
 
     sent = []
 
-    def settle():
-        for src, ssem in sent:
+    def settle(count=None):
+        for src, ssem in sent[:count]:
             pltpu.make_async_copy(src, src, ssem).wait()
-        sent.clear()
+        del sent[:count]
 
     barrier = pltpu.get_barrier_semaphore()
     for peer in ep_peers + ring_peers:
@@ -544,6 +549,21 @@
             third(cls, f)
     for cls in range(3):
         to_pair(cls, 0, 0)
+    for copy in copies[2:]:
+        copy.wait()
+
+    def expert_in(h, cls, shift):
+        at = plane_at(cls, shift)
+        n = WIDTHS[cls]
+        x = gath[(h, cls) + at].reshape(256, PART)[:, :n]
+        rows = pl.ds(pl.multiple_of(h * HALF + cls * PART, 128), n)
+        for k, w in enumerate((v_gate, v_up)):
+            y = jnp.dot(x, w[0, rows, :], preferred_element_type=F32).reshape(4, 4, 16, 256)
+            acc[(k,) + at] = acc[(k,) + at] + y
+
+    def from_pair(cls, k, shift):
+        landed(gath.at[(other, cls) + plane_at(cls, shift)], sib_r.at[cls, k])
+
     for f in (0, 1, 3, 2):
         for cls, order in enumerate(ORDERS):
             landed(quarter(cls, f, 3), ag3_r.at[cls, f, 0])
@@ -552,42 +572,29 @@
             landed(quarter(cls, f, 1), ag3_r.at[cls, f, 1])
             b = quarter(cls, f, 1, halves[1])
             remote(b, b, ag3_s.at[cls, f, 3], ag3_r.at[cls, f, 3], along(order[2], 3))
+        if f == 1:
+            for cls in range(3):
+                expert_in(core, cls, 0)
+        if f == 3:
+            for cls in range(3):
+                from_pair(cls, 0, 0)
+                expert_in(other, cls, 0)
     for k, shift in ((1, 3), (2, 1)):
         for cls in range(3):
             to_pair(cls, k, shift)
 
-    for copy in copies[2:]:
-        copy.wait()
-
-    def expert_in(h, cls, shift):
-        at = plane_at(cls, shift)
-        n = WIDTHS[cls]
-        x = gath[(h, cls) + at].reshape(256, PART)[:, :n]
-        rows = pl.ds(pl.multiple_of(h * HALF + cls * PART, 128), n)
-        for k, w in enumerate((v_gate, v_up)):
-            y = jnp.dot(x, w[0, rows, :], preferred_element_type=F32).reshape(4, 4, 16, 256)
-            acc[(k,) + at] = acc[(k,) + at] + y
-
-    def from_pair(cls, k, shift):
-        landed(gath.at[(other, cls) + plane_at(cls, shift)], sib_r.at[cls, k])
-
-    for cls in range(3):
-        expert_in(core, cls, 0)
-    for cls in range(3):
-        from_pair(cls, 0, 0)
-        expert_in(other, cls, 0)
     for k, shift in ((1, 3), (2, 1)):
         for cls in range(3):
             expert_in(core, cls, shift)
+    for k, shift in ((1, 3), (2, 1)):
+        for cls in range(3):
+            from_pair(cls, k, shift)
+            expert_in(other, cls, shift)
     for cls in range(3):
         for f in range(4):
             landed(quarter(cls, f, 2, halves[0]), ag3_r.at[cls, f, 2])
             landed(quarter(cls, f, 2, halves[1]), ag3_r.at[cls, f, 3])
         to_pair(cls, 3, 2)
-    for k, shift in ((1, 3), (2, 1)):
-        for cls in range(3):
-            from_pair(cls, k, shift)
-            expert_in(other, cls, shift)
     for cls in range(3):
         expert_in(core, cls, 2)
     for cls in range(3):
@@ -643,6 +650,7 @@
             sum_s.at[cls, 0, k], sum_r.at[cls, 0, k], along(ORDERS[cls][2], delta),
         )
 
+    gathered = len(sent)
     for_pair(2)
     for_pair(1)
     for_self(2)
@@ -656,6 +664,7 @@
     for_self(3)
     for cls in range(3):
         send(cls, 3, 0, ur1, 3, 3)
+    settle(gathered)
     for cls in range(3):
         for half, shift, buf, k, delta in ((0, 1, ul1, 0, 1), (1, 3, ur1, 1, 3)):
             at, tmp = block(cls, shift, halves[half]), temp(cls, halves[half])
@@ -664,7 +673,7 @@
             send(cls, shift, half, buf, k + 4, delta)
     for_pair(0)
     for_self(0)
-    settle()
+    first_axis = len(sent)
     for cls, order in enumerate(ORDERS):
         a1, a2, a3 = order
         n = WIDTHS[cls]
@@ -700,6 +709,7 @@
             if d:
                 dst = last.at[cls, d - 1, :, pl.ds(0, n)]
                 remote(mix.at[at], dst, sum_s.at[cls, 2, d], sum_r.at[cls, 2, d], along(a1, d))
+    settle(first_axis)
     for cls in range(3):
         n = WIDTHS[cls]
         total = mix[cls, pos[0], pos[1], pos[2], :, 0:n].astype(F32)

time: 202 us -> 202 us (level)
  no operation moved by 1% of the time
where the time goes in v9:
time: 202 us
  Pallas kernels  200 us (99%)
    pallas_call x1, Pallas kernels, exchange(): pl.pallas_call(exchange_kernel, out_shape=jax.ShapeDtypeStruct((4, 4, 4,...  113 us
    pallas_call x1, Pallas kernels, layer(): pl.pallas_call(layer_kernel, out_shape=jax.ShapeDtypeStruct((2, 4, 2 * HA...  75 us
    pallas_call x1, Pallas kernels, attend(): pl.pallas_call(attend_kernel, out_shape=jax.ShapeDtypeStruct((8, 64, LATE...  12.1 us

profile of v9, /device:TPU:1, one launch (start us, length us, event | category | flops | bytes accessed | tf_op | source)
XLA Modules:
  0.0 201.7 jit_solution(1610643503271479011)
XLA Ops:
  0.0 113.0 %exchange.1 = bf16[4,4,4,2,3,96,128]{6,5,4,3,2,1,0:T(8,128)(2,1)} custom-call(s32[64,128]{1,0:T(8,128)} %bitcast.7, bf16[64,576,128]{2,1,0:T(8,128)(2,1)} %bitcast.5), custom_call_target="tpu_custom_call" | custom-call | tf_op jit(solution)/shard_map/exchange/pallas_call | solution.py:194
  113.0 12.1 %attend.1.attended = bf16[8,64,512]{2,1,0:T(8,128)(2,1)} custom-call(s32[64,128]{1,0:T(8,128)} %bitcast.8, s32[1,4]{1,0:T(1,128)} %counts.1, bf16[2,4,64,576]{3,2,1,0:T(8,128)(2,1)} %queries.1, bf16[2,4,576]{2,1,0:T(4,128)(2,1)} %new.1, bf16[128,3,96,128]{3,2,1,0:T(8,128)(2,1)} %bitcast.4), custom_call_target="tpu_custom_call" | custom-call | tf_op jit(solution)/shard_map/attend/pallas_call | solution.py:321
  125.1 75.0 %layer.1 = f32[2,4,3584]{2,1,0:T(4,128)} custom-call(bf16[8,64,512]{2,1,0:T(8,128)(2,1)} %attend.1.attended, bf16[2,4,3584]{2,1,0:T(4,128)(2,1)} %residual_in.1, s32[2,4,8]{2,1,0:T(4,128)} %routes_in.1, f32[3584]{0:T(1024)} %gain_in.1, f32[16,3584]{1,0:T(8,128)} %bitcast.6, bf16[8,512,128]{2,1,0:T(8,128)(2,1)} %w_uv.1, bf16[1024,3584]{1,0:T(8,128)(2,1)} %w_out.1, ...), custom_call_target="tpu_custom_call" | custom-call | tf_op jit(solution)/shard_map/layer/pallas_call | solution.py:737
  200.1 1.5 convert_element_type.3

commit v10 on v9

--- a/solution.py
+++ b/solution.py
@@ -121,7 +121,7 @@
                 rope_rows(cls, part - 4, 16 * part)
             if part == 0 and cls == 0:
                 pl.semaphore_wait(barrier, len(peers))
-            for d in (1, 2, 3):
+            for d in (2, 1, 3):
                 src = spec_of(order, ((pos[a1] + d) % 4, whole, whole))
                 dst = spec_of(order, (pos[a1], whole, whole))
                 remote(
@@ -136,7 +136,7 @@
     def second(cls, buf, e):
         a1, a2, a3 = order = ORDERS[cls]
         src1 = (pos[a1] + 4 - e) % 4
-        for d in (1, 2, 3):
+        for d in (2, 1, 3):
             src = spec_of(order, (src1, (pos[a2] + d) % 4, whole))
             dst = spec_of(order, (src1, pos[a2], whole))
             remote(
@@ -147,7 +147,7 @@
     def third(cls, buf, f):
         a1, a2, a3 = order = ORDERS[cls]
         src2 = (pos[a2] + 4 - f) % 4
-        for d in (1, 2, 3, 0):
+        for d in (2, 1, 3, 0):
             for k, c in ((0, core), (1, other)):
                 src = spec_of(order, (whole, src2, (pos[a3] + d) % 4))
                 dst = spec_of(order, (whole, src2, pos[a3]))
@@ -394,7 +394,7 @@
         copy.start()
     pl.semaphore_wait(barrier, len(ep_peers) + len(ring_peers))
 
-    for o in range(1, 8):
+    for o in (4, 3, 5, 2, 6, 7, 1):
         to = (ep + o) % 8
         remote(attended.at[to], heads_in.at[ep], head_s.at[o], head_r.at[o], (dp, to))
     own_heads = pltpu.make_async_copy(attended.at[ep], heads_in.at[ep], lsem.at[0])

time: 202 us -> 202 us (level)
  no operation moved by 1% of the time
where the time goes in v10:
time: 202 us
  Pallas kernels  200 us (99%)
    pallas_call x1, Pallas kernels, exchange(): pl.pallas_call(exchange_kernel, out_shape=jax.ShapeDtypeStruct((4, 4, 4,...  112 us
    pallas_call x1, Pallas kernels, layer(): pl.pallas_call(layer_kernel, out_shape=jax.ShapeDtypeStruct((2, 4, 2 * HA...  76.8 us
    pallas_call x1, Pallas kernels, attend(): pl.pallas_call(attend_kernel, out_shape=jax.ShapeDtypeStruct((8, 64, LATE...  11.2 us

profile of v10, /device:TPU:1, one launch (start us, length us, event | category | flops | bytes accessed | tf_op | source)
XLA Modules:
  0.0 201.8 jit_solution(3666036742390726190)
XLA Ops:
  0.0 112.2 %exchange.1 = bf16[4,4,4,2,3,96,128]{6,5,4,3,2,1,0:T(8,128)(2,1)} custom-call(s32[64,128]{1,0:T(8,128)} %bitcast.7, bf16[64,576,128]{2,1,0:T(8,128)(2,1)} %bitcast.5), custom_call_target="tpu_custom_call" | custom-call | tf_op jit(solution)/shard_map/exchange/pallas_call | solution.py:194
  112.2 11.2 %attend.1.attended = bf16[8,64,512]{2,1,0:T(8,128)(2,1)} custom-call(s32[64,128]{1,0:T(8,128)} %bitcast.8, s32[1,4]{1,0:T(1,128)} %counts.1, bf16[2,4,64,576]{3,2,1,0:T(8,128)(2,1)} %queries.1, bf16[2,4,576]{2,1,0:T(4,128)(2,1)} %new.1, bf16[128,3,96,128]{3,2,1,0:T(8,128)(2,1)} %bitcast.4), custom_call_target="tpu_custom_call" | custom-call | tf_op jit(solution)/shard_map/attend/pallas_call | solution.py:321
  123.4 76.8 %layer.1 = f32[2,4,3584]{2,1,0:T(4,128)} custom-call(bf16[8,64,512]{2,1,0:T(8,128)(2,1)} %attend.1.attended, bf16[2,4,3584]{2,1,0:T(4,128)(2,1)} %residual_in.1, s32[2,4,8]{2,1,0:T(4,128)} %routes_in.1, f32[3584]{0:T(1024)} %gain_in.1, f32[16,3584]{1,0:T(8,128)} %bitcast.6, bf16[8,512,128]{2,1,0:T(8,128)(2,1)} %w_uv.1, bf16[1024,3584]{1,0:T(8,128)(2,1)} %w_out.1, ...), custom_call_target="tpu_custom_call" | custom-call | tf_op jit(solution)/shard_map/layer/pallas_call | solution.py:737
  200.2 1.5 convert_element_type.3
